TPU v7x, 32 devices: a whole 2x2x4 slice. The times are simulated.
32 devices in a mesh: parts: 1, node: 4 (over y, x), local: 8 (over z, core).
Axes of the slice: x: 2, y: 2, z: 4, core: 2. Of those that a mesh axis runs over, the one named last changes fastest.
Arguments:
- tokens: bfloat16 [2048, 4096], P(('parts', 'node', 'local')), may hold values from -6 to 6
- expert_ids: int32 [2048, 8], P(('parts', 'node', 'local')), may hold values from 0 to 15, all different within a row; in each aligned block of 64 rows (0 to 63, 64 to 127, ...) at most 40 rows name the same one
- gate_weights: float32 [2048, 8], P(('parts', 'node', 'local')), may hold values from 0.02 to 0.5
- w_gate: bfloat16 [4096, 12288], P(None, ('parts', 'node', 'local')), may hold values from -0.09375 to 0.09375
- w_up: bfloat16 [4096, 12288], P(None, ('parts', 'node', 'local')), may hold values from -0.09375 to 0.09375
- w_down: bfloat16 [12288, 4096], P(('parts', 'node', 'local')), may hold values from -0.21875 to 0.21875
Outputs:
- mixed: bfloat16 [2048, 4096], P(('parts', 'node', 'local'))
Inputs may be any that keep to these rules, and one draw needn't show every extreme that they name: `expert_ids`: each token names 8 different experts; among the 64 tokens of one device no expert is named more than 40 times, and in some such block one expert is named exactly 40 times.
All inputs are finite; a program needn't handle non-finite values.
Results may differ from a plain program's by a relative error of at most 0.0058.
Values may be sent and summed in bfloat16 or wider, within the bound.
No kernel may reach another device: no remote copies, remote signals or barrier semaphores. Data moves between devices by JAX's collectives and lax.ppermute only.
A program may use at most 128 MiB of HBM per device.

v0:
```python
import jax
import jax.numpy as jnp
from jax import lax
from jax.sharding import PartitionSpec as P


def partner_2(value, axis, bit):
    mask = 2**bit
    pairs = [(source, source ^ mask) for source in range(lax.axis_size(axis))]
    return lax.ppermute(value, axis, pairs)


def per_device(tokens, expert_ids, gate_weights, w_gate, w_up, w_down):
    node_count = lax.axis_size("node")
    local_count = lax.axis_size("local")
    devices = node_count * local_count
    experts = devices // 2
    tok_rows, top_count = expert_ids.shape
    width = tokens.shape[1]
    capacity = tok_rows * top_count * 5 // (4 * experts)
    flat_ids = expert_ids.reshape(-1)
    one_hot = (flat_ids[:, None] == jnp.arange(experts, dtype=jnp.int32)[None, :]).astype(jnp.int32)
    earlier = jnp.cumsum(one_hot, axis=0) - one_hot
    slot_rank = jnp.sum(earlier * one_hot, axis=1)
    slot_index = (flat_ids * capacity + slot_rank).reshape(tok_rows, top_count)
    slot_table = jnp.any(
        slot_index[None, :, :] == jnp.arange(experts * capacity, dtype=jnp.int32)[:, None, None],
        axis=2,
    ).astype(jnp.bfloat16)
    outgoing = jnp.dot(slot_table, tokens, preferred_element_type=jnp.float32).astype(jnp.bfloat16)
    outgoing = outgoing.reshape(devices, capacity // 2, width)
    partner = partner_2((w_gate, w_up, w_down), "local", 0)
    full_gate = jnp.concatenate([w_gate, partner[0]], axis=1)
    full_up = jnp.concatenate([w_up, partner[1]], axis=1)
    full_down = jnp.concatenate([w_down, partner[2]], axis=0)
    block = lax.all_to_all(outgoing, ("node", "local"), split_axis=0, concat_axis=0, tiled=True)
    rows = block.reshape(-1, width)
    gate = jnp.dot(rows, full_gate, preferred_element_type=jnp.float32)
    upper = jnp.dot(rows, full_up, preferred_element_type=jnp.float32)
    hidden = (jax.nn.silu(gate) * upper).astype(jnp.bfloat16)
    result = jnp.dot(hidden, full_down, preferred_element_type=jnp.float32).astype(jnp.bfloat16)
    processed = result.reshape(block.shape)
    returned = lax.all_to_all(processed, ("node", "local"), split_axis=0, concat_axis=0, tiled=True)
    results = returned.reshape(experts * capacity, width)
    chosen = results[slot_index]
    mixed = jnp.sum(gate_weights[:, :, None] * chosen.astype(jnp.float32), axis=1)
    return mixed.astype(jnp.bfloat16)


def solution(mesh):
    placed = (
        P(("parts", "node", "local"), None),
        P(("parts", "node", "local"), None),
        P(("parts", "node", "local"), None),
        P(None, ("parts", "node", "local")),
        P(None, ("parts", "node", "local")),
        P(("parts", "node", "local"), None),
    )
    return jax.shard_map(
        per_device,
        mesh=mesh,
        in_specs=placed,
        out_specs=P(("parts", "node", "local"), None),
        check_vma=False,
    )
```

profile of v0, /device:TPU:0, one launch (start us, length us, event | category | flops | bytes accessed | tf_op | source)
XLA Modules:
  0.0 376.2 jit_solution(10786451935689527593)
XLA Ops:
  0.0 0.8 copy.22
  0.8 0.1 eq.42
  0.9 0.1 eq.38
  1.0 1.2 reduce-window.6
  2.2 0.2 slice_reduce_fusion
  2.4 0.1 fusion.20
  2.5 0.1 reduce_sum.21
  2.6 0.1 copy.25
  2.7 0.7 compare_select_fusion
  3.4 0.1 copy.26
  3.5 0.5 fusion.12
  4.0 3.9 %convolution_convert_fusion.1 = bf16[640,4096]{1,0:T(8,128)(2,1)} fusion(pred[640,64]{0,1:T(8,128)(4,1)S(1)} %fusion.12, bf16[64,4096]{1,0:T(8,128)(2,1)S(1)} %copy-done), kind=kOutput, calls=%fused_computation.4 | convolution fusion | flops 338165760 | bytes 5808128 | tf_op jit(solution)/shard_map/dot_general | solution.py:30
  7.8 7.6 %reshape.40 = bf16[32,20,4096]{2,1,0:T(8,128)(2,1)} reshape(bf16[640,4096]{1,0:T(8,128)(2,1)} %convolution_convert_fusion.1) | data formatting | bytes 10485760 | tf_op jit(solution)/shard_map/reshape | solution.py:31
  15.5 7.6 %all-to-all-start = ((bf16[32,20,4096]{2,1,0:T(8,128)(2,1)}), bf16[32,20,4096]{2,1,0:T(8,128)(2,1)}, u32[]{:S(2)}, u32[]{:S(2)}) async-start(bf16[32,20,4096]{2,1,0:T(8,128)(2,1)} %reshape.40), calls=%async_computation | async-start | bytes 12582912 | tf_op jit(solution)/shard_map/all_to_all | solution.py:36
  23.1 0.1 collective-permute-start.1
  23.2 0.5 collective-permute-start
  23.6 0.1 collective-permute-start.2
  23.7 139.1 %all-to-all-done = bf16[32,20,4096]{2,1,0:T(8,128)(2,1)} async-done(((bf16[32,20,4096]{2,1,0:T(8,128)(2,1)}), bf16[32,20,4096]{2,1,0:T(8,128)(2,1)}, u32[]{:S(2)}, u32[]{:S(2)}) %all-to-all-start) | async-done | bytes 5242912 | tf_op jit(solution)/shard_map/all_to_all | solution.py:36
  162.9 7.8 %reshape.41 = bf16[640,4096]{1,0:T(8,128)(2,1)} reshape(bf16[32,20,4096]{2,1,0:T(8,128)(2,1)} %all-to-all-done) | data formatting | bytes 10485760 | tf_op jit(solution)/shard_map/reshape | solution.py:37
  170.7 0.0 collective-permute-done.1
  170.7 8.6 %fusion.5 = f32[640,768]{1,0:T(8,128)S(1)} fusion(bf16[640,4096]{1,0:T(8,128)(2,1)} %reshape.41, bf16[4096,384]{1,0:T(8,128)(2,1)} %collective-permute-done.1, bf16[4096,384]{1,0:T(8,128)(2,1)} %param.10), kind=kOutput, calls=%fused_computation.9 | convolution fusion | flops 4039114752 | bytes 13500416 | tf_op jit(solution)/shard_map/dot_general | solution.py:39
  179.3 0.0 collective-permute-done.2
  179.3 19.5 %convolution_convert_fusion = bf16[640,4096]{1,0:T(8,128)(2,1)} fusion(bf16[384,4096]{1,0:T(8,128)(2,1)} %collective-permute-done.2, bf16[384,4096]{1,0:T(8,128)(2,1)} %param.11, f32[640,768]{1,0:T(8,128)S(1)} %fusion.5, bf16[640,4096]{1,0:T(8,128)(2,1)} %reshape.41, bf16[4096,384]{1,0:T(8,128)(2,1)} %collective-permute-done, bf16[4096,384]{1,0:T(8,128)(2,1)} %param.9), kind=kOutput, calls=%fused_computation.3 | convolution fusion | flops 8083800064 | bytes 25034752 | tf_op jit(solution)/shard_map/dot_general | solution.py:41
  198.8 7.6 %reshape.42 = bf16[32,20,4096]{2,1,0:T(8,128)(2,1)} reshape(bf16[640,4096]{1,0:T(8,128)(2,1)} %convolution_convert_fusion) | data formatting | bytes 10485760 | tf_op jit(solution)/shard_map/reshape | solution.py:42
  206.4 4.0 %all-to-all-start.1 = ((bf16[32,20,4096]{2,1,0:T(8,128)(2,1)}), bf16[32,20,4096]{2,1,0:T(8,128)(2,1)}, u32[]{:S(2)}, u32[]{:S(2)}) async-start(bf16[32,20,4096]{2,1,0:T(8,128)(2,1)} %reshape.42), calls=%async_computation.1 | async-start | bytes 12582912 | tf_op jit(solution)/shard_map/all_to_all | solution.py:43
  210.4 0.1 copy.27
  210.5 0.1 reshape.46
  210.6 0.1 copy.21
  210.7 139.5 %all-to-all-done.1 = bf16[32,20,4096]{2,1,0:T(8,128)(2,1)} async-done(((bf16[32,20,4096]{2,1,0:T(8,128)(2,1)}), bf16[32,20,4096]{2,1,0:T(8,128)(2,1)}, u32[]{:S(2)}, u32[]{:S(2)}) %all-to-all-start.1) | async-done | bytes 5242912 | tf_op jit(solution)/shard_map/all_to_all | solution.py:43
  350.1 7.8 %reshape.43 = bf16[640,4096]{1,0:T(8,128)(2,1)} reshape(bf16[32,20,4096]{2,1,0:T(8,128)(2,1)} %all-to-all-done.1) | data formatting | bytes 10485760 | tf_op jit(solution)/shard_map/reshape | solution.py:44
  358.0 11.8 %gather_fusion = bf16[512,4096]{1,0:T(8,128)(2,1)} fusion(bf16[640,4096]{1,0:T(8,128)(2,1)} %reshape.43, s32[1024]{0:T(1024)S(1)} %pad_clamp_fusion), kind=kCustom, calls=%fused_computation | custom fusion | bytes 8390656 | tf_op jit(solution)/shard_map/gather | solution.py:45
  369.8 6.5 %fusion = bf16[64,4096]{1,0:T(8,128)(2,1)} fusion(bf16[512,4096]{1,0:T(8,128)(2,1)} %gather_fusion, f32[64,8]{1,0:T(8,128)S(1)} %copy.21), kind=kLoop, calls=%fused_computation.2 | loop fusion | flops 6029312 | bytes 4720640 | tf_op jit(solution)/shard_map/reduce_sum | solution.py:46
  (11 shorter events, 0.1 us)
Async XLA Ops:
  0.0 4.0 %copy-start = (bf16[64,4096]{1,0:T(8,128)(2,1)S(1)}, bf16[64,4096]{1,0:T(8,128)(2,1)}, u32[]{:S(2)}) copy-start(bf16[64,4096]{1,0:T(8,128)(2,1)} %param.6) | copy-start | bytes 1572868
  15.5 147.4 %all-to-all-start = ((bf16[32,20,4096]{2,1,0:T(8,128)(2,1)}), bf16[32,20,4096]{2,1,0:T(8,128)(2,1)}, u32[]{:S(2)}, u32[]{:S(2)}) async-start(bf16[32,20,4096]{2,1,0:T(8,128)(2,1)} %reshape.40), calls=%async_computation | async-start | bytes 12582912 | tf_op jit(solution)/shard_map/all_to_all | solution.py:36
  23.1 147.6 %collective-permute-start.1 = (bf16[4096,384]{1,0:T(8,128)(2,1)}, bf16[4096,384]{1,0:T(8,128)(2,1)}, u32[]{:S(2)}, u32[]{:S(2)}) collective-permute-start(bf16[4096,384]{1,0:T(8,128)(2,1)} %param.10), channel_id=1, source_target_pairs={{0,1},{1,0},{2,3},{3,2},{4,5},{5,4},{6,7},{7,6},{8,9},{9,8},{10,11... | collective-permute-start | bytes 9437192 | tf_op jit(solution)/shard_map/ppermute | solution.py:10
  23.2 156.2 %collective-permute-start = (bf16[4096,384]{1,0:T(8,128)(2,1)}, bf16[4096,384]{1,0:T(8,128)(2,1)}, u32[]{:S(2)}, u32[]{:S(2)}) collective-permute-start(bf16[4096,384]{1,0:T(8,128)(2,1)} %param.9), channel_id=1, source_target_pairs={{0,1},{1,0},{2,3},{3,2},{4,5},{5,4},{6,7},{7,6},{8,9},{9,8},{10,11... | collective-permute-start | bytes 9437192 | tf_op jit(solution)/shard_map/ppermute | solution.py:10
  23.6 155.7 %collective-permute-start.2 = (bf16[384,4096]{1,0:T(8,128)(2,1)}, bf16[384,4096]{1,0:T(8,128)(2,1)}, u32[]{:S(2)}, u32[]{:S(2)}) collective-permute-start(bf16[384,4096]{1,0:T(8,128)(2,1)} %param.11), channel_id=1, source_target_pairs={{0,1},{1,0},{2,3},{3,2},{4,5},{5,4},{6,7},{7,6},{8,9},{9,8},{10,11... | collective-permute-start | bytes 9437192 | tf_op jit(solution)/shard_map/ppermute | solution.py:10
  206.4 4.2 %copy-start.2 = (f32[64,8]{0,1:T(8,128)S(1)}, f32[64,8]{0,1:T(8,128)}, u32[]{:S(2)}) copy-start(f32[64,8]{0,1:T(8,128)} %param.8) | copy-start | bytes 6148
  206.4 143.7 %all-to-all-start.1 = ((bf16[32,20,4096]{2,1,0:T(8,128)(2,1)}), bf16[32,20,4096]{2,1,0:T(8,128)(2,1)}, u32[]{:S(2)}, u32[]{:S(2)}) async-start(bf16[32,20,4096]{2,1,0:T(8,128)(2,1)} %reshape.42), calls=%async_computation.1 | async-start | bytes 12582912 | tf_op jit(solution)/shard_map/all_to_all | solution.py:43
  358.0 18.2 %copy-start.1 = (bf16[64,4096]{1,0:T(8,128)(2,1)S(1)}, bf16[64,4096]{1,0:T(8,128)(2,1)}, u32[]{:S(2)}) copy-start(bf16[64,4096]{1,0:T(8,128)(2,1)} %param.6) | copy-start | bytes 1572868
where the time goes:
time: 377 us; the launch traced here: 376 us
  waiting for transfers between devices  279 us (74%)
  local copies, waits for them, and re-layouts  44.4 us (12%)
  matrix products  31.9 us (8%)
  starting transfers between devices  12.2 us (3%)
  other arithmetic  8.92 us (2%)
    all_to_all x1, waiting for transfers between devices, per_device(): lax.all_to_all(processed, ('node', 'local'), split_axis=0, concat_axis=0,...  139 us
    all_to_all x1, waiting for transfers between devices, per_device(): lax.all_to_all(outgoing, ('node', 'local'), split_axis=0, concat_axis=0,...  139 us
    dot_general x1, matrix products, per_device(): jnp.dot(hidden, full_down, preferred_element_type=jnp.float32)  19.5 us
    gather x1, local copies, waits for them, and re-layouts, per_device(): chosen = results[slot_index]  11.8 us
    dot_general x1, matrix products, per_device(): upper = jnp.dot(rows, full_up, preferred_element_type=jnp.float32)  8.6 us
    reshape x1, local copies, waits for them, and re-layouts, per_device(): rows = block.reshape(-1, width)  7.84 us
    reshape x1, local copies, waits for them, and re-layouts, per_device(): results = returned.reshape(experts * capacity, width)  7.84 us
    reshape x1, local copies, waits for them, and re-layouts, per_device(): outgoing = outgoing.reshape(devices, capacity // 2, width)  7.62 us
  transfers between devices with their start and end apart: 5, of which 2 were waited for; matrix products, arithmetic and copies ran while one was open for 4% of the time, Pallas kernels for 0%

commit v1 on v0

v1 whole, which is shorter than its diff:
```python
import functools

import jax
import jax.numpy as jnp
from jax import lax
from jax.experimental import pallas as pl
from jax.experimental.pallas import tpu as pltpu
from jax.sharding import PartitionSpec as P

LANES = 128
VMEM_BYTES = 50 * 2**20


def swap(value, axis, mask):
    pairs = [(source, source ^ mask) for source in range(lax.axis_size(axis))]
    return lax.ppermute(value, axis, pairs)


def pack_block(tokens, expert_ids, gate_weights):
    parts = [expert_ids.astype(jnp.float32)]
    rest = gate_weights
    for _ in range(3):
        piece = lax.reduce_precision(rest, exponent_bits=8, mantissa_bits=7)
        parts.append(piece)
        rest = rest - piece
    meta = jnp.concatenate(parts, axis=1).astype(jnp.bfloat16)
    meta = jnp.pad(meta, ((0, 0), (0, -meta.shape[1] % LANES)))
    return jnp.concatenate([tokens, meta], axis=1)


def slots(place, meta, top, chain, capacity, count):
    rows = meta.shape[0]
    node, link = place[0], place[1]
    lane = lax.broadcasted_iota(jnp.int32, (rows, LANES), 1)
    expert = (jnp.bitwise_xor(lane, node) * chain + link).astype(jnp.float32)
    chosen = jnp.zeros((rows, LANES), jnp.float32)
    weight = jnp.zeros((rows, LANES), jnp.float32)
    for k in range(top):
        hit = meta[:, k : k + 1] == expert
        gate = meta[:, top + k : top + k + 1] + meta[:, 2 * top + k : 2 * top + k + 1]
        gate = gate + meta[:, 3 * top + k : 3 * top + k + 1]
        chosen = chosen + jnp.where(hit, 1.0, 0.0)
        weight = weight + jnp.where(hit, gate, 0.0)
    before = lax.broadcasted_iota(jnp.int32, (rows, rows), 0) > lax.broadcasted_iota(jnp.int32, (rows, rows), 1)
    rank = jnp.dot(
        jnp.where(before, 1.0, 0.0).astype(jnp.bfloat16),
        chosen.astype(jnp.bfloat16),
        preferred_element_type=jnp.float32,
    )
    rank = jnp.where(chosen > 0.5, rank, -1.0)
    slot = lax.broadcasted_iota(jnp.int32, (rows, capacity), 1).astype(jnp.float32)
    return [(jnp.where(rank[:, n : n + 1] == slot, 1.0, 0.0), weight[:, n : n + 1]) for n in range(count)]


def select_kernel(top, chain, capacity, place, block, *outs):
    width = outs[0].shape[1]
    meta = block[:, width:].astype(jnp.float32)
    hots = [hot for hot, _ in slots(place, meta, top, chain, capacity, len(outs))]
    tokens = block[:, :width]
    for hot, out in zip(hots, outs):
        picked = lax.dot_general(
            hot.astype(jnp.bfloat16), tokens, (((0,), (0,)), ((), ())), preferred_element_type=jnp.float32
        )
        out[...] = picked.astype(jnp.bfloat16)


def smem():
    return pl.BlockSpec(memory_space=pltpu.SMEM)


def vmem():
    return pl.BlockSpec(memory_space=pltpu.VMEM)


def select(place, block, width, top, chain, capacity, count):
    return pl.pallas_call(
        functools.partial(select_kernel, top, chain, capacity),
        out_shape=[jax.ShapeDtypeStruct((capacity, width), jnp.bfloat16)] * count,
        in_specs=[smem(), vmem()],
        out_specs=[vmem()] * count,
        compiler_params=pltpu.CompilerParams(vmem_limit_bytes=VMEM_BYTES),
        cost_estimate=pl.CostEstimate(flops=0, bytes_accessed=6 * block.size, transcendentals=0),
        name="select",
    )(place, block)


def expert_kernel(pieces, half, *refs):
    rows, (gate0, gate1, up0, up1, down0, down1) = refs[:pieces], refs[pieces : pieces + 6]
    outs, (x, total) = refs[pieces + 6 : -2], refs[-2:]
    step = pl.program_id(0)
    size = rows[0].shape[0]

    @pl.when(step == 0)
    def _():
        x[...] = jnp.concatenate([r[...].astype(jnp.float32) for r in rows], axis=0).astype(jnp.bfloat16)

    def part(gate, up, down, first):
        both = jnp.concatenate([gate[...], up[...]], axis=1)
        product = jnp.dot(x[...], both, preferred_element_type=jnp.float32)
        tile = gate.shape[1]
        g, u = product[:, :tile], product[:, tile:]
        hidden = (g / (1.0 + jnp.exp(-g)) * u).astype(jnp.bfloat16)
        out = jnp.dot(hidden, down[...], preferred_element_type=jnp.float32)

        @pl.when(step == 0)
        def _():
            total[...] = out

        @pl.when(step > 0)
        def _():
            total[...] += out

    @pl.when(step < half)
    def _():
        part(gate0, up0, down0, True)

    @pl.when(step >= half)
    def _():
        part(gate1, up1, down1, False)

    @pl.when(step == 2 * half - 1)
    def _():
        for i, out in enumerate(outs):
            out[...] = total[i * size : (i + 1) * size, :].astype(jnp.bfloat16)


def expert(rows, own, other):
    size, width = rows[0].shape
    count = size * len(rows)
    hidden = own[0].shape[1]
    tile = LANES
    half = hidden // tile
    first = lambda i: jnp.minimum(i, half - 1)
    second = lambda i: jnp.maximum(i - half, 0)
    column = lambda at: pl.BlockSpec((width, tile), lambda i: (0, at(i)))
    row = lambda at: pl.BlockSpec((tile, width), lambda i: (at(i), 0))
    whole = pl.BlockSpec((size, width), lambda i: (0, 0))
    return pl.pallas_call(
        functools.partial(expert_kernel, len(rows), half),
        grid=(2 * half,),
        out_shape=[jax.ShapeDtypeStruct((size, width), jnp.bfloat16)] * len(rows),
        in_specs=[whole] * len(rows)
        + [column(first), column(second), column(first), column(second), row(first), row(second)],
        out_specs=[whole] * len(rows),
        scratch_shapes=[pltpu.VMEM((count, width), jnp.bfloat16), pltpu.VMEM((count, width), jnp.float32)],
        compiler_params=pltpu.CompilerParams(vmem_limit_bytes=VMEM_BYTES),
        cost_estimate=pl.CostEstimate(
            flops=12 * count * width * hidden, bytes_accessed=12 * width * hidden + 4 * count * width, transcendentals=0
        ),
        name="expert",
    )(*rows, own[0], other[0], own[1], other[1], own[2], other[2])


def combine_kernel(top, chain, capacity, count, place, block, *refs):
    results, others, out = refs[:count], refs[count:-1], refs[-1]
    meta = block[...].astype(jnp.float32)
    total = None
    for other in others:
        value = other[...].astype(jnp.float32)
        total = value if total is None else total + value
    for (hot, weight), result in zip(slots(place, meta, top, chain, capacity, count), results):
        scaled = hot * weight
        high = scaled.astype(jnp.bfloat16)
        low = (scaled - high.astype(jnp.float32)).astype(jnp.bfloat16)
        value = result[...]
        piece = jnp.dot(high, value, preferred_element_type=jnp.float32)
        piece = piece + jnp.dot(low, value, preferred_element_type=jnp.float32)
        total = piece if total is None else total + piece
    out[...] = total.astype(jnp.bfloat16)


def combine(place, block, results, others, top, chain):
    capacity, width = results[0].shape
    rows = block.shape[0]
    lead = pl.BlockSpec((rows, LANES), lambda i: (0, width // LANES))
    whole = lambda shape: pl.BlockSpec(shape, lambda i: (0, 0))
    return pl.pallas_call(
        functools.partial(combine_kernel, top, chain, capacity, len(results)),
        grid=(1,),
        out_shape=jax.ShapeDtypeStruct((rows, width), jnp.bfloat16),
        in_specs=[smem(), lead] + [whole((capacity, width))] * len(results) + [whole((rows, width))] * len(others),
        out_specs=whole((rows, width)),
        compiler_params=pltpu.CompilerParams(vmem_limit_bytes=VMEM_BYTES),
        cost_estimate=pl.CostEstimate(
            flops=0, bytes_accessed=2 * width * (rows * (1 + len(others)) + capacity * len(results)), transcendentals=0
        ),
        name="combine",
    )(place, block, *results, *others)


def per_device(tokens, expert_ids, gate_weights, w_gate, w_up, w_down):
    nodes = lax.axis_size("node")
    chain = lax.axis_size("local") // 2
    rows, top = expert_ids.shape
    width = tokens.shape[1]
    capacity = rows * top * 5 // (4 * nodes * chain)
    capacity = -(-capacity // 8) * 8
    place = jnp.stack([lax.axis_index("node"), lax.axis_index("local") // 2]).astype(jnp.int32)

    packed = pack_block(tokens, expert_ids, gate_weights)
    blocks = [packed] + [swap(packed, "local", 2 * step) for step in range(1, chain)]
    own = (w_gate, w_up, w_down)
    other = tuple(swap(weight, "local", 1) for weight in own)

    groups = [[0]]
    while groups[-1][-1] + 1 < chain:
        start = groups[-1][-1] + 1
        groups.append(list(range(start, 2 * start)))
    back = {}
    for group in groups:
        arrived = []
        for step in group:
            picked = select(place, blocks[step], width, top, chain, capacity, nodes)
            arrived += [picked[0]] + [swap(picked[n], "node", n) for n in range(1, nodes)]
        results = expert(arrived, own, other)
        for i, step in enumerate(group):
            back[step] = results[i * nodes : (i + 1) * nodes]
    sums = []
    for step in list(range(1, chain)) + [0]:
        result = back[step]
        returned = [result[0]] + [swap(result[n], "node", n) for n in range(1, nodes)]
        if step:
            partial = combine(place, blocks[step], returned, [], top, chain)
            sums.append(swap(partial, "local", 2 * step))
    return combine(place, packed, returned, sums, top, chain)


def solution(mesh):
    spread = ("parts", "node", "local")
    placed = (P(spread, None), P(spread, None), P(spread, None), P(None, spread), P(None, spread), P(spread, None))
    return jax.shard_map(
        per_device, mesh=mesh, in_specs=placed, out_specs=P(spread, None), check_vma=False
    )
```

time: 377 us -> 208 us (0.55)
  waiting for transfers between devices: 279 us -> 92.2 us
  Pallas kernels: 0 us -> 68.3 us
  local copies, waits for them, and re-layouts: 44.4 us -> 1.07 us
  matrix products: 31.9 us -> 0 us
  starting transfers between devices: 12.2 us -> 43.4 us
  other arithmetic: 8.92 us -> 2.64 us
    all_to_all x2 -> x0, waiting for transfers between devices: 279 us -> none  [the longest x1 139 us: per_device(): lax.all_to_all(processed, ('node', 'local'), split_axis=0, concat_axis=0,...]
    ppermute x3 -> x33, waiting for transfers between devices: 0.01 us -> 92.2 us  [swap(): return lax.ppermute(value, axis, pairs)]
    pallas_call x0 -> x11, Pallas kernels: none -> 68.3 us  [the longest x3 53.2 us: expert(): pl.pallas_call(functools.partial(expert_kernel, len(rows), half), grid=(2...]
    ppermute x3 -> x33, starting transfers between devices: 0.66 us -> 43.4 us  [swap(): return lax.ppermute(value, axis, pairs)]
    dot_general x3 -> x0, matrix products: 31.9 us -> none  [the longest x1 19.5 us: per_device(): jnp.dot(hidden, full_down, preferred_element_type=jnp.float32)]
    reshape x4 -> x0, local copies, waits for them, and re-layouts: 30.9 us -> none  [the longest x1 7.84 us: per_device(): rows = block.reshape(-1, width)]
    gather x1 -> x0, local copies, waits for them, and re-layouts: 11.8 us -> none  [per_device(): chosen = results[slot_index]]
    all_to_all x2 -> x0, starting transfers between devices: 11.6 us -> none  [the longest x1 7.59 us: per_device(): lax.all_to_all(outgoing, ('node', 'local'), split_axis=0, concat_axis=0,...]
  transfers between devices with their start and end apart: 5 -> 33, of which waited for: 2 -> 8; matrix products, arithmetic and copies ran while one was open for 4% -> 2% of each run, Pallas kernels for 0% -> 31%
where the time goes in v1:
time: 208 us
  waiting for transfers between devices  92.2 us (44%)
  Pallas kernels  68.3 us (33%)
  starting transfers between devices  43.4 us (21%)
  other arithmetic  2.64 us (1%)
    ppermute x33, waiting for transfers between devices, swap(): return lax.ppermute(value, axis, pairs)  92.2 us
    pallas_call x3, Pallas kernels, expert(): pl.pallas_call(functools.partial(expert_kernel, len(rows), half), grid=(2...  53.2 us
    ppermute x33, starting transfers between devices, swap(): return lax.ppermute(value, axis, pairs)  43.4 us
    pallas_call x4, Pallas kernels, combine(): pl.pallas_call(functools.partial(combine_kernel, top, chain, capacity, le...  9.28 us
    pallas_call x4, Pallas kernels, select(): pl.pallas_call(functools.partial(select_kernel, top, chain, capacity), ou...  5.86 us
  transfers between devices with their start and end apart: 33, of which 8 were waited for; matrix products, arithmetic and copies ran while one was open for 2% of the time, Pallas kernels for 31%

profile of v1, /device:TPU:0, one launch (start us, length us, event | category | flops | bytes accessed | tf_op | source)
XLA Modules:
  0.0 207.9 jit_solution(10834091125719160938)
XLA Ops:
  4.6 3.7 %collective-permute-start.17 = (bf16[64,4224]{1,0:T(8,128)(2,1)S(1)}, bf16[64,4224]{1,0:T(8,128)(2,1)S(1)}, u32[]{:S(2)}, u32[]{:S(2)}) collective-permute-start(bf16[64,4224]{1,0:T(8,128)(2,1)S(1)} %pad_maximum_fusion.block), channel_id=1, source_target_pairs={{0,4},{1,5},{2,6},{3,7},{4,0},{5,1},{6,2},{7,3},{8,12},{9,13},{10,... | collective-permute-start | bytes 1622024 | tf_op jit(solution)/shard_map/ppermute | solution.py:16
  8.3 1.5 select.29
  9.8 1.6 collective-permute-start
  11.4 8.4 %collective-permute-done.refs_1_ = bf16[40,4096]{1,0:T(8,128)(2,1)S(1)} collective-permute-done((bf16[40,4096]{1,0:T(8,128)(2,1)S(1)}, bf16[40,4096]{1,0:T(8,128)(2,1)S(1)}, u32[]{:S(2)}, u32[]{:S(2)}) %collective-permute-start) | collective-permute-done | bytes 327712 | tf_op jit(solution)/shard_map/ppermute | solution.py:16
  21.1 23.5 %collective-permute-done.17.block = bf16[64,4224]{1,0:T(8,128)(2,1)S(1)} collective-permute-done((bf16[64,4224]{1,0:T(8,128)(2,1)S(1)}, bf16[64,4224]{1,0:T(8,128)(2,1)S(1)}, u32[]{:S(2)}, u32[]{:S(2)}) %collective-permute-start.17) | collective-permute-done | bytes 540704 | tf_op jit(solution)/shard_map/ppermute | solution.py:16
  45.1 1.5 select.31
  46.6 1.6 collective-permute-start.18
  48.2 10.3 %collective-permute-done.9.block = bf16[64,4224]{1,0:T(8,128)(2,1)S(1)} collective-permute-done((bf16[64,4224]{1,0:T(8,128)(2,1)S(1)}, bf16[64,4224]{1,0:T(8,128)(2,1)S(1)}, u32[]{:S(2)}, u32[]{:S(2)}) %collective-permute-start.9) | collective-permute-done | bytes 540704 | tf_op jit(solution)/shard_map/ppermute | solution.py:16
  59.8 1.5 select.32
  61.3 1.5 collective-permute-start.20
  62.8 11.1 %collective-permute-done.19.refs_2_ = bf16[40,4096]{1,0:T(8,128)(2,1)S(1)} collective-permute-done((bf16[40,4096]{1,0:T(8,128)(2,1)S(1)}, bf16[40,4096]{1,0:T(8,128)(2,1)S(1)}, u32[]{:S(2)}, u32[]{:S(2)}) %collective-permute-start.19) | collective-permute-done | bytes 327712 | tf_op jit(solution)/shard_map/ppermute | solution.py:16
  74.9 1.5 collective-permute-start.23
  76.4 6.2 %collective-permute-done.22.refs_5_ = bf16[40,4096]{1,0:T(8,128)(2,1)S(1)} collective-permute-done((bf16[40,4096]{1,0:T(8,128)(2,1)S(1)}, bf16[40,4096]{1,0:T(8,128)(2,1)S(1)}, u32[]{:S(2)}, u32[]{:S(2)}) %collective-permute-start.22) | collective-permute-done | bytes 327712 | tf_op jit(solution)/shard_map/ppermute | solution.py:16
  82.7 1.4 collective-permute-start.24
  84.0 1.5 select.30
  85.5 6.6 %collective-permute-done.23.refs_6_ = bf16[40,4096]{1,0:T(8,128)(2,1)S(1)} collective-permute-done((bf16[40,4096]{1,0:T(8,128)(2,1)S(1)}, bf16[40,4096]{1,0:T(8,128)(2,1)S(1)}, u32[]{:S(2)}, u32[]{:S(2)}) %collective-permute-start.23) | collective-permute-done | bytes 327712 | tf_op jit(solution)/shard_map/ppermute | solution.py:16
  92.2 2.5 %collective-permute-start.1 = (bf16[40,4096]{1,0:T(8,128)(2,1)S(1)}, bf16[40,4096]{1,0:T(8,128)(2,1)S(1)}, u32[]{:S(2)}, u32[]{:S(2)}) collective-permute-start(bf16[40,4096]{1,0:T(8,128)(2,1)S(1)} %get-tuple-element.39), channel_id=1, source_target_pairs={{0,16},{8,24},{16,0},{24,8},{1,17},{9,25},{17,1},{25,9},{2,18},{10... | collective-permute-start | bytes 983048 | tf_op jit(solution)/shard_map/ppermute | solution.py:16
  96.2 1.9 collective-permute-start.11
  99.0 24.5 %expert.5 = (bf16[40,4096]{1,0:T(8,128)(2,1)S(1)}, bf16[40,4096]{1,0:T(8,128)(2,1)S(1)}, bf16[40,4096]{1,0:T(8,128)(2,1)S(1)}, bf16[40,4096]{1,0:T(8,128)(2,1)S(...) custom-call(bf16[40,4096]{1,0:T(8,128)(2,1)S(1)} %get-tuple-element., ...), custom_call_target="tpu_custom_call" | custom-call | flops 6039797760 | bytes 24117248 | tf_op jit(solution)/shard_map/expert/pallas_call | solution.py:138
  124.3 1.9 collective-permute-start.30
  127.8 1.9 collective-permute-start.26
  129.7 14.4 %expert.4 = (bf16[40,4096]{1,0:T(8,128)(2,1)S(1)}, bf16[40,4096]{1,0:T(8,128)(2,1)S(1)}, bf16[40,4096]{1,0:T(8,128)(2,1)S(1)}, bf16[40,4096]{1,0:T(8,128)(2,1)S(1)}) custom-call(bf16[40,4096]{1,0:T(8,128)(2,1)S(1)} %get-tuple-element.45.refs_0_, bf16[40,4096]{1,0:T(8,128)(2,1)S(1)} %collective-permute-done.10.refs_1_, ...), custom_call_target="tpu_custom_call" | custom-call | flops 3019898880 | bytes 21495808 | tf_op jit(solution)/shard_map/expert/pallas_call | solution.py:138
  145.7 1.9 collective-permute-start.14
  148.5 14.4 %expert.3 = (bf16[40,4096]{1,0:T(8,128)(2,1)S(1)}, bf16[40,4096]{1,0:T(8,128)(2,1)S(1)}, bf16[40,4096]{1,0:T(8,128)(2,1)S(1)}, bf16[40,4096]{1,0:T(8,128)(2,1)S(1)}) custom-call(bf16[40,4096]{1,0:T(8,128)(2,1)S(1)} %get-tuple-element.37.refs_0_, bf16[40,4096]{1,0:T(8,128)(2,1)S(1)} %collective-permute-done.refs_1_, ...), custom_call_target="tpu_custom_call" | custom-call | flops 3019898880 | bytes 21495808 | tf_op jit(solution)/shard_map/expert/pallas_call | solution.py:138
  163.6 2.1 %combine.6 = bf16[64,4096]{1,0:T(8,128)(2,1)S(1)} custom-call(s32[2]{0:T(128)S(1)} %pad_add_fusion.place, bf16[64,4224]{1,0:T(8,128)(2,1)S(1)} %collective-permute-done.21.block, bf16[40,4096]{1,0:T(8,128)(2,1)S(1)} %get-tuple-element.65.refs_0_, bf16[40,4096]{1,0:T(8,128)(2,1)S(1)} %collective-permute-done.29.refs_1_, ...), custom_call_target="tpu_custom_call" | custom-call | bytes 1835008 | tf_op jit(solution)/shard_map/combine/pallas_call | solution.py:177
  165.8 5.1 %collective-permute-start.32 = (bf16[64,4096]{1,0:T(8,128)(2,1)S(1)}, bf16[64,4096]{1,0:T(8,128)(2,1)S(1)}, u32[]{:S(2)}, u32[]{:S(2)}) collective-permute-start(bf16[64,4096]{1,0:T(8,128)(2,1)S(1)} %combine.6), channel_id=1, source_target_pairs={{0,6},{1,7},{2,4},{3,5},{4,2},{5,3},{6,0},{7,1},{8,14},{9,15},{10,... | collective-permute-start | bytes 1572872 | tf_op jit(solution)/shard_map/ppermute | solution.py:16
  170.9 2.1 %combine.5 = bf16[64,4096]{1,0:T(8,128)(2,1)S(1)} custom-call(s32[2]{0:T(128)S(1)} %pad_add_fusion.place, bf16[64,4224]{1,0:T(8,128)(2,1)S(1)} %collective-permute-done.17.block, bf16[40,4096]{1,0:T(8,128)(2,1)S(1)} %get-tuple-element.61.refs_0_, bf16[40,4096]{1,0:T(8,128)(2,1)S(1)} %collective-permute-done.25.refs_1_, ...), custom_call_target="tpu_custom_call" | custom-call | bytes 1835008 | tf_op jit(solution)/shard_map/combine/pallas_call | solution.py:177
  173.4 2.1 %combine.4 = bf16[64,4096]{1,0:T(8,128)(2,1)S(1)} custom-call(s32[2]{0:T(128)S(1)} %pad_add_fusion.place, bf16[64,4224]{1,0:T(8,128)(2,1)S(1)} %collective-permute-done.9.block, bf16[40,4096]{1,0:T(8,128)(2,1)S(1)} %get-tuple-element.49.refs_0_, bf16[40,4096]{1,0:T(8,128)(2,1)S(1)} %collective-permute-done.13.refs_1_, ...), custom_call_target="tpu_custom_call" | custom-call | bytes 1835008 | tf_op jit(solution)/shard_map/combine/pallas_call | solution.py:177
  176.2 1.8 collective-permute-start.7
  178.9 7.8 %collective-permute-done.7.refs_2_ = bf16[40,4096]{1,0:T(8,128)(2,1)S(1)} collective-permute-done((bf16[40,4096]{1,0:T(8,128)(2,1)S(1)}, bf16[40,4096]{1,0:T(8,128)(2,1)S(1)}, u32[]{:S(2)}, u32[]{:S(2)}) %collective-permute-start.7) | collective-permute-done | bytes 327712 | tf_op jit(solution)/shard_map/ppermute | solution.py:16
  186.8 18.2 %collective-permute-done.28.refs_5_ = bf16[64,4096]{1,0:T(8,128)(2,1)S(1)} collective-permute-done((bf16[64,4096]{1,0:T(8,128)(2,1)S(1)}, bf16[64,4096]{1,0:T(8,128)(2,1)S(1)}, u32[]{:S(2)}, u32[]{:S(2)}) %collective-permute-start.28) | collective-permute-done | bytes 524320 | tf_op jit(solution)/shard_map/ppermute | solution.py:16
  204.9 2.9 %combine.7 = bf16[64,4096]{1,0:T(8,128)(2,1)} custom-call(s32[2]{0:T(128)S(1)} %pad_add_fusion.place, bf16[64,4224]{1,0:T(8,128)(2,1)S(1)} %pad_maximum_fusion.block, bf16[40,4096]{1,0:T(8,128)(2,1)S(1)} %get-tuple-element.41.refs_0_, bf16[40,4096]{1,0:T(8,128)(2,1)S(1)} %collective-permute-done.6.refs_1_, ...), custom_call_target="tpu_custom_call" | custom-call | bytes 3407872 | tf_op jit(solution)/shard_map/combine/pallas_call | solution.py:177
  (63 shorter events, 18.9 us)
Async XLA Ops:
  0.0 95.5 %collective-permute-start.3 = (bf16[4096,384]{1,0:T(8,128)(2,1)}, bf16[4096,384]{1,0:T(8,128)(2,1)}, u32[]{:S(2)}, u32[]{:S(2)}) collective-permute-start(bf16[4096,384]{1,0:T(8,128)(2,1)} %refs_8_.5), channel_id=1, source_target_pairs={{0,1},{1,0},{2,3},{3,2},{4,5},{5,4},{6,7},{7,6},{8,9},{9,8},{10,11... | collective-permute-start | bytes 9437192 | tf_op jit(solution)/shard_map/ppermute | solution.py:16
  0.5 95.7 %collective-permute-start.4 = (bf16[4096,384]{1,0:T(8,128)(2,1)}, bf16[4096,384]{1,0:T(8,128)(2,1)}, u32[]{:S(2)}, u32[]{:S(2)}) collective-permute-start(bf16[4096,384]{1,0:T(8,128)(2,1)} %refs_10_.1), channel_id=1, source_target_pairs={{0,1},{1,0},{2,3},{3,2},{4,5},{5,4},{6,7},{7,6},{8,9},{9,8},{10,11... | collective-permute-start | bytes 9437192 | tf_op jit(solution)/shard_map/ppermute | solution.py:16
  0.5 97.6 %collective-permute-start.5 = (bf16[384,4096]{1,0:T(8,128)(2,1)}, bf16[384,4096]{1,0:T(8,128)(2,1)}, u32[]{:S(2)}, u32[]{:S(2)}) collective-permute-start(bf16[384,4096]{1,0:T(8,128)(2,1)} %refs_12_.1), channel_id=1, source_target_pairs={{0,1},{1,0},{2,3},{3,2},{4,5},{5,4},{6,7},{7,6},{8,9},{9,8},{10,11... | collective-permute-start | bytes 9437192 | tf_op jit(solution)/shard_map/ppermute | solution.py:16
  4.6 40.0 %collective-permute-start.17 = (bf16[64,4224]{1,0:T(8,128)(2,1)S(1)}, bf16[64,4224]{1,0:T(8,128)(2,1)S(1)}, u32[]{:S(2)}, u32[]{:S(2)}) collective-permute-start(bf16[64,4224]{1,0:T(8,128)(2,1)S(1)} %pad_maximum_fusion.block), channel_id=1, source_target_pairs={{0,4},{1,5},{2,6},{3,7},{4,0},{5,1},{6,2},{7,3},{8,12},{9,13},{10,... | collective-permute-start | bytes 1622024 | tf_op jit(solution)/shard_map/ppermute | solution.py:16
  9.8 9.9 %collective-permute-start = (bf16[40,4096]{1,0:T(8,128)(2,1)S(1)}, bf16[40,4096]{1,0:T(8,128)(2,1)S(1)}, u32[]{:S(2)}, u32[]{:S(2)}) collective-permute-start(bf16[40,4096]{1,0:T(8,128)(2,1)S(1)} %get-tuple-element.38), channel_id=1, source_target_pairs={{0,8},{8,0},{16,24},{24,16},{1,9},{9,1},{17,25},{25,17},{2,10},{10... | collective-permute-start | bytes 983048 | tf_op jit(solution)/shard_map/ppermute | solution.py:16
  19.7 26.9 %collective-permute-start.21 = (bf16[64,4224]{1,0:T(8,128)(2,1)S(1)}, bf16[64,4224]{1,0:T(8,128)(2,1)S(1)}, u32[]{:S(2)}, u32[]{:S(2)}) collective-permute-start(bf16[64,4224]{1,0:T(8,128)(2,1)S(1)} %pad_maximum_fusion.block), channel_id=1, source_target_pairs={{0,6},{1,7},{2,4},{3,5},{4,2},{5,3},{6,0},{7,1},{8,14},{9,15},{10,... | collective-permute-start | bytes 1622024 | tf_op jit(solution)/shard_map/ppermute | solution.py:16
  44.6 13.9 %collective-permute-start.9 = (bf16[64,4224]{1,0:T(8,128)(2,1)S(1)}, bf16[64,4224]{1,0:T(8,128)(2,1)S(1)}, u32[]{:S(2)}, u32[]{:S(2)}) collective-permute-start(bf16[64,4224]{1,0:T(8,128)(2,1)S(1)} %pad_maximum_fusion.block), channel_id=1, source_target_pairs={{0,2},{1,3},{2,0},{3,1},{4,6},{5,7},{6,4},{7,5},{8,10},{9,11},{10,... | collective-permute-start | bytes 1622024 | tf_op jit(solution)/shard_map/ppermute | solution.py:16
  46.6 14.7 %collective-permute-start.18 = (bf16[40,4096]{1,0:T(8,128)(2,1)S(1)}, bf16[40,4096]{1,0:T(8,128)(2,1)S(1)}, u32[]{:S(2)}, u32[]{:S(2)}) collective-permute-start(bf16[40,4096]{1,0:T(8,128)(2,1)S(1)} %get-tuple-element.54), channel_id=1, source_target_pairs={{0,8},{8,0},{16,24},{24,16},{1,9},{9,1},{17,25},{25,17},{2,10},{10... | collective-permute-start | bytes 983048 | tf_op jit(solution)/shard_map/ppermute | solution.py:16
  58.5 15.5 %collective-permute-start.19 = (bf16[40,4096]{1,0:T(8,128)(2,1)S(1)}, bf16[40,4096]{1,0:T(8,128)(2,1)S(1)}, u32[]{:S(2)}, u32[]{:S(2)}) collective-permute-start(bf16[40,4096]{1,0:T(8,128)(2,1)S(1)} %get-tuple-element.55), channel_id=1, source_target_pairs={{0,16},{8,24},{16,0},{24,8},{1,17},{9,25},{17,1},{25,9},{2,18},{10... | collective-permute-start | bytes 983048 | tf_op jit(solution)/shard_map/ppermute | solution.py:16
  61.3 13.5 %collective-permute-start.20 = (bf16[40,4096]{1,0:T(8,128)(2,1)S(1)}, bf16[40,4096]{1,0:T(8,128)(2,1)S(1)}, u32[]{:S(2)}, u32[]{:S(2)}) collective-permute-start(bf16[40,4096]{1,0:T(8,128)(2,1)S(1)} %get-tuple-element.56), channel_id=1, source_target_pairs={{0,24},{8,16},{16,8},{24,0},{1,25},{9,17},{17,9},{25,1},{2,26},{10... | collective-permute-start | bytes 983048 | tf_op jit(solution)/shard_map/ppermute | solution.py:16
  74.9 17.3 %collective-permute-start.23 = (bf16[40,4096]{1,0:T(8,128)(2,1)S(1)}, bf16[40,4096]{1,0:T(8,128)(2,1)S(1)}, u32[]{:S(2)}, u32[]{:S(2)}) collective-permute-start(bf16[40,4096]{1,0:T(8,128)(2,1)S(1)} %get-tuple-element.59), channel_id=1, source_target_pairs={{0,16},{8,24},{16,0},{24,8},{1,17},{9,25},{17,1},{25,9},{2,18},{10... | collective-permute-start | bytes 983048 | tf_op jit(solution)/shard_map/ppermute | solution.py:16
  82.7 12.0 %collective-permute-start.24 = (bf16[40,4096]{1,0:T(8,128)(2,1)S(1)}, bf16[40,4096]{1,0:T(8,128)(2,1)S(1)}, u32[]{:S(2)}, u32[]{:S(2)}) collective-permute-start(bf16[40,4096]{1,0:T(8,128)(2,1)S(1)} %get-tuple-element.60), channel_id=1, source_target_pairs={{0,24},{8,16},{16,8},{24,0},{1,25},{9,17},{17,9},{25,1},{2,26},{10... | collective-permute-start | bytes 983048 | tf_op jit(solution)/shard_map/ppermute | solution.py:16
  92.2 31.3 %collective-permute-start.1 = (bf16[40,4096]{1,0:T(8,128)(2,1)S(1)}, bf16[40,4096]{1,0:T(8,128)(2,1)S(1)}, u32[]{:S(2)}, u32[]{:S(2)}) collective-permute-start(bf16[40,4096]{1,0:T(8,128)(2,1)S(1)} %get-tuple-element.39), channel_id=1, source_target_pairs={{0,16},{8,24},{16,0},{24,8},{1,17},{9,25},{17,1},{25,9},{2,18},{10... | collective-permute-start | bytes 983048 | tf_op jit(solution)/shard_map/ppermute | solution.py:16
  94.7 29.6 %collective-permute-start.2 = (bf16[40,4096]{1,0:T(8,128)(2,1)S(1)}, bf16[40,4096]{1,0:T(8,128)(2,1)S(1)}, u32[]{:S(2)}, u32[]{:S(2)}) collective-permute-start(bf16[40,4096]{1,0:T(8,128)(2,1)S(1)} %get-tuple-element.40), channel_id=1, source_target_pairs={{0,24},{8,16},{16,8},{24,0},{1,25},{9,17},{17,9},{25,1},{2,26},{10... | collective-permute-start | bytes 983048 | tf_op jit(solution)/shard_map/ppermute | solution.py:16
  95.5 30.7 %collective-permute-start.10 = (bf16[40,4096]{1,0:T(8,128)(2,1)S(1)}, bf16[40,4096]{1,0:T(8,128)(2,1)S(1)}, u32[]{:S(2)}, u32[]{:S(2)}) collective-permute-start(bf16[40,4096]{1,0:T(8,128)(2,1)S(1)} %get-tuple-element.46), channel_id=1, source_target_pairs={{0,8},{8,0},{16,24},{24,16},{1,9},{9,1},{17,25},{25,17},{2,10},{10... | collective-permute-start | bytes 983048 | tf_op jit(solution)/shard_map/ppermute | solution.py:16
  96.2 30.8 %collective-permute-start.11 = (bf16[40,4096]{1,0:T(8,128)(2,1)S(1)}, bf16[40,4096]{1,0:T(8,128)(2,1)S(1)}, u32[]{:S(2)}, u32[]{:S(2)}) collective-permute-start(bf16[40,4096]{1,0:T(8,128)(2,1)S(1)} %get-tuple-element.47), channel_id=1, source_target_pairs={{0,16},{8,24},{16,0},{24,8},{1,17},{9,25},{17,1},{25,9},{2,18},{10... | collective-permute-start | bytes 983048 | tf_op jit(solution)/shard_map/ppermute | solution.py:16
  98.2 29.6 %collective-permute-start.12 = (bf16[40,4096]{1,0:T(8,128)(2,1)S(1)}, bf16[40,4096]{1,0:T(8,128)(2,1)S(1)}, u32[]{:S(2)}, u32[]{:S(2)}) collective-permute-start(bf16[40,4096]{1,0:T(8,128)(2,1)S(1)} %get-tuple-element.48), channel_id=1, source_target_pairs={{0,24},{8,16},{16,8},{24,0},{1,25},{9,17},{17,9},{25,1},{2,26},{10... | collective-permute-start | bytes 983048 | tf_op jit(solution)/shard_map/ppermute | solution.py:16
  123.5 20.6 %collective-permute-start.29 = (bf16[40,4096]{1,0:T(8,128)(2,1)S(1)}, bf16[40,4096]{1,0:T(8,128)(2,1)S(1)}, u32[]{:S(2)}, u32[]{:S(2)}) collective-permute-start(bf16[40,4096]{1,0:T(8,128)(2,1)S(1)} %get-tuple-element.66), channel_id=1, source_target_pairs={{0,8},{8,0},{16,24},{24,16},{1,9},{9,1},{17,25},{25,17},{2,10},{10... | collective-permute-start | bytes 983048 | tf_op jit(solution)/shard_map/ppermute | solution.py:16
  124.3 20.7 %collective-permute-start.30 = (bf16[40,4096]{1,0:T(8,128)(2,1)S(1)}, bf16[40,4096]{1,0:T(8,128)(2,1)S(1)}, u32[]{:S(2)}, u32[]{:S(2)}) collective-permute-start(bf16[40,4096]{1,0:T(8,128)(2,1)S(1)} %get-tuple-element.67), channel_id=1, source_target_pairs={{0,16},{8,24},{16,0},{24,8},{1,17},{9,25},{17,1},{25,9},{2,18},{10... | collective-permute-start | bytes 983048 | tf_op jit(solution)/shard_map/ppermute | solution.py:16
  126.2 19.5 %collective-permute-start.31 = (bf16[40,4096]{1,0:T(8,128)(2,1)S(1)}, bf16[40,4096]{1,0:T(8,128)(2,1)S(1)}, u32[]{:S(2)}, u32[]{:S(2)}) collective-permute-start(bf16[40,4096]{1,0:T(8,128)(2,1)S(1)} %get-tuple-element.68), channel_id=1, source_target_pairs={{0,24},{8,16},{16,8},{24,0},{1,25},{9,17},{17,9},{25,1},{2,26},{10... | collective-permute-start | bytes 983048 | tf_op jit(solution)/shard_map/ppermute | solution.py:16
  127.0 20.6 %collective-permute-start.25 = (bf16[40,4096]{1,0:T(8,128)(2,1)S(1)}, bf16[40,4096]{1,0:T(8,128)(2,1)S(1)}, u32[]{:S(2)}, u32[]{:S(2)}) collective-permute-start(bf16[40,4096]{1,0:T(8,128)(2,1)S(1)} %get-tuple-element.62), channel_id=1, source_target_pairs={{0,8},{8,0},{16,24},{24,16},{1,9},{9,1},{17,25},{25,17},{2,10},{10... | collective-permute-start | bytes 983048 | tf_op jit(solution)/shard_map/ppermute | solution.py:16
  127.8 35.1 %collective-permute-start.26 = (bf16[40,4096]{1,0:T(8,128)(2,1)S(1)}, bf16[40,4096]{1,0:T(8,128)(2,1)S(1)}, u32[]{:S(2)}, u32[]{:S(2)}) collective-permute-start(bf16[40,4096]{1,0:T(8,128)(2,1)S(1)} %get-tuple-element.63), channel_id=1, source_target_pairs={{0,16},{8,24},{16,0},{24,8},{1,17},{9,25},{17,1},{25,9},{2,18},{10... | collective-permute-start | bytes 983048 | tf_op jit(solution)/shard_map/ppermute | solution.py:16
  144.1 21.7 %collective-permute-start.27 = (bf16[40,4096]{1,0:T(8,128)(2,1)S(1)}, bf16[40,4096]{1,0:T(8,128)(2,1)S(1)}, u32[]{:S(2)}, u32[]{:S(2)}) collective-permute-start(bf16[40,4096]{1,0:T(8,128)(2,1)S(1)} %get-tuple-element.64), channel_id=1, source_target_pairs={{0,24},{8,16},{16,8},{24,0},{1,25},{9,17},{17,9},{25,1},{2,26},{10... | collective-permute-start | bytes 983048 | tf_op jit(solution)/shard_map/ppermute | solution.py:16
  145.0 28.0 %collective-permute-start.13 = (bf16[40,4096]{1,0:T(8,128)(2,1)S(1)}, bf16[40,4096]{1,0:T(8,128)(2,1)S(1)}, u32[]{:S(2)}, u32[]{:S(2)}) collective-permute-start(bf16[40,4096]{1,0:T(8,128)(2,1)S(1)} %get-tuple-element.50), channel_id=1, source_target_pairs={{0,8},{8,0},{16,24},{24,16},{1,9},{9,1},{17,25},{25,17},{2,10},{10... | collective-permute-start | bytes 983048 | tf_op jit(solution)/shard_map/ppermute | solution.py:16
  145.7 27.7 %collective-permute-start.14 = (bf16[40,4096]{1,0:T(8,128)(2,1)S(1)}, bf16[40,4096]{1,0:T(8,128)(2,1)S(1)}, u32[]{:S(2)}, u32[]{:S(2)}) collective-permute-start(bf16[40,4096]{1,0:T(8,128)(2,1)S(1)} %get-tuple-element.51), channel_id=1, source_target_pairs={{0,16},{8,24},{16,0},{24,8},{1,17},{9,25},{17,1},{25,9},{2,18},{10... | collective-permute-start | bytes 983048 | tf_op jit(solution)/shard_map/ppermute | solution.py:16
  147.7 25.7 %collective-permute-start.15 = (bf16[40,4096]{1,0:T(8,128)(2,1)S(1)}, bf16[40,4096]{1,0:T(8,128)(2,1)S(1)}, u32[]{:S(2)}, u32[]{:S(2)}) collective-permute-start(bf16[40,4096]{1,0:T(8,128)(2,1)S(1)} %get-tuple-element.52), channel_id=1, source_target_pairs={{0,24},{8,16},{16,8},{24,0},{1,25},{9,17},{17,9},{25,1},{2,26},{10... | collective-permute-start | bytes 983048 | tf_op jit(solution)/shard_map/ppermute | solution.py:16
  162.9 15.1 %collective-permute-start.6 = (bf16[40,4096]{1,0:T(8,128)(2,1)S(1)}, bf16[40,4096]{1,0:T(8,128)(2,1)S(1)}, u32[]{:S(2)}, u32[]{:S(2)}) collective-permute-start(bf16[40,4096]{1,0:T(8,128)(2,1)S(1)} %get-tuple-element.42), channel_id=1, source_target_pairs={{0,8},{8,0},{16,24},{24,16},{1,9},{9,1},{17,25},{25,17},{2,10},{10... | collective-permute-start | bytes 983048 | tf_op jit(solution)/shard_map/ppermute | solution.py:16
  165.8 21.0 %collective-permute-start.32 = (bf16[64,4096]{1,0:T(8,128)(2,1)S(1)}, bf16[64,4096]{1,0:T(8,128)(2,1)S(1)}, u32[]{:S(2)}, u32[]{:S(2)}) collective-permute-start(bf16[64,4096]{1,0:T(8,128)(2,1)S(1)} %combine.6), channel_id=1, source_target_pairs={{0,6},{1,7},{2,4},{3,5},{4,2},{5,3},{6,0},{7,1},{8,14},{9,15},{10,... | collective-permute-start | bytes 1572872 | tf_op jit(solution)/shard_map/ppermute | solution.py:16
  173.0 31.9 %collective-permute-start.28 = (bf16[64,4096]{1,0:T(8,128)(2,1)S(1)}, bf16[64,4096]{1,0:T(8,128)(2,1)S(1)}, u32[]{:S(2)}, u32[]{:S(2)}) collective-permute-start(bf16[64,4096]{1,0:T(8,128)(2,1)S(1)} %combine.5), channel_id=1, source_target_pairs={{0,4},{1,5},{2,6},{3,7},{4,0},{5,1},{6,2},{7,3},{8,12},{9,13},{10,... | collective-permute-start | bytes 1572872 | tf_op jit(solution)/shard_map/ppermute | solution.py:16
  175.5 29.4 %collective-permute-start.16 = (bf16[64,4096]{1,0:T(8,128)(2,1)S(1)}, bf16[64,4096]{1,0:T(8,128)(2,1)S(1)}, u32[]{:S(2)}, u32[]{:S(2)}) collective-permute-start(bf16[64,4096]{1,0:T(8,128)(2,1)S(1)} %combine.4), channel_id=1, source_target_pairs={{0,2},{1,3},{2,0},{3,1},{4,6},{5,7},{6,4},{7,5},{8,10},{9,11},{10,... | collective-permute-start | bytes 1572872 | tf_op jit(solution)/shard_map/ppermute | solution.py:16
  176.2 10.6 %collective-permute-start.7 = (bf16[40,4096]{1,0:T(8,128)(2,1)S(1)}, bf16[40,4096]{1,0:T(8,128)(2,1)S(1)}, u32[]{:S(2)}, u32[]{:S(2)}) collective-permute-start(bf16[40,4096]{1,0:T(8,128)(2,1)S(1)} %get-tuple-element.43), channel_id=1, source_target_pairs={{0,16},{8,24},{16,0},{24,8},{1,17},{9,25},{17,1},{25,9},{2,18},{10... | collective-permute-start | bytes 983048 | tf_op jit(solution)/shard_map/ppermute | solution.py:16
  177.9 8.8 %collective-permute-start.8 = (bf16[40,4096]{1,0:T(8,128)(2,1)S(1)}, bf16[40,4096]{1,0:T(8,128)(2,1)S(1)}, u32[]{:S(2)}, u32[]{:S(2)}) collective-permute-start(bf16[40,4096]{1,0:T(8,128)(2,1)S(1)} %get-tuple-element.44), channel_id=1, source_target_pairs={{0,24},{8,16},{16,8},{24,0},{1,25},{9,17},{17,9},{25,1},{2,26},{10... | collective-permute-start | bytes 983048 | tf_op jit(solution)/shard_map/ppermute | solution.py:16
  (5 other events, 73.8 us)

commit v2 on v0

v2 whole, which is shorter than its diff:
```python
import functools

import jax
import jax.numpy as jnp
from jax import lax
from jax.experimental import pallas as pl
from jax.experimental.pallas import tpu as pltpu
from jax.sharding import PartitionSpec as P

LANES = 128
ORDER = [(2,), (3,), (1,), (0,)]
VMEM_BYTES = 34 * 2**20


def swap(value, axis, mask):
    pairs = [(source, source ^ mask) for source in range(lax.axis_size(axis))]
    return lax.ppermute(value, axis, pairs)


def after(value, earlier):
    if not earlier:
        return value
    return lax.optimization_barrier((value, *earlier))[0]


def together(moved, arrived):
    values = lax.optimization_barrier((*moved, *arrived[1:]))
    return values[: len(moved)], [arrived[0], *values[len(moved) :]]


def meta_of(ids, gates):
    rows, top = ids.shape
    parts = [ids[...].astype(jnp.float32)]
    rest = gates[...]
    for _ in range(3):
        piece = rest.astype(jnp.bfloat16).astype(jnp.float32)
        parts.append(piece)
        rest = rest - piece
    lane = lax.broadcasted_iota(jnp.int32, (rows, LANES), 1)
    meta = jnp.zeros((rows, LANES), jnp.float32)
    for i, part in enumerate(parts):
        for k in range(top):
            meta = jnp.where(lane == i * top + k, part[:, k : k + 1], meta)
    return meta


def slots(place, meta, top, chain, capacity, count):
    meta = meta.astype(jnp.float32)
    rows = meta.shape[0]
    node, link = place[0], place[1]
    lane = lax.broadcasted_iota(jnp.int32, (rows, LANES), 1)
    expert = (jnp.bitwise_xor(lane, node) * chain + link).astype(jnp.float32)
    chosen = jnp.zeros((rows, LANES), jnp.float32)
    weight = jnp.zeros((rows, LANES), jnp.float32)
    for k in range(top):
        hit = meta[:, k : k + 1] == expert
        gate = meta[:, top + k : top + k + 1] + meta[:, 2 * top + k : 2 * top + k + 1]
        gate = gate + meta[:, 3 * top + k : 3 * top + k + 1]
        chosen = chosen + jnp.where(hit, 1.0, 0.0)
        weight = weight + jnp.where(hit, gate, 0.0)
    before = lax.broadcasted_iota(jnp.int32, (rows, rows), 0) > lax.broadcasted_iota(jnp.int32, (rows, rows), 1)
    rank = jnp.dot(
        jnp.where(before, 1.0, 0.0).astype(jnp.bfloat16),
        chosen.astype(jnp.bfloat16),
        preferred_element_type=jnp.float32,
    )
    rank = jnp.where(chosen > 0.5, rank, -1.0)
    slot = lax.broadcasted_iota(jnp.int32, (rows, capacity), 1).astype(jnp.float32)
    return [(jnp.where(rank[:, n : n + 1] == slot, 1.0, 0.0), weight[:, n : n + 1]) for n in range(count)]


def smem():
    return pl.BlockSpec(memory_space=pltpu.SMEM)


def vmem():
    return pl.BlockSpec(memory_space=pltpu.VMEM)


def call(kernel, name, place, inputs, outs, scratch=(), flops=0, stay=0):
    moved = sum(2 * v.size for v in inputs) + sum(2 * v.size for v in outs)
    return pl.pallas_call(
        kernel,
        out_shape=outs,
        in_specs=[smem()] + [vmem()] * (len(inputs) - stay) + [pl.BlockSpec(memory_space=pl.ANY)] * stay,
        out_specs=[vmem()] * len(outs),
        scratch_shapes=list(scratch),
        compiler_params=pltpu.CompilerParams(vmem_limit_bytes=VMEM_BYTES),
        cost_estimate=pl.CostEstimate(flops=flops, bytes_accessed=moved, transcendentals=0),
        name=name,
    )(place, *inputs)


def array(*shape):
    return jax.ShapeDtypeStruct(shape, jnp.bfloat16)


def pick(top, chain, capacity, place, meta, tokens, outs):
    for (hot, _), out in zip(slots(place, meta, top, chain, capacity, len(outs)), outs):
        rows = lax.dot_general(
            hot.astype(jnp.bfloat16), tokens, (((0,), (0,)), ((), ())), preferred_element_type=jnp.float32
        )
        out[...] = rows.astype(jnp.bfloat16)


def first_kernel(top, chain, capacity, place, tokens, ids, gates, packed, *outs):
    width = tokens.shape[1]
    meta = meta_of(ids, gates)
    pick(top, chain, capacity, place, meta, tokens[...], outs)
    packed[:, :width] = tokens[...]
    packed[:, width:] = meta.astype(jnp.bfloat16)


def select_kernel(top, chain, capacity, place, block, *outs):
    width = outs[0].shape[1]
    pick(top, chain, capacity, place, block[:, width:], block[:, :width], outs)


def expert_kernel(capacity, count, place, *refs):
    rows, weights, outs = refs[:count], refs[count : count + 6], refs[count + 6 : 2 * count + 6]
    refs = refs[2 * count + 6 :]
    x, hidden, held, sems = refs[0], refs[1], refs[2:8], refs[8]
    cuts = 2
    copies = []
    for i, (source, target) in enumerate(zip(weights, held)):
        step = source.shape[0] // cuts
        copies.append(
            [
                pltpu.make_async_copy(
                    source.at[pl.ds(c * step, step)], target.at[pl.ds(c * step, step)], sems.at[i * cuts + c]
                )
                for c in range(cuts)
            ]
        )
    order = [copies[i + j][c] for i in (0, 3) for c in range(cuts) for j in range(2)]
    order += [copies[i][c] for i in (2, 5) for c in range(cuts)]
    for copy in order:
        copy.start()
    x[...] = jnp.concatenate([ref[...].astype(jnp.float32) for ref in rows], axis=0).astype(jnp.bfloat16)
    size = hidden.shape[1] // 2
    depth = x.shape[1] // 4
    for i in range(2):
        product = None
        for k in range(0, x.shape[1], depth):
            for c in range(cuts):
                if k == c * (x.shape[1] // cuts):
                    copies[3 * i][c].wait()
                    copies[3 * i + 1][c].wait()
            both = jnp.concatenate([held[3 * i][k : k + depth, :], held[3 * i + 1][k : k + depth, :]], axis=1)
            term = jnp.dot(x[:, k : k + depth], both, preferred_element_type=jnp.float32)
            product = term if product is None else product + term
        gate, up = product[:, :size], product[:, size:]
        hidden[:, i * size : (i + 1) * size] = (gate / (1.0 + jnp.exp(-gate)) * up).astype(jnp.bfloat16)
    for i in (2, 5):
        for copy in copies[i]:
            copy.wait()
    tile = 512
    for start in range(0, x.shape[1], tile):
        result = jnp.dot(hidden[:, :size], held[2][:, start : start + tile], preferred_element_type=jnp.float32)
        result += jnp.dot(hidden[:, size:], held[5][:, start : start + tile], preferred_element_type=jnp.float32)
        for n, out in enumerate(outs):
            out[:, start : start + tile] = result[n * capacity : (n + 1) * capacity].astype(jnp.bfloat16)


def weigh(pairs, values):
    total = None
    for (hot, weight), value in zip(pairs, values):
        scaled = hot * weight
        high = scaled.astype(jnp.bfloat16)
        low = (scaled - high.astype(jnp.float32)).astype(jnp.bfloat16)
        for factor in (high, low):
            piece = jnp.dot(factor, value, preferred_element_type=jnp.float32)
            total = piece if total is None else total + piece
    return total


def combine_kernel(top, chain, capacity, count, place, block, *refs):
    results, others, out = refs[:count], refs[count:-1], refs[-1]
    width = out.shape[1]
    total = weigh(slots(place, block[:, width:], top, chain, capacity, count), [ref[...] for ref in results])
    for ref in others:
        total = total + ref[...].astype(jnp.float32)
    out[...] = total.astype(jnp.bfloat16)


def chain_pairs(pairs):
    return [(2 * source + core, 2 * target + core) for source, target in pairs for core in range(2)]


def per_device(tokens, expert_ids, gate_weights, w_gate, w_up, w_down):
    nodes = lax.axis_size("node")
    chain = lax.axis_size("local") // 2
    rows, top = expert_ids.shape
    width = tokens.shape[1]
    capacity = rows * top * 5 // (4 * nodes * chain)
    capacity = -(-capacity // 8) * 8
    spot = lax.axis_index("local") // 2
    place = jnp.stack([lax.axis_index("node"), spot]).astype(jnp.int32)
    sizes = (top, chain, capacity)
    relay = chain == 4
    middle = (spot == 1) | (spot == 2)
    inner, outward, inward = [(1, 2), (2, 1)], [(1, 0), (2, 3)], [(0, 1), (3, 2)]
    hop = lambda value, pairs: lax.ppermute(value, "local", chain_pairs(pairs))
    send = lambda values: [values[0]] + [swap(values[n], "node", n) for n in range(1, nodes)]

    packed, *picked = call(
        functools.partial(first_kernel, *sizes),
        "first",
        place,
        [tokens, expert_ids, gate_weights],
        [array(rows, width + LANES)] + [array(capacity, width)] * nodes,
    )
    arrived = {0: send(picked)}
    own = (w_gate, w_up, w_down)
    other = [swap(w_gate, "local", 1)]
    blocks = [packed]

    def pick_for(step, *token):
        block = after(blocks[step], token)
        picked = call(
            functools.partial(select_kernel, *sizes), "select", place, [block], [array(capacity, width)] * nodes
        )
        arrived[step] = send(picked)

    if relay:
        moved = [swap(packed, "local", 2), hop(after(packed, other), inner)]
        (first, third), arrived[0] = together(moved, arrived[0])
        blocks.append(first)
        pick_for(1)
        moved = [hop(first, inner), hop(third, outward)]
        moved, arrived[1] = together(moved, arrived[1])
        blocks.append(jnp.where(middle, *moved))
        pick_for(2)
        other.append(swap(after(w_up, blocks[2:]), "local", 1))
        (last_hop, other[1]), arrived[2] = together([hop(blocks[2], outward), other[1]], arrived[2])
        blocks.append(jnp.where(middle, third, last_hop))
        pick_for(3)
    else:
        for step in range(1, chain):
            blocks.append(swap(packed, "local", 2 * step))
            pick_for(step)
        other.append(swap(w_up, "local", 1))
    other.append(swap(after(w_down, [other[1], blocks[-1]]), "local", 1))

    def run(group):
        count = nodes * len(group)
        inputs = [value for step in group for value in arrived[step]]
        inputs[0] = after(inputs[0], last)
        outs = call(
            functools.partial(expert_kernel, capacity, count),
            "expert",
            place,
            [*inputs, *own, *other],
            [array(capacity, width)] * count,
            [
                pltpu.VMEM((count * capacity, width), jnp.bfloat16),
                pltpu.VMEM((count * capacity, 2 * w_gate.shape[1]), jnp.bfloat16),
            ]
            + [pltpu.VMEM(weight.shape, weight.dtype) for weight in own * 2]
            + [pltpu.SemaphoreType.DMA((12,))],
            flops=12 * count * capacity * width * w_gate.shape[1],
            stay=6,
        )
        last[:] = [outs[0]]
        for i, step in enumerate(group):
            results[step] = outs[i * nodes : (i + 1) * nodes]

    results, last = {}, []
    for group in ORDER if relay else [(step,) for step in range(chain)]:
        run(group)
    extra = {step: [] for step in range(chain)}
    kept = None
    for step in reversed(range(chain)):
        (total,) = call(
            functools.partial(combine_kernel, *sizes, nodes),
            "combine",
            place,
            [after(blocks[step], last), *send(results[step]), *extra[step]],
            [array(rows, width)],
        )
        last = [total]
        if relay and step == 3:
            kept = total
            extra[2].append(hop(total, inward))
        elif relay and step == 2:
            ends = hop(total, inward).astype(jnp.float32)
            kept = (kept.astype(jnp.float32) + ends).astype(jnp.bfloat16)
            extra[0].append(hop(kept, inner))
            extra[1].append(hop(total, inner))
        elif step:
            extra[0].append(swap(total, "local", 2 * step))
    return total


def solution(mesh):
    spread = ("parts", "node", "local")
    placed = (P(spread, None), P(spread, None), P(spread, None), P(None, spread), P(None, spread), P(spread, None))
    return jax.shard_map(
        per_device, mesh=mesh, in_specs=placed, out_specs=P(spread, None), check_vma=False
    )
```

time: 377 us -> 190 us (0.50)
  waiting for transfers between devices: 279 us -> 74.5 us
  Pallas kernels: 0 us -> 48.5 us
  starting transfers between devices: 12.2 us -> 52.2 us
  local copies, waits for them, and re-layouts: 44.4 us -> 12 us
  matrix products: 31.9 us -> 0 us
  other arithmetic: 8.92 us -> 1.39 us
    all_to_all x2 -> x0, waiting for transfers between devices: 279 us -> none  [the longest x1 139 us: per_device(): lax.all_to_all(processed, ('node', 'local'), split_axis=0, concat_axis=0,...]
    ppermute x3 -> x37, waiting for transfers between devices: 0.01 us -> 74.5 us  [the longest x29 69.1 us: swap(): return lax.ppermute(value, axis, pairs)]
    ppermute x3 -> x37, starting transfers between devices: 0.66 us -> 52.2 us  [the longest x29 35 us: swap(): return lax.ppermute(value, axis, pairs)]
    pallas_call x0 -> x12, Pallas kernels: none -> 48.5 us  [call(): pl.pallas_call(kernel, out_shape=outs, in_specs=[smem()] + [vmem()] * (le...]
    dot_general x3 -> x0, matrix products: 31.9 us -> none  [the longest x1 19.5 us: per_device(): jnp.dot(hidden, full_down, preferred_element_type=jnp.float32)]
    reshape x4 -> x0, local copies, waits for them, and re-layouts: 30.9 us -> none  [the longest x1 7.84 us: per_device(): rows = block.reshape(-1, width)]
    gather x1 -> x0, local copies, waits for them, and re-layouts: 11.8 us -> none  [per_device(): chosen = results[slot_index]]
    all_to_all x2 -> x0, starting transfers between devices: 11.6 us -> none  [the longest x1 7.59 us: per_device(): lax.all_to_all(outgoing, ('node', 'local'), split_axis=0, concat_axis=0,...]
  transfers between devices with their start and end apart: 5 -> 37, of which waited for: 2 -> 16; matrix products, arithmetic and copies ran while one was open for 4% -> 1% of each run, Pallas kernels for 0% -> 18%
where the time goes in v2:
time: 190 us; the launch traced here: 189 us
  waiting for transfers between devices  74.5 us (39%)
  starting transfers between devices  52.2 us (27%)
  Pallas kernels  48.5 us (26%)
  local copies, waits for them, and re-layouts  12 us (6%)
    ppermute x29, waiting for transfers between devices, swap(): return lax.ppermute(value, axis, pairs)  69.1 us
    pallas_call x12, Pallas kernels, call(): pl.pallas_call(kernel, out_shape=outs, in_specs=[smem()] + [vmem()] * (le...  48.5 us
    ppermute x29, starting transfers between devices, swap(): return lax.ppermute(value, axis, pairs)  35 us
    ppermute x8, starting transfers between devices, per_device(): hop = lambda value, pairs: lax.ppermute(value, 'local', chain_pairs(pairs))  17.2 us
    unnamed x32, local copies, waits for them, and re-layouts  12 us
    ppermute x8, waiting for transfers between devices, per_device(): hop = lambda value, pairs: lax.ppermute(value, 'local', chain_pairs(pairs))  5.46 us
  transfers between devices with their start and end apart: 37, of which 16 were waited for; matrix products, arithmetic and copies ran while one was open for 1% of the time, Pallas kernels for 18%

profile of v2, /device:TPU:0, one launch (start us, length us, event | category | flops | bytes accessed | tf_op | source)
XLA Modules:
  0.0 188.9 jit_solution(7980464147786562532)
XLA Ops:
  3.3 1.9 first.1
  5.2 2.6 %collective-permute-start = (bf16[64,4224]{1,0:T(8,128)(2,1)S(1)}, bf16[64,4224]{1,0:T(8,128)(2,1)}, u32[]{:S(2)}, u32[]{:S(2)}) collective-permute-start(bf16[64,4224]{1,0:T(8,128)(2,1)S(1)} %get-tuple-element.117.block), channel_id=1, source_target_pairs={{0,2},{1,3},{2,0},{3,1},{4,6},{5,7},{6,4},{7,5},{8,10},{9,11},{10,... | collective-permute-start | bytes 1622024 | tf_op jit(solution)/shard_map/ppermute | solution.py:17
  13.6 7.0 %collective-permute-done.3.refs_1_ = bf16[40,4096]{1,0:T(8,128)(2,1)S(1)} collective-permute-done((bf16[40,4096]{1,0:T(8,128)(2,1)S(1)}, bf16[40,4096]{1,0:T(8,128)(2,1)S(1)}, u32[]{:S(2)}, u32[]{:S(2)}) %collective-permute-start.3) | collective-permute-done | bytes 327712 | tf_op jit(solution)/shard_map/ppermute | solution.py:17
  21.3 6.9 %collective-permute-done.4.refs_2_ = bf16[40,4096]{1,0:T(8,128)(2,1)S(1)} collective-permute-done((bf16[40,4096]{1,0:T(8,128)(2,1)S(1)}, bf16[40,4096]{1,0:T(8,128)(2,1)S(1)}, u32[]{:S(2)}, u32[]{:S(2)}) %collective-permute-start.4) | collective-permute-done | bytes 327712 | tf_op jit(solution)/shard_map/ppermute | solution.py:17
  32.5 2.8 %select.7 = (bf16[40,4096]{1,0:T(8,128)(2,1)S(1)}, bf16[40,4096]{1,0:T(8,128)(2,1)}, bf16[40,4096]{1,0:T(8,128)(2,1)}, bf16[40,4096]{1,0:T(8,128)(2,1)}) custom-call(s32[2]{0:T(128)S(1)} %pad_add_fusion.place, bf16[64,4224]{1,0:T(8,128)(2,1)} %collective-permute-done.block), custom_call_target="tpu_custom_call" | custom-call | bytes 1851392 | tf_op jit(solution)/shard_map/select/pallas_call | solution.py:82
  39.5 7.5 %collective-permute-done.8.refs_1_ = bf16[40,4096]{1,0:T(8,128)(2,1)} collective-permute-done((bf16[40,4096]{1,0:T(8,128)(2,1)}, bf16[40,4096]{1,0:T(8,128)(2,1)}, u32[]{:S(2)}, u32[]{:S(2)}) %collective-permute-start.8) | collective-permute-done | bytes 327712 | tf_op jit(solution)/shard_map/ppermute | solution.py:17
  47.0 4.3 %collective-permute-done.9.refs_2_ = bf16[40,4096]{1,0:T(8,128)(2,1)} collective-permute-done((bf16[40,4096]{1,0:T(8,128)(2,1)}, bf16[40,4096]{1,0:T(8,128)(2,1)}, u32[]{:S(2)}, u32[]{:S(2)}) %collective-permute-start.9) | collective-permute-done | bytes 327712 | tf_op jit(solution)/shard_map/ppermute | solution.py:17
  51.3 1.9 collective-permute-done.10.refs_3_
  57.9 1.7 collective-permute-start.14
  60.9 7.0 %collective-permute-done.13.refs_1_ = bf16[40,4096]{1,0:T(8,128)(2,1)S(1)} collective-permute-done((bf16[40,4096]{1,0:T(8,128)(2,1)S(1)}, bf16[40,4096]{1,0:T(8,128)(2,1)S(1)}, u32[]{:S(2)}, u32[]{:S(2)}) %collective-permute-start.13) | collective-permute-done | bytes 327712 | tf_op jit(solution)/shard_map/ppermute | solution.py:17
  67.9 6.9 %collective-permute-done.14.refs_2_ = bf16[40,4096]{1,0:T(8,128)(2,1)S(1)} collective-permute-done((bf16[40,4096]{1,0:T(8,128)(2,1)S(1)}, bf16[40,4096]{1,0:T(8,128)(2,1)S(1)}, u32[]{:S(2)}, u32[]{:S(2)}) %collective-permute-start.14) | collective-permute-done | bytes 327712 | tf_op jit(solution)/shard_map/ppermute | solution.py:17
  82.5 1.9 copy-done.1
  84.4 1.9 copy-done.2
  86.3 7.6 %expert.4 = (bf16[40,4096]{1,0:T(8,128)(2,1)S(1)}, bf16[40,4096]{1,0:T(8,128)(2,1)S(1)}, bf16[40,4096]{1,0:T(8,128)(2,1)S(1)}, bf16[40,4096]{1,0:T(8,128)(2,1)S(1)}) custom-call(s32[2]{0:T(128)S(1)} %pad_add_fusion.place, bf16[40,4096]{1,0:T(8,128)(2,1)S(1)} %get-tuple-element.83.refs_0_, bf16[40,4096]{1,0:T(8,128)(2,1)S(1)} %collective-permute-done.13.refs_1_, ...), custom_call_target="tpu_custom_call" | custom-call | flops 3019898880 | bytes 21495808 | tf_op jit(solution)/shard_map/expert/pallas_call | solution.py:82
  94.8 7.6 %expert.5 = (bf16[40,4096]{1,0:T(8,128)(2,1)S(1)}, bf16[40,4096]{1,0:T(8,128)(2,1)S(1)}, bf16[40,4096]{1,0:T(8,128)(2,1)S(1)}, bf16[40,4096]{1,0:T(8,128)(2,1)S(1)}) custom-call(s32[2]{0:T(128)S(1)} %pad_add_fusion.place, bf16[40,4096]{1,0:T(8,128)(2,1)S(1)} %get-tuple-element.90.refs_0_, bf16[40,4096]{1,0:T(8,128)(2,1)S(1)} %collective-permute-done.17.refs_1_, ...), custom_call_target="tpu_custom_call" | custom-call | flops 3019898880 | bytes 21495808 | tf_op jit(solution)/shard_map/expert/pallas_call | solution.py:82
  103.0 1.7 collective-permute-start.21
  106.0 8.4 %expert.6 = (bf16[40,4096]{1,0:T(8,128)(2,1)S(1)}, bf16[40,4096]{1,0:T(8,128)(2,1)S(1)}, bf16[40,4096]{1,0:T(8,128)(2,1)S(1)}, bf16[40,4096]{1,0:T(8,128)(2,1)S(1)}) custom-call(s32[2]{0:T(128)S(1)} %pad_add_fusion.place, bf16[40,4096]{1,0:T(8,128)(2,1)S(1)} %copy-done.13, bf16[40,4096]{1,0:T(8,128)(2,1)} %collective-permute-done.8.refs_1_, ...), custom_call_target="tpu_custom_call" | custom-call | flops 3019898880 | bytes 21495808 | tf_op jit(solution)/shard_map/expert/pallas_call | solution.py:82
  114.4 7.6 %expert.7 = (bf16[40,4096]{1,0:T(8,128)(2,1)S(1)}, bf16[40,4096]{1,0:T(8,128)(2,1)S(1)}, bf16[40,4096]{1,0:T(8,128)(2,1)S(1)}, bf16[40,4096]{1,0:T(8,128)(2,1)S(1)}) custom-call(s32[2]{0:T(128)S(1)} %pad_add_fusion.place, bf16[40,4096]{1,0:T(8,128)(2,1)S(1)} %get-tuple-element.100.refs_0_, bf16[40,4096]{1,0:T(8,128)(2,1)S(1)} %copy-done.7, ...), custom_call_target="tpu_custom_call" | custom-call | flops 3019898880 | bytes 21495808 | tf_op jit(solution)/shard_map/expert/pallas_call | solution.py:82
  122.0 2.1 %combine.4 = bf16[64,4096]{1,0:T(8,128)(2,1)S(1)} custom-call(s32[2]{0:T(128)S(1)} %pad_add_fusion.place, bf16[64,4224]{1,0:T(8,128)(2,1)S(1)} %broadcast_select_fusion.block, bf16[40,4096]{1,0:T(8,128)(2,1)S(1)} %get-tuple-element.94.refs_0_, bf16[40,4096]{1,0:T(8,128)(2,1)S(1)} %collective-permute-done.20.refs_1_, ...), custom_call_target="tpu_custom_call" | custom-call | bytes 2375680 | tf_op jit(solution)/shard_map/combine/pallas_call | solution.py:82
  124.1 8.3 %collective-permute-start.26 = (bf16[64,4096]{1,0:T(8,128)(2,1)S(1)}, bf16[64,4096]{1,0:T(8,128)(2,1)S(1)}, u32[]{:S(2)}, u32[]{:S(2)}) collective-permute-start(bf16[64,4096]{1,0:T(8,128)(2,1)S(1)} %combine.4), channel_id=1, source_target_pairs={{0,2},{1,3},{6,4},{7,5},{8,10},{9,11},{14,12},{15,13},{16,18},{17,... | collective-permute-start | bytes 1572872 | tf_op jit(solution)/shard_map/ppermute | solution.py:203
  133.1 1.7 collective-permute-start.24
  136.0 7.2 %collective-permute-done.23.refs_1_ = bf16[40,4096]{1,0:T(8,128)(2,1)S(1)} collective-permute-done((bf16[40,4096]{1,0:T(8,128)(2,1)S(1)}, bf16[40,4096]{1,0:T(8,128)(2,1)S(1)}, u32[]{:S(2)}, u32[]{:S(2)}) %collective-permute-start.23) | collective-permute-done | bytes 327712 | tf_op jit(solution)/shard_map/ppermute | solution.py:17
  143.3 5.0 %collective-permute-done.25.refs_3_ = bf16[40,4096]{1,0:T(8,128)(2,1)S(1)} collective-permute-done((bf16[40,4096]{1,0:T(8,128)(2,1)S(1)}, bf16[40,4096]{1,0:T(8,128)(2,1)S(1)}, u32[]{:S(2)}, u32[]{:S(2)}) %collective-permute-start.25) | collective-permute-done | bytes 327712 | tf_op jit(solution)/shard_map/ppermute | solution.py:17
  148.4 2.1 %combine.5 = bf16[64,4096]{1,0:T(8,128)(2,1)S(1)} custom-call(s32[2]{0:T(128)S(1)} %pad_add_fusion.place, bf16[64,4224]{1,0:T(8,128)(2,1)S(1)} %broadcast_select_fusion.1.block, bf16[40,4096]{1,0:T(8,128)(2,1)S(1)} %get-tuple-element.89.refs_0_, bf16[40,4096]{1,0:T(8,128)(2,1)S(1)} %collective-permute-done.23.refs_1_, ...), custom_call_target="tpu_custom_call" | custom-call | bytes 2899968 | tf_op jit(solution)/shard_map/combine/pallas_call | solution.py:82
  156.3 5.4 %collective-permute-done.34 = bf16[64,4096]{1,0:T(8,128)(2,1)S(1)} collective-permute-done((bf16[64,4096]{1,0:T(8,128)(2,1)S(1)}, bf16[64,4096]{1,0:T(8,128)(2,1)S(1)}, u32[]{:S(2)}, u32[]{:S(2)}) %collective-permute-start.34) | collective-permute-done | bytes 524320 | tf_op jit(solution)/shard_map/ppermute | solution.py:203
  162.9 4.2 %collective-permute-done.28.refs_2_ = bf16[40,4096]{1,0:T(8,128)(2,1)S(1)} collective-permute-done((bf16[40,4096]{1,0:T(8,128)(2,1)S(1)}, bf16[40,4096]{1,0:T(8,128)(2,1)S(1)}, u32[]{:S(2)}, u32[]{:S(2)}) %collective-permute-start.28) | collective-permute-done | bytes 327712 | tf_op jit(solution)/shard_map/ppermute | solution.py:17
  167.1 2.6 %combine.6 = bf16[64,4096]{1,0:T(8,128)(2,1)S(1)} custom-call(s32[2]{0:T(128)S(1)} %pad_add_fusion.place, bf16[64,4224]{1,0:T(8,128)(2,1)} %collective-permute-done.block, bf16[40,4096]{1,0:T(8,128)(2,1)S(1)} %get-tuple-element.99.refs_0_, bf16[40,4096]{1,0:T(8,128)(2,1)S(1)} %collective-permute-done.27.refs_1_, ...), custom_call_target="tpu_custom_call" | custom-call | bytes 2899968 | tf_op jit(solution)/shard_map/combine/pallas_call | solution.py:82
  169.7 3.1 %collective-permute-start.36 = (bf16[64,4096]{1,0:T(8,128)(2,1)S(1)}, bf16[64,4096]{1,0:T(8,128)(2,1)S(1)}, u32[]{:S(2)}, u32[]{:S(2)}) collective-permute-start(bf16[64,4096]{1,0:T(8,128)(2,1)S(1)} %combine.6), channel_id=1, source_target_pairs={{0,2},{1,3},{2,0},{3,1},{4,6},{5,7},{6,4},{7,5},{8,10},{9,11},{10,... | collective-permute-start | bytes 1572872 | tf_op jit(solution)/shard_map/ppermute | solution.py:17
  172.8 2.5 %collective-permute-start.31 = (bf16[40,4096]{1,0:T(8,128)(2,1)S(1)}, bf16[40,4096]{1,0:T(8,128)(2,1)S(1)}, u32[]{:S(2)}, u32[]{:S(2)}) collective-permute-start(bf16[40,4096]{1,0:T(8,128)(2,1)S(1)} %get-tuple-element.118), channel_id=1, source_target_pairs={{0,8},{8,0},{16,24},{24,16},{1,9},{9,1},{17,25},{25,17},{2,10},{10... | collective-permute-start | bytes 983048 | tf_op jit(solution)/shard_map/ppermute | solution.py:17
  176.9 3.6 %collective-permute-done.31.refs_1_ = bf16[40,4096]{1,0:T(8,128)(2,1)S(1)} collective-permute-done((bf16[40,4096]{1,0:T(8,128)(2,1)S(1)}, bf16[40,4096]{1,0:T(8,128)(2,1)S(1)}, u32[]{:S(2)}, u32[]{:S(2)}) %collective-permute-start.31) | collective-permute-done | bytes 327712 | tf_op jit(solution)/shard_map/ppermute | solution.py:17
  180.5 5.5 %collective-permute-done.32.refs_2_ = bf16[40,4096]{1,0:T(8,128)(2,1)S(1)} collective-permute-done((bf16[40,4096]{1,0:T(8,128)(2,1)S(1)}, bf16[40,4096]{1,0:T(8,128)(2,1)S(1)}, u32[]{:S(2)}, u32[]{:S(2)}) %collective-permute-start.32) | collective-permute-done | bytes 327712 | tf_op jit(solution)/shard_map/ppermute | solution.py:17
  186.0 3.0 %combine.7 = bf16[64,4096]{1,0:T(8,128)(2,1)} custom-call(s32[2]{0:T(128)S(1)} %pad_add_fusion.place, bf16[64,4224]{1,0:T(8,128)(2,1)S(1)} %copy-done.4, bf16[40,4096]{1,0:T(8,128)(2,1)S(1)} %get-tuple-element.104.refs_0_, bf16[40,4096]{1,0:T(8,128)(2,1)S(1)} %collective-permute-done.31.refs_1_, bf16[40,4096]{1,0:T(8,128)(2,1)S(1)} %collective-permute-done.32.refs_2_, ...), custom_call_target="tpu_custom_call" | custom-call | bytes 3424256 | tf_op jit(solution)/shard_map/combine/pallas_call | solution.py:82
  (90 shorter events, 45.1 us)
Async XLA Ops:
  5.2 24.5 %collective-permute-start = (bf16[64,4224]{1,0:T(8,128)(2,1)S(1)}, bf16[64,4224]{1,0:T(8,128)(2,1)}, u32[]{:S(2)}, u32[]{:S(2)}) collective-permute-start(bf16[64,4224]{1,0:T(8,128)(2,1)S(1)} %get-tuple-element.117.block), channel_id=1, source_target_pairs={{0,2},{1,3},{2,0},{3,1},{4,6},{5,7},{6,4},{7,5},{8,10},{9,11},{10,... | collective-permute-start | bytes 1622024 | tf_op jit(solution)/shard_map/ppermute | solution.py:17
  7.8 21.9 %collective-permute-start.2 = (bf16[64,4224]{1,0:T(8,128)(2,1)S(1)}, bf16[64,4224]{1,0:T(8,128)(2,1)}, u32[]{:S(2)}, u32[]{:S(2)}) collective-permute-start(bf16[64,4224]{1,0:T(8,128)(2,1)S(1)} %get-tuple-element.117.block), channel_id=1, source_target_pairs={{2,4},{3,5},{4,2},{5,3},{10,12},{11,13},{12,10},{13,11},{18,20},{1... | collective-permute-start | bytes 1622024 | tf_op jit(solution)/shard_map/ppermute | solution.py:203
  11.6 16.7 %collective-permute-start.4 = (bf16[40,4096]{1,0:T(8,128)(2,1)S(1)}, bf16[40,4096]{1,0:T(8,128)(2,1)S(1)}, u32[]{:S(2)}, u32[]{:S(2)}) collective-permute-start(bf16[40,4096]{1,0:T(8,128)(2,1)S(1)} %get-tuple-element.66), channel_id=1, source_target_pairs={{0,16},{8,24},{16,0},{24,8},{1,17},{9,25},{17,1},{25,9},{2,18},{10... | collective-permute-start | bytes 983048 | tf_op jit(solution)/shard_map/ppermute | solution.py:17
  13.1 15.9 %collective-permute-start.5 = (bf16[40,4096]{1,0:T(8,128)(2,1)S(1)}, bf16[40,4096]{1,0:T(8,128)(2,1)S(1)}, u32[]{:S(2)}, u32[]{:S(2)}) collective-permute-start(bf16[40,4096]{1,0:T(8,128)(2,1)S(1)} %get-tuple-element.67), channel_id=1, source_target_pairs={{0,24},{8,16},{16,8},{24,0},{1,25},{9,17},{17,9},{25,1},{2,26},{10... | collective-permute-start | bytes 983048 | tf_op jit(solution)/shard_map/ppermute | solution.py:17
  29.8 23.4 %collective-permute-start.7 = (bf16[64,4224]{1,0:T(8,128)(2,1)}, bf16[64,4224]{1,0:T(8,128)(2,1)}, u32[]{:S(2)}, u32[]{:S(2)}) collective-permute-start(bf16[64,4224]{1,0:T(8,128)(2,1)} %collective-permute-done.2), channel_id=1, source_target_pairs={{2,0},{3,1},{4,6},{5,7},{10,8},{11,9},{12,14},{13,15},{18,16},{19,... | collective-permute-start | bytes 1622024 | tf_op jit(solution)/shard_map/ppermute | solution.py:203
  31.0 22.1 %collective-permute-start.6 = (bf16[64,4224]{1,0:T(8,128)(2,1)}, bf16[64,4224]{1,0:T(8,128)(2,1)}, u32[]{:S(2)}, u32[]{:S(2)}) collective-permute-start(bf16[64,4224]{1,0:T(8,128)(2,1)} %collective-permute-done.block), channel_id=1, source_target_pairs={{2,4},{3,5},{4,2},{5,3},{10,12},{11,13},{12,10},{13,11},{18,20},{1... | collective-permute-start | bytes 1622024 | tf_op jit(solution)/shard_map/ppermute | solution.py:203
  36.0 11.0 %collective-permute-start.8 = (bf16[40,4096]{1,0:T(8,128)(2,1)}, bf16[40,4096]{1,0:T(8,128)(2,1)}, u32[]{:S(2)}, u32[]{:S(2)}) collective-permute-start(bf16[40,4096]{1,0:T(8,128)(2,1)} %get-tuple-element.70), channel_id=1, source_target_pairs={{0,8},{8,0},{16,24},{24,16},{1,9},{9,1},{17,25},{25,17},{2,10},{10... | collective-permute-start | bytes 983048 | tf_op jit(solution)/shard_map/ppermute | solution.py:17
  36.5 14.8 %collective-permute-start.9 = (bf16[40,4096]{1,0:T(8,128)(2,1)}, bf16[40,4096]{1,0:T(8,128)(2,1)}, u32[]{:S(2)}, u32[]{:S(2)}) collective-permute-start(bf16[40,4096]{1,0:T(8,128)(2,1)} %get-tuple-element.71), channel_id=1, source_target_pairs={{0,16},{8,24},{16,0},{24,8},{1,17},{9,25},{17,1},{25,9},{2,18},{10... | collective-permute-start | bytes 983048 | tf_op jit(solution)/shard_map/ppermute | solution.py:17
  38.1 15.1 %collective-permute-start.10 = (bf16[40,4096]{1,0:T(8,128)(2,1)}, bf16[40,4096]{1,0:T(8,128)(2,1)}, u32[]{:S(2)}, u32[]{:S(2)}) collective-permute-start(bf16[40,4096]{1,0:T(8,128)(2,1)} %get-tuple-element.72), channel_id=1, source_target_pairs={{0,24},{8,16},{16,8},{24,0},{1,25},{9,17},{17,9},{25,1},{2,26},{10... | collective-permute-start | bytes 983048 | tf_op jit(solution)/shard_map/ppermute | solution.py:17
  54.3 20.5 %collective-permute-start.12 = (bf16[4096,384]{1,0:T(8,128)(2,1)}, bf16[4096,384]{1,0:T(8,128)(2,1)S(1)}, u32[]{:S(2)}, u32[]{:S(2)}) collective-permute-start(bf16[4096,384]{1,0:T(8,128)(2,1)} %refs_5_.7), channel_id=1, source_target_pairs={{0,1},{1,0},{2,3},{3,2},{4,5},{5,4},{6,7},{7,6},{8,9},{9,8},{10,11... | collective-permute-start | bytes 9437192 | tf_op jit(solution)/shard_map/ppermute | solution.py:17
  54.3 20.5 %collective-permute-start.11 = (bf16[64,4224]{1,0:T(8,128)(2,1)S(1)}, bf16[64,4224]{1,0:T(8,128)(2,1)S(1)}, u32[]{:S(2)}, u32[]{:S(2)}) collective-permute-start(bf16[64,4224]{1,0:T(8,128)(2,1)S(1)} %broadcast_select_fusion.1.block), channel_id=1, source_target_pairs={{2,0},{3,1},{4,6},{5,7},{10,8},{11,9},{12,14},{13,15},{18,16},{19,... | collective-permute-start | bytes 1622024 | tf_op jit(solution)/shard_map/ppermute | solution.py:203
  57.3 10.6 %collective-permute-start.13 = (bf16[40,4096]{1,0:T(8,128)(2,1)S(1)}, bf16[40,4096]{1,0:T(8,128)(2,1)S(1)}, u32[]{:S(2)}, u32[]{:S(2)}) collective-permute-start(bf16[40,4096]{1,0:T(8,128)(2,1)S(1)} %get-tuple-element.76), channel_id=1, source_target_pairs={{0,8},{8,0},{16,24},{24,16},{1,9},{9,1},{17,25},{25,17},{2,10},{10... | collective-permute-start | bytes 983048 | tf_op jit(solution)/shard_map/ppermute | solution.py:17
  57.9 16.9 %collective-permute-start.14 = (bf16[40,4096]{1,0:T(8,128)(2,1)S(1)}, bf16[40,4096]{1,0:T(8,128)(2,1)S(1)}, u32[]{:S(2)}, u32[]{:S(2)}) collective-permute-start(bf16[40,4096]{1,0:T(8,128)(2,1)S(1)} %get-tuple-element.77), channel_id=1, source_target_pairs={{0,16},{8,24},{16,0},{24,8},{1,17},{9,25},{17,1},{25,9},{2,18},{10... | collective-permute-start | bytes 983048 | tf_op jit(solution)/shard_map/ppermute | solution.py:17
  59.7 15.1 %collective-permute-start.15 = (bf16[40,4096]{1,0:T(8,128)(2,1)S(1)}, bf16[40,4096]{1,0:T(8,128)(2,1)S(1)}, u32[]{:S(2)}, u32[]{:S(2)}) collective-permute-start(bf16[40,4096]{1,0:T(8,128)(2,1)S(1)} %get-tuple-element.78), channel_id=1, source_target_pairs={{0,24},{8,16},{16,8},{24,0},{1,25},{9,17},{17,9},{25,1},{2,26},{10... | collective-permute-start | bytes 983048 | tf_op jit(solution)/shard_map/ppermute | solution.py:17
  76.4 17.4 %collective-permute-start.17 = (bf16[40,4096]{1,0:T(8,128)(2,1)S(1)}, bf16[40,4096]{1,0:T(8,128)(2,1)S(1)}, u32[]{:S(2)}, u32[]{:S(2)}) collective-permute-start(bf16[40,4096]{1,0:T(8,128)(2,1)S(1)} %get-tuple-element.91), channel_id=1, source_target_pairs={{0,8},{8,0},{16,24},{24,16},{1,9},{9,1},{17,25},{25,17},{2,10},{10... | collective-permute-start | bytes 983048 | tf_op jit(solution)/shard_map/ppermute | solution.py:17
  78.0 15.9 %collective-permute-start.18 = (bf16[40,4096]{1,0:T(8,128)(2,1)S(1)}, bf16[40,4096]{1,0:T(8,128)(2,1)S(1)}, u32[]{:S(2)}, u32[]{:S(2)}) collective-permute-start(bf16[40,4096]{1,0:T(8,128)(2,1)S(1)} %get-tuple-element.92), channel_id=1, source_target_pairs={{0,16},{8,24},{16,0},{24,8},{1,17},{9,25},{17,1},{25,9},{2,18},{10... | collective-permute-start | bytes 983048 | tf_op jit(solution)/shard_map/ppermute | solution.py:17
  78.6 16.2 %collective-permute-start.19 = (bf16[40,4096]{1,0:T(8,128)(2,1)S(1)}, bf16[40,4096]{1,0:T(8,128)(2,1)S(1)}, u32[]{:S(2)}, u32[]{:S(2)}) collective-permute-start(bf16[40,4096]{1,0:T(8,128)(2,1)S(1)} %get-tuple-element.93), channel_id=1, source_target_pairs={{0,24},{8,16},{16,8},{24,0},{1,25},{9,17},{17,9},{25,1},{2,26},{10... | collective-permute-start | bytes 983048 | tf_op jit(solution)/shard_map/ppermute | solution.py:17
  102.4 19.6 %collective-permute-start.20 = (bf16[40,4096]{1,0:T(8,128)(2,1)S(1)}, bf16[40,4096]{1,0:T(8,128)(2,1)S(1)}, u32[]{:S(2)}, u32[]{:S(2)}) collective-permute-start(bf16[40,4096]{1,0:T(8,128)(2,1)S(1)} %get-tuple-element.106), channel_id=1, source_target_pairs={{0,8},{8,0},{16,24},{24,16},{1,9},{9,1},{17,25},{25,17},{2,10},{10... | collective-permute-start | bytes 983048 | tf_op jit(solution)/shard_map/ppermute | solution.py:17
  103.0 19.0 %collective-permute-start.21 = (bf16[40,4096]{1,0:T(8,128)(2,1)S(1)}, bf16[40,4096]{1,0:T(8,128)(2,1)S(1)}, u32[]{:S(2)}, u32[]{:S(2)}) collective-permute-start(bf16[40,4096]{1,0:T(8,128)(2,1)S(1)} %get-tuple-element.107), channel_id=1, source_target_pairs={{0,16},{8,24},{16,0},{24,8},{1,17},{9,25},{17,1},{25,9},{2,18},{10... | collective-permute-start | bytes 983048 | tf_op jit(solution)/shard_map/ppermute | solution.py:17
  104.8 17.2 %collective-permute-start.22 = (bf16[40,4096]{1,0:T(8,128)(2,1)S(1)}, bf16[40,4096]{1,0:T(8,128)(2,1)S(1)}, u32[]{:S(2)}, u32[]{:S(2)}) collective-permute-start(bf16[40,4096]{1,0:T(8,128)(2,1)S(1)} %get-tuple-element.108), channel_id=1, source_target_pairs={{0,24},{8,16},{16,8},{24,0},{1,25},{9,17},{17,9},{25,1},{2,26},{10... | collective-permute-start | bytes 983048 | tf_op jit(solution)/shard_map/ppermute | solution.py:17
  124.1 24.2 %collective-permute-start.26 = (bf16[64,4096]{1,0:T(8,128)(2,1)S(1)}, bf16[64,4096]{1,0:T(8,128)(2,1)S(1)}, u32[]{:S(2)}, u32[]{:S(2)}) collective-permute-start(bf16[64,4096]{1,0:T(8,128)(2,1)S(1)} %combine.4), channel_id=1, source_target_pairs={{0,2},{1,3},{6,4},{7,5},{8,10},{9,11},{14,12},{15,13},{16,18},{17,... | collective-permute-start | bytes 1572872 | tf_op jit(solution)/shard_map/ppermute | solution.py:203
  132.4 10.7 %collective-permute-start.23 = (bf16[40,4096]{1,0:T(8,128)(2,1)S(1)}, bf16[40,4096]{1,0:T(8,128)(2,1)S(1)}, u32[]{:S(2)}, u32[]{:S(2)}) collective-permute-start(bf16[40,4096]{1,0:T(8,128)(2,1)S(1)} %get-tuple-element.110), channel_id=1, source_target_pairs={{0,8},{8,0},{16,24},{24,16},{1,9},{9,1},{17,25},{25,17},{2,10},{10... | collective-permute-start | bytes 983048 | tf_op jit(solution)/shard_map/ppermute | solution.py:17
  134.8 13.6 %collective-permute-start.25 = (bf16[40,4096]{1,0:T(8,128)(2,1)S(1)}, bf16[40,4096]{1,0:T(8,128)(2,1)S(1)}, u32[]{:S(2)}, u32[]{:S(2)}) collective-permute-start(bf16[40,4096]{1,0:T(8,128)(2,1)S(1)} %get-tuple-element.112), channel_id=1, source_target_pairs={{0,24},{8,16},{16,8},{24,0},{1,25},{9,17},{17,9},{25,1},{2,26},{10... | collective-permute-start | bytes 983048 | tf_op jit(solution)/shard_map/ppermute | solution.py:17
  150.5 11.3 %collective-permute-start.34 = (bf16[64,4096]{1,0:T(8,128)(2,1)S(1)}, bf16[64,4096]{1,0:T(8,128)(2,1)S(1)}, u32[]{:S(2)}, u32[]{:S(2)}) collective-permute-start(bf16[64,4096]{1,0:T(8,128)(2,1)S(1)} %combine.5), channel_id=1, source_target_pairs={{0,2},{1,3},{6,4},{7,5},{8,10},{9,11},{14,12},{15,13},{16,18},{17,... | collective-permute-start | bytes 1572872 | tf_op jit(solution)/shard_map/ppermute | solution.py:203
  152.1 10.8 %collective-permute-start.27 = (bf16[40,4096]{1,0:T(8,128)(2,1)S(1)}, bf16[40,4096]{1,0:T(8,128)(2,1)S(1)}, u32[]{:S(2)}, u32[]{:S(2)}) collective-permute-start(bf16[40,4096]{1,0:T(8,128)(2,1)S(1)} %get-tuple-element.114), channel_id=1, source_target_pairs={{0,8},{8,0},{16,24},{24,16},{1,9},{9,1},{17,25},{25,17},{2,10},{10... | collective-permute-start | bytes 983048 | tf_op jit(solution)/shard_map/ppermute | solution.py:17
  153.3 13.8 %collective-permute-start.28 = (bf16[40,4096]{1,0:T(8,128)(2,1)S(1)}, bf16[40,4096]{1,0:T(8,128)(2,1)S(1)}, u32[]{:S(2)}, u32[]{:S(2)}) collective-permute-start(bf16[40,4096]{1,0:T(8,128)(2,1)S(1)} %get-tuple-element.115), channel_id=1, source_target_pairs={{0,16},{8,24},{16,0},{24,8},{1,17},{9,25},{17,1},{25,9},{2,18},{10... | collective-permute-start | bytes 983048 | tf_op jit(solution)/shard_map/ppermute | solution.py:17
  154.5 12.6 %collective-permute-start.29 = (bf16[40,4096]{1,0:T(8,128)(2,1)S(1)}, bf16[40,4096]{1,0:T(8,128)(2,1)S(1)}, u32[]{:S(2)}, u32[]{:S(2)}) collective-permute-start(bf16[40,4096]{1,0:T(8,128)(2,1)S(1)} %get-tuple-element.116), channel_id=1, source_target_pairs={{0,24},{8,16},{16,8},{24,0},{1,25},{9,17},{17,9},{25,1},{2,26},{10... | collective-permute-start | bytes 983048 | tf_op jit(solution)/shard_map/ppermute | solution.py:17
  155.7 11.4 %collective-permute-start.30 = (bf16[64,4096]{1,0:T(8,128)(2,1)S(1)}, bf16[64,4096]{1,0:T(8,128)(2,1)S(1)}, u32[]{:S(2)}, u32[]{:S(2)}) collective-permute-start(bf16[64,4096]{1,0:T(8,128)(2,1)S(1)} %combine.5), channel_id=1, source_target_pairs={{2,4},{3,5},{4,2},{5,3},{10,12},{11,13},{12,10},{13,11},{18,20},{1... | collective-permute-start | bytes 1572872 | tf_op jit(solution)/shard_map/ppermute | solution.py:203
  161.9 24.1 %collective-permute-start.35 = (bf16[64,4096]{1,0:T(8,128)(2,1)S(1)}, bf16[64,4096]{1,0:T(8,128)(2,1)S(1)}, u32[]{:S(2)}, u32[]{:S(2)}) collective-permute-start(bf16[64,4096]{1,0:T(8,128)(2,1)S(1)} %add_convert_fusion), channel_id=1, source_target_pairs={{2,4},{3,5},{4,2},{5,3},{10,12},{11,13},{12,10},{13,11},{18,20},{1... | collective-permute-start | bytes 1572872 | tf_op jit(solution)/shard_map/ppermute | solution.py:203
  169.7 16.2 %collective-permute-start.36 = (bf16[64,4096]{1,0:T(8,128)(2,1)S(1)}, bf16[64,4096]{1,0:T(8,128)(2,1)S(1)}, u32[]{:S(2)}, u32[]{:S(2)}) collective-permute-start(bf16[64,4096]{1,0:T(8,128)(2,1)S(1)} %combine.6), channel_id=1, source_target_pairs={{0,2},{1,3},{2,0},{3,1},{4,6},{5,7},{6,4},{7,5},{8,10},{9,11},{10,... | collective-permute-start | bytes 1572872 | tf_op jit(solution)/shard_map/ppermute | solution.py:17
  175.4 10.6 %collective-permute-start.32 = (bf16[40,4096]{1,0:T(8,128)(2,1)S(1)}, bf16[40,4096]{1,0:T(8,128)(2,1)S(1)}, u32[]{:S(2)}, u32[]{:S(2)}) collective-permute-start(bf16[40,4096]{1,0:T(8,128)(2,1)S(1)} %get-tuple-element.119), channel_id=1, source_target_pairs={{0,16},{8,24},{16,0},{24,8},{1,17},{9,25},{17,1},{25,9},{2,18},{10... | collective-permute-start | bytes 983048 | tf_op jit(solution)/shard_map/ppermute | solution.py:17
  175.4 10.6 %collective-permute-start.33 = (bf16[40,4096]{1,0:T(8,128)(2,1)S(1)}, bf16[40,4096]{1,0:T(8,128)(2,1)S(1)}, u32[]{:S(2)}, u32[]{:S(2)}) collective-permute-start(bf16[40,4096]{1,0:T(8,128)(2,1)S(1)} %get-tuple-element.120), channel_id=1, source_target_pairs={{0,24},{8,16},{16,8},{24,0},{1,25},{9,17},{17,9},{25,1},{2,26},{10... | collective-permute-start | bytes 983048 | tf_op jit(solution)/shard_map/ppermute | solution.py:17
  (20 other events, 227.1 us)

commit v3 on v2

--- a/solution.py
+++ b/solution.py
@@ -9,7 +9,7 @@
 
 LANES = 128
 ORDER = [(2,), (3,), (1,), (0,)]
-VMEM_BYTES = 34 * 2**20
+VMEM_BYTES, EXPERT_BYTES = 8 * 2**20, 44 * 2**20
 
 
 def swap(value, axis, mask):
@@ -29,19 +29,17 @@
 
 
 def meta_of(ids, gates):
-    rows, top = ids.shape
     parts = [ids[...].astype(jnp.float32)]
     rest = gates[...]
     for _ in range(3):
         piece = rest.astype(jnp.bfloat16).astype(jnp.float32)
         parts.append(piece)
         rest = rest - piece
-    lane = lax.broadcasted_iota(jnp.int32, (rows, LANES), 1)
-    meta = jnp.zeros((rows, LANES), jnp.float32)
-    for i, part in enumerate(parts):
-        for k in range(top):
-            meta = jnp.where(lane == i * top + k, part[:, k : k + 1], meta)
-    return meta
+    parts = jnp.concatenate(parts, axis=0).astype(jnp.bfloat16)
+    count = parts.shape[0]
+    same = lax.broadcasted_iota(jnp.int32, (count, LANES), 0) == lax.broadcasted_iota(jnp.int32, (count, LANES), 1)
+    unit = jnp.where(same, 1.0, 0.0).astype(jnp.bfloat16)
+    return lax.dot_general(parts, unit, (((0,), (0,)), ((), ())), preferred_element_type=jnp.float32)
 
 
 def slots(place, meta, top, chain, capacity, count):
@@ -82,10 +80,10 @@
     return pl.pallas_call(
         kernel,
         out_shape=outs,
-        in_specs=[smem()] + [vmem()] * (len(inputs) - stay) + [pl.BlockSpec(memory_space=pl.ANY)] * stay,
+        in_specs=[smem()] + [vmem()] * (len(inputs) - stay) + [pl.BlockSpec(memory_space=pltpu.HBM)] * stay,
         out_specs=[vmem()] * len(outs),
         scratch_shapes=list(scratch),
-        compiler_params=pltpu.CompilerParams(vmem_limit_bytes=VMEM_BYTES),
+        compiler_params=pltpu.CompilerParams(vmem_limit_bytes=EXPERT_BYTES if stay else VMEM_BYTES),
         cost_estimate=pl.CostEstimate(flops=flops, bytes_accessed=moved, transcendentals=0),
         name=name,
     )(place, *inputs)
@@ -103,16 +101,31 @@
         out[...] = rows.astype(jnp.bfloat16)
 
 
-def first_kernel(top, chain, capacity, place, tokens, ids, gates, packed, *outs):
+def first_kernel(top, chain, capacity, place, tokens_from, ids_from, gates_from, packed, *refs):
+    outs, (tokens, ids, gates, sems) = refs[:-4], refs[-4:]
+    copies = [
+        pltpu.make_async_copy(source, target, sems.at[i])
+        for i, (source, target) in enumerate(((ids_from, ids), (gates_from, gates), (tokens_from, tokens)))
+    ]
+    for copy in copies:
+        copy.start()
+    copies[0].wait()
+    copies[1].wait()
     width = tokens.shape[1]
     meta = meta_of(ids, gates)
+    packed[:, width:] = meta.astype(jnp.bfloat16)
+    copies[2].wait()
+    packed[:, :width] = tokens[...]
     pick(top, chain, capacity, place, meta, tokens[...], outs)
-    packed[:, :width] = tokens[...]
-    packed[:, width:] = meta.astype(jnp.bfloat16)
-
-
-def select_kernel(top, chain, capacity, place, block, *outs):
+
+
+def select_kernel(top, chain, capacity, inputs, place, *refs):
+    block, outs = refs[0][...], refs[inputs:]
     width = outs[0].shape[1]
+    if inputs == 2:
+        block = jnp.where(place[2] == 1, block, refs[1][...])
+        kept, outs = outs[-1], outs[:-1]
+        kept[...] = block
     pick(top, chain, capacity, place, block[:, width:], block[:, :width], outs)
 
 
@@ -195,10 +208,10 @@
     capacity = rows * top * 5 // (4 * nodes * chain)
     capacity = -(-capacity // 8) * 8
     spot = lax.axis_index("local") // 2
-    place = jnp.stack([lax.axis_index("node"), spot]).astype(jnp.int32)
+    middle = (spot == 1) | (spot == 2)
+    place = jnp.stack([lax.axis_index("node"), spot, middle]).astype(jnp.int32)
     sizes = (top, chain, capacity)
     relay = chain == 4
-    middle = (spot == 1) | (spot == 2)
     inner, outward, inward = [(1, 2), (2, 1)], [(1, 0), (2, 3)], [(0, 1), (3, 2)]
     hop = lambda value, pairs: lax.ppermute(value, "local", chain_pairs(pairs))
     send = lambda values: [values[0]] + [swap(values[n], "node", n) for n in range(1, nodes)]
@@ -207,38 +220,42 @@
         functools.partial(first_kernel, *sizes),
         "first",
         place,
-        [tokens, expert_ids, gate_weights],
+        [tokens, expert_ids.T, gate_weights.T],
         [array(rows, width + LANES)] + [array(capacity, width)] * nodes,
+        [
+            pltpu.VMEM((rows, width), tokens.dtype),
+            pltpu.VMEM((top, rows), expert_ids.dtype),
+            pltpu.VMEM((top, rows), gate_weights.dtype),
+            pltpu.SemaphoreType.DMA((3,)),
+        ],
+        stay=3,
     )
     arrived = {0: send(picked)}
     own = (w_gate, w_up, w_down)
     other = [swap(w_gate, "local", 1)]
     blocks = [packed]
 
-    def pick_for(step, *token):
-        block = after(blocks[step], token)
+    def pick_for(step, *inputs):
+        outs = [array(capacity, width)] * nodes + [array(*packed.shape)] * (len(inputs) - 1)
         picked = call(
-            functools.partial(select_kernel, *sizes), "select", place, [block], [array(capacity, width)] * nodes
-        )
-        arrived[step] = send(picked)
+            functools.partial(select_kernel, *sizes, len(inputs)), "select", place, list(inputs), outs
+        )
+        arrived[step] = send(picked[:nodes])
+        blocks.append(picked[nodes] if len(inputs) > 1 else inputs[0])
 
     if relay:
         moved = [swap(packed, "local", 2), hop(after(packed, other), inner)]
         (first, third), arrived[0] = together(moved, arrived[0])
-        blocks.append(first)
-        pick_for(1)
+        pick_for(1, first)
         moved = [hop(first, inner), hop(third, outward)]
         moved, arrived[1] = together(moved, arrived[1])
-        blocks.append(jnp.where(middle, *moved))
-        pick_for(2)
+        pick_for(2, *moved)
         other.append(swap(after(w_up, blocks[2:]), "local", 1))
         (last_hop, other[1]), arrived[2] = together([hop(blocks[2], outward), other[1]], arrived[2])
-        blocks.append(jnp.where(middle, third, last_hop))
-        pick_for(3)
+        pick_for(3, third, last_hop)
     else:
         for step in range(1, chain):
-            blocks.append(swap(packed, "local", 2 * step))
-            pick_for(step)
+            pick_for(step, swap(packed, "local", 2 * step))
         other.append(swap(w_up, "local", 1))
     other.append(swap(after(w_down, [other[1], blocks[-1]]), "local", 1))
 
@@ -268,27 +285,21 @@
     results, last = {}, []
     for group in ORDER if relay else [(step,) for step in range(chain)]:
         run(group)
-    extra = {step: [] for step in range(chain)}
-    kept = None
+    sums, totals = [], []
     for step in reversed(range(chain)):
+        ready = [*totals[-2:-1], *sums[:-2]] if step < chain - 2 else []
+        result = results[step]
+        returned = send([result[0]] + [after(value, ready) for value in result[1:]])
         (total,) = call(
             functools.partial(combine_kernel, *sizes, nodes),
             "combine",
             place,
-            [after(blocks[step], last), *send(results[step]), *extra[step]],
+            [after(blocks[step], [*totals[-1:], *(results[0][:1] if step == chain - 2 else [])]), *returned, *([] if step else sums)],
             [array(rows, width)],
         )
-        last = [total]
-        if relay and step == 3:
-            kept = total
-            extra[2].append(hop(total, inward))
-        elif relay and step == 2:
-            ends = hop(total, inward).astype(jnp.float32)
-            kept = (kept.astype(jnp.float32) + ends).astype(jnp.bfloat16)
-            extra[0].append(hop(kept, inner))
-            extra[1].append(hop(total, inner))
-        elif step:
-            extra[0].append(swap(total, "local", 2 * step))
+        totals.append(total)
+        if step:
+            sums.append(swap(total, "local", 2 * step))
     return total
 
 

time: 190 us -> 172 us (0.905)
  local copies, waits for them, and re-layouts: 12 us -> 6.28 us
  starting transfers between devices: 52.2 us -> 47.4 us
  waiting for transfers between devices: 74.5 us -> 70.3 us
    ppermute x8 -> x4, starting transfers between devices: 17.2 us -> 4.14 us  [per_device(): hop = lambda value, pairs: lax.ppermute(value, 'local', chain_pairs(pairs))]
    ppermute x29 -> x31, starting transfers between devices: 35 us -> 43.3 us  [swap(): return lax.ppermute(value, axis, pairs)]
    unnamed x32 -> x14, local copies, waits for them, and re-layouts: 12 us -> 6.28 us
    ppermute x8 -> x4, waiting for transfers between devices: 5.46 us -> 0.96 us  [per_device(): hop = lambda value, pairs: lax.ppermute(value, 'local', chain_pairs(pairs))]
    ppermute x29 -> x31, waiting for transfers between devices: 69.1 us -> 69.3 us  [swap(): return lax.ppermute(value, axis, pairs)]
  transfers between devices with their start and end apart: 37 -> 35, of which waited for: 16 -> 13; matrix products, arithmetic and copies ran while one was open for 1% -> 0% of each run, Pallas kernels for 18% -> 20%
where the time goes in v3:
time: 172 us
  waiting for transfers between devices  70.3 us (41%)
  Pallas kernels  47.6 us (28%)
  starting transfers between devices  47.4 us (28%)
  local copies, waits for them, and re-layouts  6.28 us (4%)
    ppermute x31, waiting for transfers between devices, swap(): return lax.ppermute(value, axis, pairs)  69.3 us
    pallas_call x12, Pallas kernels, call(): pl.pallas_call(kernel, out_shape=outs, in_specs=[smem()] + [vmem()] * (le...  47.6 us
    ppermute x31, starting transfers between devices, swap(): return lax.ppermute(value, axis, pairs)  43.3 us
    unnamed x14, local copies, waits for them, and re-layouts  6.28 us
    ppermute x4, starting transfers between devices, per_device(): hop = lambda value, pairs: lax.ppermute(value, 'local', chain_pairs(pairs))  4.14 us
  transfers between devices with their start and end apart: 35, of which 13 were waited for; matrix products, arithmetic and copies ran while one was open for 0% of the time, Pallas kernels for 20%

profile of v3, /device:TPU:0, one launch (start us, length us, event | category | flops | bytes accessed | tf_op | source)
XLA Modules:
  0.0 171.9 jit_solution(1841862989421229973)
XLA Ops:
  3.2 1.8 %first.1 = (bf16[64,4224]{1,0:T(8,128)(2,1)S(1)}, bf16[40,4096]{1,0:T(8,128)(2,1)S(1)}, bf16[40,4096]{1,0:T(8,128)(2,1)S(1)}, bf16[40,4096]{1,0:T(8,128)(2,1)S(1)}, bf16[40,4096]{1,0:T(8,128)(2,1)S(1)}) custom-call(s32[3]{0:T(128)S(1)} %pad_add_fusion.place, bf16[64,4096]{1,0:T(8,128)(2,1)S(1)} %copy-done.2, s32[8,64]{1,0:T(8,128)S(1)} %bitcast.5, ...), custom_call_target="tpu_custom_call" | custom-call | bytes 2377728 | tf_op jit(solution)/shard_map/first/pallas_call | solution.py:80
  5.0 2.5 %collective-permute-start = (bf16[64,4224]{1,0:T(8,128)(2,1)S(1)}, bf16[64,4224]{1,0:T(8,128)(2,1)S(1)}, u32[]{:S(2)}, u32[]{:S(2)}) collective-permute-start(bf16[64,4224]{1,0:T(8,128)(2,1)S(1)} %get-tuple-element.128.block), channel_id=1, source_target_pairs={{0,2},{1,3},{2,0},{3,1},{4,6},{5,7},{6,4},{7,5},{8,10},{9,11},{10,... | collective-permute-start | bytes 1622024 | tf_op jit(solution)/shard_map/ppermute | solution.py:17
  8.2 1.5 collective-permute-start.3
  9.8 1.5 collective-permute-start.4
  11.8 7.0 %collective-permute-done.3.refs_1_ = bf16[40,4096]{1,0:T(8,128)(2,1)S(1)} collective-permute-done((bf16[40,4096]{1,0:T(8,128)(2,1)S(1)}, bf16[40,4096]{1,0:T(8,128)(2,1)S(1)}, u32[]{:S(2)}, u32[]{:S(2)}) %collective-permute-start.3) | collective-permute-done | bytes 327712 | tf_op jit(solution)/shard_map/ppermute | solution.py:17
  18.8 7.6 %collective-permute-done.4.refs_2_ = bf16[40,4096]{1,0:T(8,128)(2,1)S(1)} collective-permute-done((bf16[40,4096]{1,0:T(8,128)(2,1)S(1)}, bf16[40,4096]{1,0:T(8,128)(2,1)S(1)}, u32[]{:S(2)}, u32[]{:S(2)}) %collective-permute-start.4) | collective-permute-done | bytes 327712 | tf_op jit(solution)/shard_map/ppermute | solution.py:17
  33.4 7.2 %collective-permute-done.8.refs_1_ = bf16[40,4096]{1,0:T(8,128)(2,1)S(1)} collective-permute-done((bf16[40,4096]{1,0:T(8,128)(2,1)S(1)}, bf16[40,4096]{1,0:T(8,128)(2,1)S(1)}, u32[]{:S(2)}, u32[]{:S(2)}) %collective-permute-start.8) | collective-permute-done | bytes 327712 | tf_op jit(solution)/shard_map/ppermute | solution.py:17
  40.6 6.4 %collective-permute-done.9.refs_2_ = bf16[40,4096]{1,0:T(8,128)(2,1)S(1)} collective-permute-done((bf16[40,4096]{1,0:T(8,128)(2,1)S(1)}, bf16[40,4096]{1,0:T(8,128)(2,1)S(1)}, u32[]{:S(2)}, u32[]{:S(2)}) %collective-permute-start.9) | collective-permute-done | bytes 327712 | tf_op jit(solution)/shard_map/ppermute | solution.py:17
  53.6 7.0 %collective-permute-done.13.refs_1_ = bf16[40,4096]{1,0:T(8,128)(2,1)S(1)} collective-permute-done((bf16[40,4096]{1,0:T(8,128)(2,1)S(1)}, bf16[40,4096]{1,0:T(8,128)(2,1)S(1)}, u32[]{:S(2)}, u32[]{:S(2)}) %collective-permute-start.13) | collective-permute-done | bytes 327712 | tf_op jit(solution)/shard_map/ppermute | solution.py:17
  60.6 6.9 %collective-permute-done.14.refs_2_ = bf16[40,4096]{1,0:T(8,128)(2,1)S(1)} collective-permute-done((bf16[40,4096]{1,0:T(8,128)(2,1)S(1)}, bf16[40,4096]{1,0:T(8,128)(2,1)S(1)}, u32[]{:S(2)}, u32[]{:S(2)}) %collective-permute-start.14) | collective-permute-done | bytes 327712 | tf_op jit(solution)/shard_map/ppermute | solution.py:17
  72.1 1.5 collective-permute-start.19
  73.6 2.3 %collective-permute-done.16.refs_9_ = bf16[384,4096]{1,0:T(8,128)(2,1)S(1)} collective-permute-done((bf16[384,4096]{1,0:T(8,128)(2,1)}, bf16[384,4096]{1,0:T(8,128)(2,1)S(1)}, u32[]{:S(2)}, u32[]{:S(2)}) %collective-permute-start.16) | collective-permute-done | bytes 3145760 | tf_op jit(solution)/shard_map/ppermute | solution.py:17
  75.9 1.7 copy-done.6
  77.6 1.9 %copy-done.1 = bf16[4096,384]{1,0:T(8,128)(2,1)S(1)} copy-done((bf16[4096,384]{1,0:T(8,128)(2,1)S(1)}, bf16[4096,384]{1,0:T(8,128)(2,1)}, u32[]{:S(2)}) %copy-start.1) | copy-done | bytes 3145752
  79.5 7.9 %expert.4 = (bf16[40,4096]{1,0:T(8,128)(2,1)S(1)}, bf16[40,4096]{1,0:T(8,128)(2,1)S(1)}, bf16[40,4096]{1,0:T(8,128)(2,1)S(1)}, bf16[40,4096]{1,0:T(8,128)(2,1)S(1)}) custom-call(s32[3]{0:T(128)S(1)} %pad_add_fusion.place, bf16[40,4096]{1,0:T(8,128)(2,1)S(1)} %get-tuple-element.90.refs_0_, bf16[40,4096]{1,0:T(8,128)(2,1)S(1)} %collective-permute-done.13.refs_1_, ...), custom_call_target="tpu_custom_call" | custom-call | flops 3019898880 | bytes 21495808 | tf_op jit(solution)/shard_map/expert/pallas_call | solution.py:80
  87.5 7.9 %expert.5 = (bf16[40,4096]{1,0:T(8,128)(2,1)S(1)}, bf16[40,4096]{1,0:T(8,128)(2,1)S(1)}, bf16[40,4096]{1,0:T(8,128)(2,1)S(1)}, bf16[40,4096]{1,0:T(8,128)(2,1)S(1)}) custom-call(s32[3]{0:T(128)S(1)} %pad_add_fusion.place, bf16[40,4096]{1,0:T(8,128)(2,1)S(1)} %get-tuple-element.97.refs_0_, bf16[40,4096]{1,0:T(8,128)(2,1)S(1)} %collective-permute-done.17.refs_1_, ...), custom_call_target="tpu_custom_call" | custom-call | flops 3019898880 | bytes 21495808 | tf_op jit(solution)/shard_map/expert/pallas_call | solution.py:80
  97.4 1.5 collective-permute-start.22
  100.9 8.1 %expert.6 = (bf16[40,4096]{1,0:T(8,128)(2,1)S(1)}, bf16[40,4096]{1,0:T(8,128)(2,1)S(1)}, bf16[40,4096]{1,0:T(8,128)(2,1)S(1)}, bf16[40,4096]{1,0:T(8,128)(2,1)S(1)}) custom-call(s32[3]{0:T(128)S(1)} %pad_add_fusion.place, bf16[40,4096]{1,0:T(8,128)(2,1)S(1)} %get-tuple-element.107.refs_0_, bf16[40,4096]{1,0:T(8,128)(2,1)S(1)} %collective-permute-done.8.refs_1_, ...), custom_call_target="tpu_custom_call" | custom-call | flops 3019898880 | bytes 21495808 | tf_op jit(solution)/shard_map/expert/pallas_call | solution.py:80
  109.0 1.6 collective-permute-start.25
  110.6 3.9 %collective-permute-done.21.refs_2_ = bf16[40,4096]{1,0:T(8,128)(2,1)S(1)} collective-permute-done((bf16[40,4096]{1,0:T(8,128)(2,1)S(1)}, bf16[40,4096]{1,0:T(8,128)(2,1)S(1)}, u32[]{:S(2)}, u32[]{:S(2)}) %collective-permute-start.21) | collective-permute-done | bytes 327712 | tf_op jit(solution)/shard_map/ppermute | solution.py:17
  114.6 2.1 %combine.4 = bf16[64,4096]{1,0:T(8,128)(2,1)S(1)} custom-call(s32[3]{0:T(128)S(1)} %pad_add_fusion.place, bf16[64,4224]{1,0:T(8,128)(2,1)S(1)} %get-tuple-element.88.block, bf16[40,4096]{1,0:T(8,128)(2,1)S(1)} %get-tuple-element.101.refs_0_, bf16[40,4096]{1,0:T(8,128)(2,1)S(1)} %collective-permute-done.20.refs_1_, ...), custom_call_target="tpu_custom_call" | custom-call | bytes 2375680 | tf_op jit(solution)/shard_map/combine/pallas_call | solution.py:80
  116.7 2.4 %collective-permute-start.29 = (bf16[64,4096]{1,0:T(8,128)(2,1)S(1)}, bf16[64,4096]{1,0:T(8,128)(2,1)S(1)}, u32[]{:S(2)}, u32[]{:S(2)}) collective-permute-start(bf16[64,4096]{1,0:T(8,128)(2,1)S(1)} %combine.4), channel_id=1, source_target_pairs={{0,6},{1,7},{2,4},{3,5},{4,2},{5,3},{6,0},{7,1},{8,14},{9,15},{10,... | collective-permute-start | bytes 1572872 | tf_op jit(solution)/shard_map/ppermute | solution.py:17
  121.6 4.0 %collective-permute-done.24.refs_2_ = bf16[40,4096]{1,0:T(8,128)(2,1)S(1)} collective-permute-done((bf16[40,4096]{1,0:T(8,128)(2,1)S(1)}, bf16[40,4096]{1,0:T(8,128)(2,1)S(1)}, u32[]{:S(2)}, u32[]{:S(2)}) %collective-permute-start.24) | collective-permute-done | bytes 327712 | tf_op jit(solution)/shard_map/ppermute | solution.py:17
  125.6 1.6 collective-permute-start.28
  127.1 8.1 %expert.7 = (bf16[40,4096]{1,0:T(8,128)(2,1)S(1)}, bf16[40,4096]{1,0:T(8,128)(2,1)S(1)}, bf16[40,4096]{1,0:T(8,128)(2,1)S(1)}, bf16[40,4096]{1,0:T(8,128)(2,1)S(1)}) custom-call(s32[3]{0:T(128)S(1)} %pad_add_fusion.place, bf16[40,4096]{1,0:T(8,128)(2,1)S(1)} %get-tuple-element.112.refs_0_, bf16[40,4096]{1,0:T(8,128)(2,1)S(1)} %collective-permute-done.3.refs_1_, ...), custom_call_target="tpu_custom_call" | custom-call | flops 3019898880 | bytes 21495808 | tf_op jit(solution)/shard_map/expert/pallas_call | solution.py:80
  135.3 2.1 %combine.5 = bf16[64,4096]{1,0:T(8,128)(2,1)S(1)} custom-call(s32[3]{0:T(128)S(1)} %pad_add_fusion.place, bf16[64,4224]{1,0:T(8,128)(2,1)S(1)} %get-tuple-element.117.block, bf16[40,4096]{1,0:T(8,128)(2,1)S(1)} %get-tuple-element.96.refs_0_, bf16[40,4096]{1,0:T(8,128)(2,1)S(1)} %collective-permute-done.23.refs_1_, ...), custom_call_target="tpu_custom_call" | custom-call | bytes 2375680 | tf_op jit(solution)/shard_map/combine/pallas_call | solution.py:80
  137.4 6.5 %collective-permute-start.33 = (bf16[64,4096]{1,0:T(8,128)(2,1)S(1)}, bf16[64,4096]{1,0:T(8,128)(2,1)S(1)}, u32[]{:S(2)}, u32[]{:S(2)}) collective-permute-start(bf16[64,4096]{1,0:T(8,128)(2,1)S(1)} %combine.5), channel_id=1, source_target_pairs={{0,4},{1,5},{2,6},{3,7},{4,0},{5,1},{6,2},{7,3},{8,12},{9,13},{10,... | collective-permute-start | bytes 1572872 | tf_op jit(solution)/shard_map/ppermute | solution.py:17
  143.9 2.1 %combine.6 = bf16[64,4096]{1,0:T(8,128)(2,1)S(1)} custom-call(s32[3]{0:T(128)S(1)} %pad_add_fusion.place, bf16[64,4224]{1,0:T(8,128)(2,1)S(1)} %collective-permute-done.refs_0_.block, bf16[40,4096]{1,0:T(8,128)(2,1)S(1)} %get-tuple-element.111.refs_0_, bf16[40,4096]{1,0:T(8,128)(2,1)S(1)} %collective-permute-done.26.refs_1_, ...), custom_call_target="tpu_custom_call" | custom-call | bytes 2375680 | tf_op jit(solution)/shard_map/combine/pallas_call | solution.py:80
  146.1 2.4 %collective-permute-start.34 = (bf16[64,4096]{1,0:T(8,128)(2,1)S(1)}, bf16[64,4096]{1,0:T(8,128)(2,1)S(1)}, u32[]{:S(2)}, u32[]{:S(2)}) collective-permute-start(bf16[64,4096]{1,0:T(8,128)(2,1)S(1)} %combine.6), channel_id=1, source_target_pairs={{0,2},{1,3},{2,0},{3,1},{4,6},{5,7},{6,4},{7,5},{8,10},{9,11},{10,... | collective-permute-start | bytes 1572872 | tf_op jit(solution)/shard_map/ppermute | solution.py:17
  151.9 10.9 %collective-permute-done.33.refs_5_ = bf16[64,4096]{1,0:T(8,128)(2,1)S(1)} collective-permute-done((bf16[64,4096]{1,0:T(8,128)(2,1)S(1)}, bf16[64,4096]{1,0:T(8,128)(2,1)S(1)}, u32[]{:S(2)}, u32[]{:S(2)}) %collective-permute-start.33) | collective-permute-done | bytes 524320 | tf_op jit(solution)/shard_map/ppermute | solution.py:17
  162.8 6.1 %collective-permute-done.34.refs_6_ = bf16[64,4096]{1,0:T(8,128)(2,1)S(1)} collective-permute-done((bf16[64,4096]{1,0:T(8,128)(2,1)S(1)}, bf16[64,4096]{1,0:T(8,128)(2,1)S(1)}, u32[]{:S(2)}, u32[]{:S(2)}) %collective-permute-start.34) | collective-permute-done | bytes 524320 | tf_op jit(solution)/shard_map/ppermute | solution.py:17
  168.9 3.0 %combine.7 = bf16[64,4096]{1,0:T(8,128)(2,1)} custom-call(s32[3]{0:T(128)S(1)} %pad_add_fusion.place, bf16[64,4224]{1,0:T(8,128)(2,1)S(1)} %get-tuple-element.128.block, bf16[40,4096]{1,0:T(8,128)(2,1)S(1)} %get-tuple-element.116.refs_0_, bf16[40,4096]{1,0:T(8,128)(2,1)S(1)} %collective-permute-done.30.refs_1_, ...), custom_call_target="tpu_custom_call" | custom-call | bytes 3948544 | tf_op jit(solution)/shard_map/combine/pallas_call | solution.py:80
  (65 shorter events, 32.7 us)
Async XLA Ops:
  5.0 21.4 %collective-permute-start = (bf16[64,4224]{1,0:T(8,128)(2,1)S(1)}, bf16[64,4224]{1,0:T(8,128)(2,1)S(1)}, u32[]{:S(2)}, u32[]{:S(2)}) collective-permute-start(bf16[64,4224]{1,0:T(8,128)(2,1)S(1)} %get-tuple-element.128.block), channel_id=1, source_target_pairs={{0,2},{1,3},{2,0},{3,1},{4,6},{5,7},{6,4},{7,5},{8,10},{9,11},{10,... | collective-permute-start | bytes 1622024 | tf_op jit(solution)/shard_map/ppermute | solution.py:17
  7.5 18.9 %collective-permute-start.2 = (bf16[64,4224]{1,0:T(8,128)(2,1)S(1)}, bf16[64,4224]{1,0:T(8,128)(2,1)S(1)}, u32[]{:S(2)}, u32[]{:S(2)}) collective-permute-start(bf16[64,4224]{1,0:T(8,128)(2,1)S(1)} %get-tuple-element.128.block), channel_id=1, source_target_pairs={{2,4},{3,5},{4,2},{5,3},{10,12},{11,13},{12,10},{13,11},{18,20},{1... | collective-permute-start | bytes 1622024 | tf_op jit(solution)/shard_map/ppermute | solution.py:216
  8.2 10.6 %collective-permute-start.3 = (bf16[40,4096]{1,0:T(8,128)(2,1)S(1)}, bf16[40,4096]{1,0:T(8,128)(2,1)S(1)}, u32[]{:S(2)}, u32[]{:S(2)}) collective-permute-start(bf16[40,4096]{1,0:T(8,128)(2,1)S(1)} %get-tuple-element.72), channel_id=1, source_target_pairs={{0,8},{8,0},{16,24},{24,16},{1,9},{9,1},{17,25},{25,17},{2,10},{10... | collective-permute-start | bytes 983048 | tf_op jit(solution)/shard_map/ppermute | solution.py:17
  9.8 16.6 %collective-permute-start.4 = (bf16[40,4096]{1,0:T(8,128)(2,1)S(1)}, bf16[40,4096]{1,0:T(8,128)(2,1)S(1)}, u32[]{:S(2)}, u32[]{:S(2)}) collective-permute-start(bf16[40,4096]{1,0:T(8,128)(2,1)S(1)} %get-tuple-element.73), channel_id=1, source_target_pairs={{0,16},{8,24},{16,0},{24,8},{1,17},{9,25},{17,1},{25,9},{2,18},{10... | collective-permute-start | bytes 983048 | tf_op jit(solution)/shard_map/ppermute | solution.py:17
  11.3 15.1 %collective-permute-start.5 = (bf16[40,4096]{1,0:T(8,128)(2,1)S(1)}, bf16[40,4096]{1,0:T(8,128)(2,1)S(1)}, u32[]{:S(2)}, u32[]{:S(2)}) collective-permute-start(bf16[40,4096]{1,0:T(8,128)(2,1)S(1)} %get-tuple-element.74), channel_id=1, source_target_pairs={{0,24},{8,16},{16,8},{24,0},{1,25},{9,17},{17,9},{25,1},{2,26},{10... | collective-permute-start | bytes 983048 | tf_op jit(solution)/shard_map/ppermute | solution.py:17
  26.4 20.6 %collective-permute-start.7 = (bf16[64,4224]{1,0:T(8,128)(2,1)S(1)}, bf16[64,4224]{1,0:T(8,128)(2,1)S(1)}, u32[]{:S(2)}, u32[]{:S(2)}) collective-permute-start(bf16[64,4224]{1,0:T(8,128)(2,1)S(1)} %collective-permute-done.2.refs_0_), channel_id=1, source_target_pairs={{2,0},{3,1},{4,6},{5,7},{10,8},{11,9},{12,14},{13,15},{18,16},{19,... | collective-permute-start | bytes 1622024 | tf_op jit(solution)/shard_map/ppermute | solution.py:216
  27.7 19.3 %collective-permute-start.6 = (bf16[64,4224]{1,0:T(8,128)(2,1)S(1)}, bf16[64,4224]{1,0:T(8,128)(2,1)S(1)}, u32[]{:S(2)}, u32[]{:S(2)}) collective-permute-start(bf16[64,4224]{1,0:T(8,128)(2,1)S(1)} %collective-permute-done.refs_0_.block), channel_id=1, source_target_pairs={{2,4},{3,5},{4,2},{5,3},{10,12},{11,13},{12,10},{13,11},{18,20},{1... | collective-permute-start | bytes 1622024 | tf_op jit(solution)/shard_map/ppermute | solution.py:216
  29.9 10.7 %collective-permute-start.8 = (bf16[40,4096]{1,0:T(8,128)(2,1)S(1)}, bf16[40,4096]{1,0:T(8,128)(2,1)S(1)}, u32[]{:S(2)}, u32[]{:S(2)}) collective-permute-start(bf16[40,4096]{1,0:T(8,128)(2,1)S(1)} %get-tuple-element.77), channel_id=1, source_target_pairs={{0,8},{8,0},{16,24},{24,16},{1,9},{9,1},{17,25},{25,17},{2,10},{10... | collective-permute-start | bytes 983048 | tf_op jit(solution)/shard_map/ppermute | solution.py:17
  31.2 15.8 %collective-permute-start.9 = (bf16[40,4096]{1,0:T(8,128)(2,1)S(1)}, bf16[40,4096]{1,0:T(8,128)(2,1)S(1)}, u32[]{:S(2)}, u32[]{:S(2)}) collective-permute-start(bf16[40,4096]{1,0:T(8,128)(2,1)S(1)} %get-tuple-element.78), channel_id=1, source_target_pairs={{0,16},{8,24},{16,0},{24,8},{1,17},{9,25},{17,1},{25,9},{2,18},{10... | collective-permute-start | bytes 983048 | tf_op jit(solution)/shard_map/ppermute | solution.py:17
  32.0 15.0 %collective-permute-start.10 = (bf16[40,4096]{1,0:T(8,128)(2,1)S(1)}, bf16[40,4096]{1,0:T(8,128)(2,1)S(1)}, u32[]{:S(2)}, u32[]{:S(2)}) collective-permute-start(bf16[40,4096]{1,0:T(8,128)(2,1)S(1)} %get-tuple-element.79), channel_id=1, source_target_pairs={{0,24},{8,16},{16,8},{24,0},{1,25},{9,17},{17,9},{25,1},{2,26},{10... | collective-permute-start | bytes 983048 | tf_op jit(solution)/shard_map/ppermute | solution.py:17
  48.5 20.0 %collective-permute-start.12 = (bf16[4096,384]{1,0:T(8,128)(2,1)}, bf16[4096,384]{1,0:T(8,128)(2,1)S(1)}, u32[]{:S(2)}, u32[]{:S(2)}) collective-permute-start(bf16[4096,384]{1,0:T(8,128)(2,1)} %refs_5_.7), channel_id=1, source_target_pairs={{0,1},{1,0},{2,3},{3,2},{4,5},{5,4},{6,7},{7,6},{8,9},{9,8},{10,11... | collective-permute-start | bytes 9437192 | tf_op jit(solution)/shard_map/ppermute | solution.py:17
  48.5 19.9 %collective-permute-start.11 = (bf16[64,4224]{1,0:T(8,128)(2,1)S(1)}, bf16[64,4224]{1,0:T(8,128)(2,1)S(1)}, u32[]{:S(2)}, u32[]{:S(2)}) collective-permute-start(bf16[64,4224]{1,0:T(8,128)(2,1)S(1)} %get-tuple-element.117.block), channel_id=1, source_target_pairs={{2,0},{3,1},{4,6},{5,7},{10,8},{11,9},{12,14},{13,15},{18,16},{19,... | collective-permute-start | bytes 1622024 | tf_op jit(solution)/shard_map/ppermute | solution.py:216
  50.7 16.8 %collective-permute-start.14 = (bf16[40,4096]{1,0:T(8,128)(2,1)S(1)}, bf16[40,4096]{1,0:T(8,128)(2,1)S(1)}, u32[]{:S(2)}, u32[]{:S(2)}) collective-permute-start(bf16[40,4096]{1,0:T(8,128)(2,1)S(1)} %get-tuple-element.85), channel_id=1, source_target_pairs={{0,16},{8,24},{16,0},{24,8},{1,17},{9,25},{17,1},{25,9},{2,18},{10... | collective-permute-start | bytes 983048 | tf_op jit(solution)/shard_map/ppermute | solution.py:17
  52.1 15.4 %collective-permute-start.15 = (bf16[40,4096]{1,0:T(8,128)(2,1)S(1)}, bf16[40,4096]{1,0:T(8,128)(2,1)S(1)}, u32[]{:S(2)}, u32[]{:S(2)}) collective-permute-start(bf16[40,4096]{1,0:T(8,128)(2,1)S(1)} %get-tuple-element.86), channel_id=1, source_target_pairs={{0,24},{8,16},{16,8},{24,0},{1,25},{9,17},{17,9},{25,1},{2,26},{10... | collective-permute-start | bytes 983048 | tf_op jit(solution)/shard_map/ppermute | solution.py:17
  70.0 17.4 %collective-permute-start.17 = (bf16[40,4096]{1,0:T(8,128)(2,1)S(1)}, bf16[40,4096]{1,0:T(8,128)(2,1)S(1)}, u32[]{:S(2)}, u32[]{:S(2)}) collective-permute-start(bf16[40,4096]{1,0:T(8,128)(2,1)S(1)} %get-tuple-element.98), channel_id=1, source_target_pairs={{0,8},{8,0},{16,24},{24,16},{1,9},{9,1},{17,25},{25,17},{2,10},{10... | collective-permute-start | bytes 983048 | tf_op jit(solution)/shard_map/ppermute | solution.py:17
  70.7 16.8 %collective-permute-start.18 = (bf16[40,4096]{1,0:T(8,128)(2,1)S(1)}, bf16[40,4096]{1,0:T(8,128)(2,1)S(1)}, u32[]{:S(2)}, u32[]{:S(2)}) collective-permute-start(bf16[40,4096]{1,0:T(8,128)(2,1)S(1)} %get-tuple-element.99), channel_id=1, source_target_pairs={{0,16},{8,24},{16,0},{24,8},{1,17},{9,25},{17,1},{25,9},{2,18},{10... | collective-permute-start | bytes 983048 | tf_op jit(solution)/shard_map/ppermute | solution.py:17
  72.1 15.4 %collective-permute-start.19 = (bf16[40,4096]{1,0:T(8,128)(2,1)S(1)}, bf16[40,4096]{1,0:T(8,128)(2,1)S(1)}, u32[]{:S(2)}, u32[]{:S(2)}) collective-permute-start(bf16[40,4096]{1,0:T(8,128)(2,1)S(1)} %get-tuple-element.100), channel_id=1, source_target_pairs={{0,24},{8,16},{16,8},{24,0},{1,25},{9,17},{17,9},{25,1},{2,26},{10... | collective-permute-start | bytes 983048 | tf_op jit(solution)/shard_map/ppermute | solution.py:17
  95.4 13.6 %collective-permute-start.20 = (bf16[40,4096]{1,0:T(8,128)(2,1)S(1)}, bf16[40,4096]{1,0:T(8,128)(2,1)S(1)}, u32[]{:S(2)}, u32[]{:S(2)}) collective-permute-start(bf16[40,4096]{1,0:T(8,128)(2,1)S(1)} %get-tuple-element.102), channel_id=1, source_target_pairs={{0,8},{8,0},{16,24},{24,16},{1,9},{9,1},{17,25},{25,17},{2,10},{10... | collective-permute-start | bytes 983048 | tf_op jit(solution)/shard_map/ppermute | solution.py:17
  96.9 17.7 %collective-permute-start.21 = (bf16[40,4096]{1,0:T(8,128)(2,1)S(1)}, bf16[40,4096]{1,0:T(8,128)(2,1)S(1)}, u32[]{:S(2)}, u32[]{:S(2)}) collective-permute-start(bf16[40,4096]{1,0:T(8,128)(2,1)S(1)} %get-tuple-element.103), channel_id=1, source_target_pairs={{0,16},{8,24},{16,0},{24,8},{1,17},{9,25},{17,1},{25,9},{2,18},{10... | collective-permute-start | bytes 983048 | tf_op jit(solution)/shard_map/ppermute | solution.py:17
  97.4 17.1 %collective-permute-start.22 = (bf16[40,4096]{1,0:T(8,128)(2,1)S(1)}, bf16[40,4096]{1,0:T(8,128)(2,1)S(1)}, u32[]{:S(2)}, u32[]{:S(2)}) collective-permute-start(bf16[40,4096]{1,0:T(8,128)(2,1)S(1)} %get-tuple-element.104), channel_id=1, source_target_pairs={{0,24},{8,16},{16,8},{24,0},{1,25},{9,17},{17,9},{25,1},{2,26},{10... | collective-permute-start | bytes 983048 | tf_op jit(solution)/shard_map/ppermute | solution.py:17
  99.0 21.6 %collective-permute-start.23 = (bf16[40,4096]{1,0:T(8,128)(2,1)S(1)}, bf16[40,4096]{1,0:T(8,128)(2,1)S(1)}, u32[]{:S(2)}, u32[]{:S(2)}) collective-permute-start(bf16[40,4096]{1,0:T(8,128)(2,1)S(1)} %get-tuple-element.118), channel_id=1, source_target_pairs={{0,8},{8,0},{16,24},{24,16},{1,9},{9,1},{17,25},{25,17},{2,10},{10... | collective-permute-start | bytes 983048 | tf_op jit(solution)/shard_map/ppermute | solution.py:17
  100.4 25.2 %collective-permute-start.24 = (bf16[40,4096]{1,0:T(8,128)(2,1)S(1)}, bf16[40,4096]{1,0:T(8,128)(2,1)S(1)}, u32[]{:S(2)}, u32[]{:S(2)}) collective-permute-start(bf16[40,4096]{1,0:T(8,128)(2,1)S(1)} %get-tuple-element.119), channel_id=1, source_target_pairs={{0,16},{8,24},{16,0},{24,8},{1,17},{9,25},{17,1},{25,9},{2,18},{10... | collective-permute-start | bytes 983048 | tf_op jit(solution)/shard_map/ppermute | solution.py:17
  109.0 26.3 %collective-permute-start.25 = (bf16[40,4096]{1,0:T(8,128)(2,1)S(1)}, bf16[40,4096]{1,0:T(8,128)(2,1)S(1)}, u32[]{:S(2)}, u32[]{:S(2)}) collective-permute-start(bf16[40,4096]{1,0:T(8,128)(2,1)S(1)} %get-tuple-element.120), channel_id=1, source_target_pairs={{0,24},{8,16},{16,8},{24,0},{1,25},{9,17},{17,9},{25,1},{2,26},{10... | collective-permute-start | bytes 983048 | tf_op jit(solution)/shard_map/ppermute | solution.py:17
  116.7 31.7 %collective-permute-start.29 = (bf16[64,4096]{1,0:T(8,128)(2,1)S(1)}, bf16[64,4096]{1,0:T(8,128)(2,1)S(1)}, u32[]{:S(2)}, u32[]{:S(2)}) collective-permute-start(bf16[64,4096]{1,0:T(8,128)(2,1)S(1)} %combine.4), channel_id=1, source_target_pairs={{0,6},{1,7},{2,4},{3,5},{4,2},{5,3},{6,0},{7,1},{8,14},{9,15},{10,... | collective-permute-start | bytes 1572872 | tf_op jit(solution)/shard_map/ppermute | solution.py:17
  119.1 24.8 %collective-permute-start.26 = (bf16[40,4096]{1,0:T(8,128)(2,1)S(1)}, bf16[40,4096]{1,0:T(8,128)(2,1)S(1)}, u32[]{:S(2)}, u32[]{:S(2)}) collective-permute-start(bf16[40,4096]{1,0:T(8,128)(2,1)S(1)} %get-tuple-element.123), channel_id=1, source_target_pairs={{0,8},{8,0},{16,24},{24,16},{1,9},{9,1},{17,25},{25,17},{2,10},{10... | collective-permute-start | bytes 983048 | tf_op jit(solution)/shard_map/ppermute | solution.py:17
  120.6 23.4 %collective-permute-start.27 = (bf16[40,4096]{1,0:T(8,128)(2,1)S(1)}, bf16[40,4096]{1,0:T(8,128)(2,1)S(1)}, u32[]{:S(2)}, u32[]{:S(2)}) collective-permute-start(bf16[40,4096]{1,0:T(8,128)(2,1)S(1)} %get-tuple-element.125), channel_id=1, source_target_pairs={{0,16},{8,24},{16,0},{24,8},{1,17},{9,25},{17,1},{25,9},{2,18},{10... | collective-permute-start | bytes 983048 | tf_op jit(solution)/shard_map/ppermute | solution.py:17
  125.6 18.4 %collective-permute-start.28 = (bf16[40,4096]{1,0:T(8,128)(2,1)S(1)}, bf16[40,4096]{1,0:T(8,128)(2,1)S(1)}, u32[]{:S(2)}, u32[]{:S(2)}) collective-permute-start(bf16[40,4096]{1,0:T(8,128)(2,1)S(1)} %get-tuple-element.127), channel_id=1, source_target_pairs={{0,24},{8,16},{16,8},{24,0},{1,25},{9,17},{17,9},{25,1},{2,26},{10... | collective-permute-start | bytes 983048 | tf_op jit(solution)/shard_map/ppermute | solution.py:17
  137.4 25.4 %collective-permute-start.33 = (bf16[64,4096]{1,0:T(8,128)(2,1)S(1)}, bf16[64,4096]{1,0:T(8,128)(2,1)S(1)}, u32[]{:S(2)}, u32[]{:S(2)}) collective-permute-start(bf16[64,4096]{1,0:T(8,128)(2,1)S(1)} %combine.5), channel_id=1, source_target_pairs={{0,4},{1,5},{2,6},{3,7},{4,0},{5,1},{6,2},{7,3},{8,12},{9,13},{10,... | collective-permute-start | bytes 1572872 | tf_op jit(solution)/shard_map/ppermute | solution.py:17
  146.1 22.8 %collective-permute-start.34 = (bf16[64,4096]{1,0:T(8,128)(2,1)S(1)}, bf16[64,4096]{1,0:T(8,128)(2,1)S(1)}, u32[]{:S(2)}, u32[]{:S(2)}) collective-permute-start(bf16[64,4096]{1,0:T(8,128)(2,1)S(1)} %combine.6), channel_id=1, source_target_pairs={{0,2},{1,3},{2,0},{3,1},{4,6},{5,7},{6,4},{7,5},{8,10},{9,11},{10,... | collective-permute-start | bytes 1572872 | tf_op jit(solution)/shard_map/ppermute | solution.py:17
  148.4 20.4 %collective-permute-start.30 = (bf16[40,4096]{1,0:T(8,128)(2,1)S(1)}, bf16[40,4096]{1,0:T(8,128)(2,1)S(1)}, u32[]{:S(2)}, u32[]{:S(2)}) collective-permute-start(bf16[40,4096]{1,0:T(8,128)(2,1)S(1)} %get-tuple-element.130), channel_id=1, source_target_pairs={{0,8},{8,0},{16,24},{24,16},{1,9},{9,1},{17,25},{25,17},{2,10},{10... | collective-permute-start | bytes 983048 | tf_op jit(solution)/shard_map/ppermute | solution.py:17
  149.2 19.7 %collective-permute-start.31 = (bf16[40,4096]{1,0:T(8,128)(2,1)S(1)}, bf16[40,4096]{1,0:T(8,128)(2,1)S(1)}, u32[]{:S(2)}, u32[]{:S(2)}) collective-permute-start(bf16[40,4096]{1,0:T(8,128)(2,1)S(1)} %get-tuple-element.132), channel_id=1, source_target_pairs={{0,16},{8,24},{16,0},{24,8},{1,17},{9,25},{17,1},{25,9},{2,18},{10... | collective-permute-start | bytes 983048 | tf_op jit(solution)/shard_map/ppermute | solution.py:17
  150.4 18.4 %collective-permute-start.32 = (bf16[40,4096]{1,0:T(8,128)(2,1)S(1)}, bf16[40,4096]{1,0:T(8,128)(2,1)S(1)}, u32[]{:S(2)}, u32[]{:S(2)}) collective-permute-start(bf16[40,4096]{1,0:T(8,128)(2,1)S(1)} %get-tuple-element.134), channel_id=1, source_target_pairs={{0,24},{8,16},{16,8},{24,0},{1,25},{9,17},{17,9},{25,1},{2,26},{10... | collective-permute-start | bytes 983048 | tf_op jit(solution)/shard_map/ppermute | solution.py:17
  (10 other events, 117.0 us)

commit v4 on v3

--- a/solution.py
+++ b/solution.py
@@ -9,7 +9,7 @@
 
 LANES = 128
 ORDER = [(2,), (3,), (1,), (0,)]
-VMEM_BYTES, EXPERT_BYTES = 8 * 2**20, 44 * 2**20
+VMEM_BYTES, EXPERT_BYTES = 8 * 2**20, 26 * 2**20
 
 
 def swap(value, axis, mask):
@@ -83,7 +83,7 @@
         in_specs=[smem()] + [vmem()] * (len(inputs) - stay) + [pl.BlockSpec(memory_space=pltpu.HBM)] * stay,
         out_specs=[vmem()] * len(outs),
         scratch_shapes=list(scratch),
-        compiler_params=pltpu.CompilerParams(vmem_limit_bytes=EXPERT_BYTES if stay else VMEM_BYTES),
+        compiler_params=pltpu.CompilerParams(vmem_limit_bytes=EXPERT_BYTES if flops else VMEM_BYTES),
         cost_estimate=pl.CostEstimate(flops=flops, bytes_accessed=moved, transcendentals=0),
         name=name,
     )(place, *inputs)
@@ -132,10 +132,10 @@
 def expert_kernel(capacity, count, place, *refs):
     rows, weights, outs = refs[:count], refs[count : count + 6], refs[count + 6 : 2 * count + 6]
     refs = refs[2 * count + 6 :]
-    x, hidden, held, sems = refs[0], refs[1], refs[2:8], refs[8]
+    x, hidden, held, sems = refs[0], refs[1], [*weights[:3], *refs[2:5]], refs[5]
     cuts = 2
     copies = []
-    for i, (source, target) in enumerate(zip(weights, held)):
+    for i, (source, target) in enumerate(zip(weights[3:], held[3:])):
         step = source.shape[0] // cuts
         copies.append(
             [
@@ -145,8 +145,7 @@
                 for c in range(cuts)
             ]
         )
-    order = [copies[i + j][c] for i in (0, 3) for c in range(cuts) for j in range(2)]
-    order += [copies[i][c] for i in (2, 5) for c in range(cuts)]
+    order = [copies[i][c] for c in range(cuts) for i in range(2)] + copies[2]
     for copy in order:
         copy.start()
     x[...] = jnp.concatenate([ref[...].astype(jnp.float32) for ref in rows], axis=0).astype(jnp.bfloat16)
@@ -156,17 +155,16 @@
         product = None
         for k in range(0, x.shape[1], depth):
             for c in range(cuts):
-                if k == c * (x.shape[1] // cuts):
-                    copies[3 * i][c].wait()
-                    copies[3 * i + 1][c].wait()
+                if i == 1 and k == c * (x.shape[1] // cuts):
+                    copies[0][c].wait()
+                    copies[1][c].wait()
             both = jnp.concatenate([held[3 * i][k : k + depth, :], held[3 * i + 1][k : k + depth, :]], axis=1)
             term = jnp.dot(x[:, k : k + depth], both, preferred_element_type=jnp.float32)
             product = term if product is None else product + term
         gate, up = product[:, :size], product[:, size:]
         hidden[:, i * size : (i + 1) * size] = (gate / (1.0 + jnp.exp(-gate)) * up).astype(jnp.bfloat16)
-    for i in (2, 5):
-        for copy in copies[i]:
-            copy.wait()
+    for copy in copies[2]:
+        copy.wait()
     tile = 512
     for start in range(0, x.shape[1], tile):
         result = jnp.dot(hidden[:, :size], held[2][:, start : start + tile], preferred_element_type=jnp.float32)
@@ -181,9 +179,9 @@
         scaled = hot * weight
         high = scaled.astype(jnp.bfloat16)
         low = (scaled - high.astype(jnp.float32)).astype(jnp.bfloat16)
-        for factor in (high, low):
-            piece = jnp.dot(factor, value, preferred_element_type=jnp.float32)
-            total = piece if total is None else total + piece
+        both = jnp.dot(jnp.concatenate([high, low], axis=0), value, preferred_element_type=jnp.float32)
+        piece = both[: hot.shape[0]] + both[hot.shape[0] :]
+        total = piece if total is None else total + piece
     return total
 
 
@@ -273,10 +271,10 @@
                 pltpu.VMEM((count * capacity, width), jnp.bfloat16),
                 pltpu.VMEM((count * capacity, 2 * w_gate.shape[1]), jnp.bfloat16),
             ]
-            + [pltpu.VMEM(weight.shape, weight.dtype) for weight in own * 2]
-            + [pltpu.SemaphoreType.DMA((12,))],
+            + [pltpu.VMEM(weight.shape, weight.dtype) for weight in own]
+            + [pltpu.SemaphoreType.DMA((6,))],
             flops=12 * count * capacity * width * w_gate.shape[1],
-            stay=6,
+            stay=3,
         )
         last[:] = [outs[0]]
         for i, step in enumerate(group):
@@ -287,7 +285,7 @@
         run(group)
     sums, totals = [], []
     for step in reversed(range(chain)):
-        ready = [*totals[-2:-1], *sums[:-2]] if step < chain - 2 else []
+        ready = [*totals[:1], *(sums[:1] if step == 0 else [])] if step < chain - 2 else []
         result = results[step]
         returned = send([result[0]] + [after(value, ready) for value in result[1:]])
         (total,) = call(

time: 172 us -> 171 us (level)
  waiting for transfers between devices: 70.3 us -> 74.4 us
  Pallas kernels: 47.6 us -> 43.8 us
    ppermute x31, waiting for transfers between devices: 69.3 us -> 73.5 us  [swap(): return lax.ppermute(value, axis, pairs)]
    pallas_call x12, Pallas kernels: 47.6 us -> 43.8 us  [call(): pl.pallas_call(kernel, out_shape=outs, in_specs=[smem()] + [vmem()] * (le...]
    unnamed x14 -> x12, local copies, waits for them, and re-layouts: 6.28 us -> 6.46 us
  transfers between devices with their start and end apart: 35 -> 35, of which waited for: 13 -> 13; matrix products, arithmetic and copies ran while one was open for 0% -> 0% of each run, Pallas kernels for 20% -> 18%
where the time goes in v4:
time: 171 us
  waiting for transfers between devices  74.4 us (44%)
  starting transfers between devices  46.2 us (27%)
  Pallas kernels  43.8 us (26%)
  local copies, waits for them, and re-layouts  6.46 us (4%)
    ppermute x31, waiting for transfers between devices, swap(): return lax.ppermute(value, axis, pairs)  73.5 us
    pallas_call x12, Pallas kernels, call(): pl.pallas_call(kernel, out_shape=outs, in_specs=[smem()] + [vmem()] * (le...  43.8 us
    ppermute x31, starting transfers between devices, swap(): return lax.ppermute(value, axis, pairs)  42.1 us
    unnamed x12, local copies, waits for them, and re-layouts  6.46 us
    ppermute x4, starting transfers between devices, per_device(): hop = lambda value, pairs: lax.ppermute(value, 'local', chain_pairs(pairs))  4.14 us
  transfers between devices with their start and end apart: 35, of which 13 were waited for; matrix products, arithmetic and copies ran while one was open for 0% of the time, Pallas kernels for 18%

profile of v4, /device:TPU:0, one launch (start us, length us, event | category | flops | bytes accessed | tf_op | source)
XLA Modules:
  0.0 171.2 jit_solution(4445425313750644693)
XLA Ops:
  3.2 1.8 %first.1 = (bf16[64,4224]{1,0:T(8,128)(2,1)S(1)}, bf16[40,4096]{1,0:T(8,128)(2,1)S(1)}, bf16[40,4096]{1,0:T(8,128)(2,1)S(1)}, bf16[40,4096]{1,0:T(8,128)(2,1)S(1)}, bf16[40,4096]{1,0:T(8,128)(2,1)S(1)}) custom-call(s32[3]{0:T(128)S(1)} %pad_add_fusion.place, bf16[64,4096]{1,0:T(8,128)(2,1)S(1)} %copy-done.3, s32[8,64]{1,0:T(8,128)S(1)} %bitcast.5, ...), custom_call_target="tpu_custom_call" | custom-call | bytes 2377728 | tf_op jit(solution)/shard_map/first/pallas_call | solution.py:80
  5.0 2.5 %collective-permute-start = (bf16[64,4224]{1,0:T(8,128)(2,1)S(1)}, bf16[64,4224]{1,0:T(8,128)(2,1)S(1)}, u32[]{:S(2)}, u32[]{:S(2)}) collective-permute-start(bf16[64,4224]{1,0:T(8,128)(2,1)S(1)} %get-tuple-element.128.block), channel_id=1, source_target_pairs={{0,2},{1,3},{2,0},{3,1},{4,6},{5,7},{6,4},{7,5},{8,10},{9,11},{10,... | collective-permute-start | bytes 1622024 | tf_op jit(solution)/shard_map/ppermute | solution.py:17
  8.2 1.5 collective-permute-start.3
  9.8 1.5 collective-permute-start.4
  11.8 7.0 %collective-permute-done.3.refs_1_ = bf16[40,4096]{1,0:T(8,128)(2,1)S(1)} collective-permute-done((bf16[40,4096]{1,0:T(8,128)(2,1)S(1)}, bf16[40,4096]{1,0:T(8,128)(2,1)S(1)}, u32[]{:S(2)}, u32[]{:S(2)}) %collective-permute-start.3) | collective-permute-done | bytes 327712 | tf_op jit(solution)/shard_map/ppermute | solution.py:17
  18.8 7.6 %collective-permute-done.4.refs_2_ = bf16[40,4096]{1,0:T(8,128)(2,1)S(1)} collective-permute-done((bf16[40,4096]{1,0:T(8,128)(2,1)S(1)}, bf16[40,4096]{1,0:T(8,128)(2,1)S(1)}, u32[]{:S(2)}, u32[]{:S(2)}) %collective-permute-start.4) | collective-permute-done | bytes 327712 | tf_op jit(solution)/shard_map/ppermute | solution.py:17
  33.4 7.2 %collective-permute-done.8.refs_1_ = bf16[40,4096]{1,0:T(8,128)(2,1)S(1)} collective-permute-done((bf16[40,4096]{1,0:T(8,128)(2,1)S(1)}, bf16[40,4096]{1,0:T(8,128)(2,1)S(1)}, u32[]{:S(2)}, u32[]{:S(2)}) %collective-permute-start.8) | collective-permute-done | bytes 327712 | tf_op jit(solution)/shard_map/ppermute | solution.py:17
  40.6 6.4 %collective-permute-done.9.refs_2_ = bf16[40,4096]{1,0:T(8,128)(2,1)S(1)} collective-permute-done((bf16[40,4096]{1,0:T(8,128)(2,1)S(1)}, bf16[40,4096]{1,0:T(8,128)(2,1)S(1)}, u32[]{:S(2)}, u32[]{:S(2)}) %collective-permute-start.9) | collective-permute-done | bytes 327712 | tf_op jit(solution)/shard_map/ppermute | solution.py:17
  53.6 7.0 %collective-permute-done.13.refs_1_ = bf16[40,4096]{1,0:T(8,128)(2,1)S(1)} collective-permute-done((bf16[40,4096]{1,0:T(8,128)(2,1)S(1)}, bf16[40,4096]{1,0:T(8,128)(2,1)S(1)}, u32[]{:S(2)}, u32[]{:S(2)}) %collective-permute-start.13) | collective-permute-done | bytes 327712 | tf_op jit(solution)/shard_map/ppermute | solution.py:17
  60.6 6.9 %collective-permute-done.14.refs_2_ = bf16[40,4096]{1,0:T(8,128)(2,1)S(1)} collective-permute-done((bf16[40,4096]{1,0:T(8,128)(2,1)S(1)}, bf16[40,4096]{1,0:T(8,128)(2,1)S(1)}, u32[]{:S(2)}, u32[]{:S(2)}) %collective-permute-start.14) | collective-permute-done | bytes 327712 | tf_op jit(solution)/shard_map/ppermute | solution.py:17
  73.6 2.3 %collective-permute-done.16.refs_9_ = bf16[384,4096]{1,0:T(8,128)(2,1)S(1)} collective-permute-done((bf16[384,4096]{1,0:T(8,128)(2,1)}, bf16[384,4096]{1,0:T(8,128)(2,1)S(1)}, u32[]{:S(2)}, u32[]{:S(2)}) %collective-permute-start.16) | collective-permute-done | bytes 3145760 | tf_op jit(solution)/shard_map/ppermute | solution.py:17
  75.9 1.9 %copy-done.1 = bf16[4096,384]{1,0:T(8,128)(2,1)S(1)} copy-done((bf16[4096,384]{1,0:T(8,128)(2,1)S(1)}, bf16[4096,384]{1,0:T(8,128)(2,1)}, u32[]{:S(2)}) %copy-start.1) | copy-done | bytes 3145752
  77.8 1.9 %copy-done.2 = bf16[384,4096]{1,0:T(8,128)(2,1)S(1)} copy-done((bf16[384,4096]{1,0:T(8,128)(2,1)S(1)}, bf16[384,4096]{1,0:T(8,128)(2,1)}, u32[]{:S(2)}) %copy-start.2) | copy-done | bytes 3145752
  79.6 6.9 %expert.4 = (bf16[40,4096]{1,0:T(8,128)(2,1)S(1)}, bf16[40,4096]{1,0:T(8,128)(2,1)S(1)}, bf16[40,4096]{1,0:T(8,128)(2,1)S(1)}, bf16[40,4096]{1,0:T(8,128)(2,1)S(1)}) custom-call(s32[3]{0:T(128)S(1)} %pad_add_fusion.place, bf16[40,4096]{1,0:T(8,128)(2,1)S(1)} %get-tuple-element.90.refs_0_, bf16[40,4096]{1,0:T(8,128)(2,1)S(1)} %collective-permute-done.13.refs_1_, ...), custom_call_target="tpu_custom_call" | custom-call | flops 3019898880 | bytes 21495808 | tf_op jit(solution)/shard_map/expert/pallas_call | solution.py:80
  87.5 7.0 %expert.5 = (bf16[40,4096]{1,0:T(8,128)(2,1)S(1)}, bf16[40,4096]{1,0:T(8,128)(2,1)S(1)}, bf16[40,4096]{1,0:T(8,128)(2,1)S(1)}, bf16[40,4096]{1,0:T(8,128)(2,1)S(1)}) custom-call(s32[3]{0:T(128)S(1)} %pad_add_fusion.place, bf16[40,4096]{1,0:T(8,128)(2,1)S(1)} %get-tuple-element.97.refs_0_, bf16[40,4096]{1,0:T(8,128)(2,1)S(1)} %collective-permute-done.17.refs_1_, ...), custom_call_target="tpu_custom_call" | custom-call | flops 3019898880 | bytes 21495808 | tf_op jit(solution)/shard_map/expert/pallas_call | solution.py:80
  94.4 1.5 collective-permute-start.20
  96.5 1.5 collective-permute-start.22
  100.0 7.2 %expert.6 = (bf16[40,4096]{1,0:T(8,128)(2,1)S(1)}, bf16[40,4096]{1,0:T(8,128)(2,1)S(1)}, bf16[40,4096]{1,0:T(8,128)(2,1)S(1)}, bf16[40,4096]{1,0:T(8,128)(2,1)S(1)}) custom-call(s32[3]{0:T(128)S(1)} %pad_add_fusion.place, bf16[40,4096]{1,0:T(8,128)(2,1)S(1)} %get-tuple-element.107.refs_0_, bf16[40,4096]{1,0:T(8,128)(2,1)S(1)} %collective-permute-done.8.refs_1_, ...), custom_call_target="tpu_custom_call" | custom-call | flops 3019898880 | bytes 21495808 | tf_op jit(solution)/shard_map/expert/pallas_call | solution.py:80
  107.2 1.6 collective-permute-start.25
  108.8 4.8 %collective-permute-done.21.refs_2_ = bf16[40,4096]{1,0:T(8,128)(2,1)S(1)} collective-permute-done((bf16[40,4096]{1,0:T(8,128)(2,1)S(1)}, bf16[40,4096]{1,0:T(8,128)(2,1)S(1)}, u32[]{:S(2)}, u32[]{:S(2)}) %collective-permute-start.21) | collective-permute-done | bytes 327712 | tf_op jit(solution)/shard_map/ppermute | solution.py:17
  113.6 2.1 %combine.4 = bf16[64,4096]{1,0:T(8,128)(2,1)S(1)} custom-call(s32[3]{0:T(128)S(1)} %pad_add_fusion.place, bf16[64,4224]{1,0:T(8,128)(2,1)S(1)} %get-tuple-element.88.block, bf16[40,4096]{1,0:T(8,128)(2,1)S(1)} %get-tuple-element.101.refs_0_, bf16[40,4096]{1,0:T(8,128)(2,1)S(1)} %collective-permute-done.20.refs_1_, ...), custom_call_target="tpu_custom_call" | custom-call | bytes 2375680 | tf_op jit(solution)/shard_map/combine/pallas_call | solution.py:80
  115.7 2.4 %collective-permute-start.29 = (bf16[64,4096]{1,0:T(8,128)(2,1)S(1)}, bf16[64,4096]{1,0:T(8,128)(2,1)S(1)}, u32[]{:S(2)}, u32[]{:S(2)}) collective-permute-start(bf16[64,4096]{1,0:T(8,128)(2,1)S(1)} %combine.4), channel_id=1, source_target_pairs={{0,6},{1,7},{2,4},{3,5},{4,2},{5,3},{6,0},{7,1},{8,14},{9,15},{10,... | collective-permute-start | bytes 1572872 | tf_op jit(solution)/shard_map/ppermute | solution.py:17
  120.6 5.4 %collective-permute-done.24.refs_2_ = bf16[40,4096]{1,0:T(8,128)(2,1)S(1)} collective-permute-done((bf16[40,4096]{1,0:T(8,128)(2,1)S(1)}, bf16[40,4096]{1,0:T(8,128)(2,1)S(1)}, u32[]{:S(2)}, u32[]{:S(2)}) %collective-permute-start.24) | collective-permute-done | bytes 327712 | tf_op jit(solution)/shard_map/ppermute | solution.py:17
  126.1 1.5 collective-permute-start.28
  127.6 7.2 %expert.7 = (bf16[40,4096]{1,0:T(8,128)(2,1)S(1)}, bf16[40,4096]{1,0:T(8,128)(2,1)S(1)}, bf16[40,4096]{1,0:T(8,128)(2,1)S(1)}, bf16[40,4096]{1,0:T(8,128)(2,1)S(1)}) custom-call(s32[3]{0:T(128)S(1)} %pad_add_fusion.place, bf16[40,4096]{1,0:T(8,128)(2,1)S(1)} %get-tuple-element.112.refs_0_, bf16[40,4096]{1,0:T(8,128)(2,1)S(1)} %collective-permute-done.3.refs_1_, ...), custom_call_target="tpu_custom_call" | custom-call | flops 3019898880 | bytes 21495808 | tf_op jit(solution)/shard_map/expert/pallas_call | solution.py:80
  134.8 2.1 %combine.5 = bf16[64,4096]{1,0:T(8,128)(2,1)S(1)} custom-call(s32[3]{0:T(128)S(1)} %pad_add_fusion.place, bf16[64,4224]{1,0:T(8,128)(2,1)S(1)} %get-tuple-element.117.block, bf16[40,4096]{1,0:T(8,128)(2,1)S(1)} %get-tuple-element.96.refs_0_, bf16[40,4096]{1,0:T(8,128)(2,1)S(1)} %collective-permute-done.23.refs_1_, ...), custom_call_target="tpu_custom_call" | custom-call | bytes 2375680 | tf_op jit(solution)/shard_map/combine/pallas_call | solution.py:80
  136.9 4.4 %collective-permute-start.33 = (bf16[64,4096]{1,0:T(8,128)(2,1)S(1)}, bf16[64,4096]{1,0:T(8,128)(2,1)S(1)}, u32[]{:S(2)}, u32[]{:S(2)}) collective-permute-start(bf16[64,4096]{1,0:T(8,128)(2,1)S(1)} %combine.5), channel_id=1, source_target_pairs={{0,4},{1,5},{2,6},{3,7},{4,0},{5,1},{6,2},{7,3},{8,12},{9,13},{10,... | collective-permute-start | bytes 1572872 | tf_op jit(solution)/shard_map/ppermute | solution.py:17
  141.3 2.1 %combine.6 = bf16[64,4096]{1,0:T(8,128)(2,1)S(1)} custom-call(s32[3]{0:T(128)S(1)} %pad_add_fusion.place, bf16[64,4224]{1,0:T(8,128)(2,1)S(1)} %collective-permute-done.refs_0_.block, bf16[40,4096]{1,0:T(8,128)(2,1)S(1)} %get-tuple-element.111.refs_0_, bf16[40,4096]{1,0:T(8,128)(2,1)S(1)} %collective-permute-done.26.refs_1_, ...), custom_call_target="tpu_custom_call" | custom-call | bytes 2375680 | tf_op jit(solution)/shard_map/combine/pallas_call | solution.py:80
  143.5 3.3 %collective-permute-start.34 = (bf16[64,4096]{1,0:T(8,128)(2,1)S(1)}, bf16[64,4096]{1,0:T(8,128)(2,1)S(1)}, u32[]{:S(2)}, u32[]{:S(2)}) collective-permute-start(bf16[64,4096]{1,0:T(8,128)(2,1)S(1)} %combine.6), channel_id=1, source_target_pairs={{0,2},{1,3},{2,0},{3,1},{4,6},{5,7},{6,4},{7,5},{8,10},{9,11},{10,... | collective-permute-start | bytes 1572872 | tf_op jit(solution)/shard_map/ppermute | solution.py:17
  150.3 11.4 %collective-permute-done.33.refs_5_ = bf16[64,4096]{1,0:T(8,128)(2,1)S(1)} collective-permute-done((bf16[64,4096]{1,0:T(8,128)(2,1)S(1)}, bf16[64,4096]{1,0:T(8,128)(2,1)S(1)}, u32[]{:S(2)}, u32[]{:S(2)}) %collective-permute-start.33) | collective-permute-done | bytes 524320 | tf_op jit(solution)/shard_map/ppermute | solution.py:17
  161.6 6.6 %collective-permute-done.34.refs_6_ = bf16[64,4096]{1,0:T(8,128)(2,1)S(1)} collective-permute-done((bf16[64,4096]{1,0:T(8,128)(2,1)S(1)}, bf16[64,4096]{1,0:T(8,128)(2,1)S(1)}, u32[]{:S(2)}, u32[]{:S(2)}) %collective-permute-start.34) | collective-permute-done | bytes 524320 | tf_op jit(solution)/shard_map/ppermute | solution.py:17
  168.2 2.9 %combine.7 = bf16[64,4096]{1,0:T(8,128)(2,1)} custom-call(s32[3]{0:T(128)S(1)} %pad_add_fusion.place, bf16[64,4224]{1,0:T(8,128)(2,1)S(1)} %get-tuple-element.128.block, bf16[40,4096]{1,0:T(8,128)(2,1)S(1)} %get-tuple-element.116.refs_0_, bf16[40,4096]{1,0:T(8,128)(2,1)S(1)} %collective-permute-done.30.refs_1_, ...), custom_call_target="tpu_custom_call" | custom-call | bytes 3948544 | tf_op jit(solution)/shard_map/combine/pallas_call | solution.py:80
  (63 shorter events, 33.4 us)
Async XLA Ops:
  5.0 21.4 %collective-permute-start = (bf16[64,4224]{1,0:T(8,128)(2,1)S(1)}, bf16[64,4224]{1,0:T(8,128)(2,1)S(1)}, u32[]{:S(2)}, u32[]{:S(2)}) collective-permute-start(bf16[64,4224]{1,0:T(8,128)(2,1)S(1)} %get-tuple-element.128.block), channel_id=1, source_target_pairs={{0,2},{1,3},{2,0},{3,1},{4,6},{5,7},{6,4},{7,5},{8,10},{9,11},{10,... | collective-permute-start | bytes 1622024 | tf_op jit(solution)/shard_map/ppermute | solution.py:17
  7.5 18.9 %collective-permute-start.2 = (bf16[64,4224]{1,0:T(8,128)(2,1)S(1)}, bf16[64,4224]{1,0:T(8,128)(2,1)S(1)}, u32[]{:S(2)}, u32[]{:S(2)}) collective-permute-start(bf16[64,4224]{1,0:T(8,128)(2,1)S(1)} %get-tuple-element.128.block), channel_id=1, source_target_pairs={{2,4},{3,5},{4,2},{5,3},{10,12},{11,13},{12,10},{13,11},{18,20},{1... | collective-permute-start | bytes 1622024 | tf_op jit(solution)/shard_map/ppermute | solution.py:214
  8.2 10.6 %collective-permute-start.3 = (bf16[40,4096]{1,0:T(8,128)(2,1)S(1)}, bf16[40,4096]{1,0:T(8,128)(2,1)S(1)}, u32[]{:S(2)}, u32[]{:S(2)}) collective-permute-start(bf16[40,4096]{1,0:T(8,128)(2,1)S(1)} %get-tuple-element.72), channel_id=1, source_target_pairs={{0,8},{8,0},{16,24},{24,16},{1,9},{9,1},{17,25},{25,17},{2,10},{10... | collective-permute-start | bytes 983048 | tf_op jit(solution)/shard_map/ppermute | solution.py:17
  9.8 16.6 %collective-permute-start.4 = (bf16[40,4096]{1,0:T(8,128)(2,1)S(1)}, bf16[40,4096]{1,0:T(8,128)(2,1)S(1)}, u32[]{:S(2)}, u32[]{:S(2)}) collective-permute-start(bf16[40,4096]{1,0:T(8,128)(2,1)S(1)} %get-tuple-element.73), channel_id=1, source_target_pairs={{0,16},{8,24},{16,0},{24,8},{1,17},{9,25},{17,1},{25,9},{2,18},{10... | collective-permute-start | bytes 983048 | tf_op jit(solution)/shard_map/ppermute | solution.py:17
  11.3 15.1 %collective-permute-start.5 = (bf16[40,4096]{1,0:T(8,128)(2,1)S(1)}, bf16[40,4096]{1,0:T(8,128)(2,1)S(1)}, u32[]{:S(2)}, u32[]{:S(2)}) collective-permute-start(bf16[40,4096]{1,0:T(8,128)(2,1)S(1)} %get-tuple-element.74), channel_id=1, source_target_pairs={{0,24},{8,16},{16,8},{24,0},{1,25},{9,17},{17,9},{25,1},{2,26},{10... | collective-permute-start | bytes 983048 | tf_op jit(solution)/shard_map/ppermute | solution.py:17
  26.4 20.6 %collective-permute-start.7 = (bf16[64,4224]{1,0:T(8,128)(2,1)S(1)}, bf16[64,4224]{1,0:T(8,128)(2,1)S(1)}, u32[]{:S(2)}, u32[]{:S(2)}) collective-permute-start(bf16[64,4224]{1,0:T(8,128)(2,1)S(1)} %collective-permute-done.2.refs_0_), channel_id=1, source_target_pairs={{2,0},{3,1},{4,6},{5,7},{10,8},{11,9},{12,14},{13,15},{18,16},{19,... | collective-permute-start | bytes 1622024 | tf_op jit(solution)/shard_map/ppermute | solution.py:214
  27.7 19.3 %collective-permute-start.6 = (bf16[64,4224]{1,0:T(8,128)(2,1)S(1)}, bf16[64,4224]{1,0:T(8,128)(2,1)S(1)}, u32[]{:S(2)}, u32[]{:S(2)}) collective-permute-start(bf16[64,4224]{1,0:T(8,128)(2,1)S(1)} %collective-permute-done.refs_0_.block), channel_id=1, source_target_pairs={{2,4},{3,5},{4,2},{5,3},{10,12},{11,13},{12,10},{13,11},{18,20},{1... | collective-permute-start | bytes 1622024 | tf_op jit(solution)/shard_map/ppermute | solution.py:214
  29.9 10.7 %collective-permute-start.8 = (bf16[40,4096]{1,0:T(8,128)(2,1)S(1)}, bf16[40,4096]{1,0:T(8,128)(2,1)S(1)}, u32[]{:S(2)}, u32[]{:S(2)}) collective-permute-start(bf16[40,4096]{1,0:T(8,128)(2,1)S(1)} %get-tuple-element.77), channel_id=1, source_target_pairs={{0,8},{8,0},{16,24},{24,16},{1,9},{9,1},{17,25},{25,17},{2,10},{10... | collective-permute-start | bytes 983048 | tf_op jit(solution)/shard_map/ppermute | solution.py:17
  31.2 15.8 %collective-permute-start.9 = (bf16[40,4096]{1,0:T(8,128)(2,1)S(1)}, bf16[40,4096]{1,0:T(8,128)(2,1)S(1)}, u32[]{:S(2)}, u32[]{:S(2)}) collective-permute-start(bf16[40,4096]{1,0:T(8,128)(2,1)S(1)} %get-tuple-element.78), channel_id=1, source_target_pairs={{0,16},{8,24},{16,0},{24,8},{1,17},{9,25},{17,1},{25,9},{2,18},{10... | collective-permute-start | bytes 983048 | tf_op jit(solution)/shard_map/ppermute | solution.py:17
  32.0 15.0 %collective-permute-start.10 = (bf16[40,4096]{1,0:T(8,128)(2,1)S(1)}, bf16[40,4096]{1,0:T(8,128)(2,1)S(1)}, u32[]{:S(2)}, u32[]{:S(2)}) collective-permute-start(bf16[40,4096]{1,0:T(8,128)(2,1)S(1)} %get-tuple-element.79), channel_id=1, source_target_pairs={{0,24},{8,16},{16,8},{24,0},{1,25},{9,17},{17,9},{25,1},{2,26},{10... | collective-permute-start | bytes 983048 | tf_op jit(solution)/shard_map/ppermute | solution.py:17
  48.5 20.0 %collective-permute-start.12 = (bf16[4096,384]{1,0:T(8,128)(2,1)}, bf16[4096,384]{1,0:T(8,128)(2,1)S(1)}, u32[]{:S(2)}, u32[]{:S(2)}) collective-permute-start(bf16[4096,384]{1,0:T(8,128)(2,1)} %refs_5_.7), channel_id=1, source_target_pairs={{0,1},{1,0},{2,3},{3,2},{4,5},{5,4},{6,7},{7,6},{8,9},{9,8},{10,11... | collective-permute-start | bytes 9437192 | tf_op jit(solution)/shard_map/ppermute | solution.py:17
  48.5 19.9 %collective-permute-start.11 = (bf16[64,4224]{1,0:T(8,128)(2,1)S(1)}, bf16[64,4224]{1,0:T(8,128)(2,1)S(1)}, u32[]{:S(2)}, u32[]{:S(2)}) collective-permute-start(bf16[64,4224]{1,0:T(8,128)(2,1)S(1)} %get-tuple-element.117.block), channel_id=1, source_target_pairs={{2,0},{3,1},{4,6},{5,7},{10,8},{11,9},{12,14},{13,15},{18,16},{19,... | collective-permute-start | bytes 1622024 | tf_op jit(solution)/shard_map/ppermute | solution.py:214
  50.7 16.8 %collective-permute-start.14 = (bf16[40,4096]{1,0:T(8,128)(2,1)S(1)}, bf16[40,4096]{1,0:T(8,128)(2,1)S(1)}, u32[]{:S(2)}, u32[]{:S(2)}) collective-permute-start(bf16[40,4096]{1,0:T(8,128)(2,1)S(1)} %get-tuple-element.85), channel_id=1, source_target_pairs={{0,16},{8,24},{16,0},{24,8},{1,17},{9,25},{17,1},{25,9},{2,18},{10... | collective-permute-start | bytes 983048 | tf_op jit(solution)/shard_map/ppermute | solution.py:17
  52.1 15.4 %collective-permute-start.15 = (bf16[40,4096]{1,0:T(8,128)(2,1)S(1)}, bf16[40,4096]{1,0:T(8,128)(2,1)S(1)}, u32[]{:S(2)}, u32[]{:S(2)}) collective-permute-start(bf16[40,4096]{1,0:T(8,128)(2,1)S(1)} %get-tuple-element.86), channel_id=1, source_target_pairs={{0,24},{8,16},{16,8},{24,0},{1,25},{9,17},{17,9},{25,1},{2,26},{10... | collective-permute-start | bytes 983048 | tf_op jit(solution)/shard_map/ppermute | solution.py:17
  70.0 16.6 %collective-permute-start.17 = (bf16[40,4096]{1,0:T(8,128)(2,1)S(1)}, bf16[40,4096]{1,0:T(8,128)(2,1)S(1)}, u32[]{:S(2)}, u32[]{:S(2)}) collective-permute-start(bf16[40,4096]{1,0:T(8,128)(2,1)S(1)} %get-tuple-element.98), channel_id=1, source_target_pairs={{0,8},{8,0},{16,24},{24,16},{1,9},{9,1},{17,25},{25,17},{2,10},{10... | collective-permute-start | bytes 983048 | tf_op jit(solution)/shard_map/ppermute | solution.py:17
  70.7 16.8 %collective-permute-start.18 = (bf16[40,4096]{1,0:T(8,128)(2,1)S(1)}, bf16[40,4096]{1,0:T(8,128)(2,1)S(1)}, u32[]{:S(2)}, u32[]{:S(2)}) collective-permute-start(bf16[40,4096]{1,0:T(8,128)(2,1)S(1)} %get-tuple-element.99), channel_id=1, source_target_pairs={{0,16},{8,24},{16,0},{24,8},{1,17},{9,25},{17,1},{25,9},{2,18},{10... | collective-permute-start | bytes 983048 | tf_op jit(solution)/shard_map/ppermute | solution.py:17
  72.1 15.4 %collective-permute-start.19 = (bf16[40,4096]{1,0:T(8,128)(2,1)S(1)}, bf16[40,4096]{1,0:T(8,128)(2,1)S(1)}, u32[]{:S(2)}, u32[]{:S(2)}) collective-permute-start(bf16[40,4096]{1,0:T(8,128)(2,1)S(1)} %get-tuple-element.100), channel_id=1, source_target_pairs={{0,24},{8,16},{16,8},{24,0},{1,25},{9,17},{17,9},{25,1},{2,26},{10... | collective-permute-start | bytes 983048 | tf_op jit(solution)/shard_map/ppermute | solution.py:17
  94.4 12.7 %collective-permute-start.20 = (bf16[40,4096]{1,0:T(8,128)(2,1)S(1)}, bf16[40,4096]{1,0:T(8,128)(2,1)S(1)}, u32[]{:S(2)}, u32[]{:S(2)}) collective-permute-start(bf16[40,4096]{1,0:T(8,128)(2,1)S(1)} %get-tuple-element.102), channel_id=1, source_target_pairs={{0,8},{8,0},{16,24},{24,16},{1,9},{9,1},{17,25},{25,17},{2,10},{10... | collective-permute-start | bytes 983048 | tf_op jit(solution)/shard_map/ppermute | solution.py:17
  96.0 17.7 %collective-permute-start.21 = (bf16[40,4096]{1,0:T(8,128)(2,1)S(1)}, bf16[40,4096]{1,0:T(8,128)(2,1)S(1)}, u32[]{:S(2)}, u32[]{:S(2)}) collective-permute-start(bf16[40,4096]{1,0:T(8,128)(2,1)S(1)} %get-tuple-element.103), channel_id=1, source_target_pairs={{0,16},{8,24},{16,0},{24,8},{1,17},{9,25},{17,1},{25,9},{2,18},{10... | collective-permute-start | bytes 983048 | tf_op jit(solution)/shard_map/ppermute | solution.py:17
  96.5 17.1 %collective-permute-start.22 = (bf16[40,4096]{1,0:T(8,128)(2,1)S(1)}, bf16[40,4096]{1,0:T(8,128)(2,1)S(1)}, u32[]{:S(2)}, u32[]{:S(2)}) collective-permute-start(bf16[40,4096]{1,0:T(8,128)(2,1)S(1)} %get-tuple-element.104), channel_id=1, source_target_pairs={{0,24},{8,16},{16,8},{24,0},{1,25},{9,17},{17,9},{25,1},{2,26},{10... | collective-permute-start | bytes 983048 | tf_op jit(solution)/shard_map/ppermute | solution.py:17
  98.0 21.6 %collective-permute-start.23 = (bf16[40,4096]{1,0:T(8,128)(2,1)S(1)}, bf16[40,4096]{1,0:T(8,128)(2,1)S(1)}, u32[]{:S(2)}, u32[]{:S(2)}) collective-permute-start(bf16[40,4096]{1,0:T(8,128)(2,1)S(1)} %get-tuple-element.118), channel_id=1, source_target_pairs={{0,8},{8,0},{16,24},{24,16},{1,9},{9,1},{17,25},{25,17},{2,10},{10... | collective-permute-start | bytes 983048 | tf_op jit(solution)/shard_map/ppermute | solution.py:17
  99.4 26.6 %collective-permute-start.24 = (bf16[40,4096]{1,0:T(8,128)(2,1)S(1)}, bf16[40,4096]{1,0:T(8,128)(2,1)S(1)}, u32[]{:S(2)}, u32[]{:S(2)}) collective-permute-start(bf16[40,4096]{1,0:T(8,128)(2,1)S(1)} %get-tuple-element.119), channel_id=1, source_target_pairs={{0,16},{8,24},{16,0},{24,8},{1,17},{9,25},{17,1},{25,9},{2,18},{10... | collective-permute-start | bytes 983048 | tf_op jit(solution)/shard_map/ppermute | solution.py:17
  107.2 27.6 %collective-permute-start.25 = (bf16[40,4096]{1,0:T(8,128)(2,1)S(1)}, bf16[40,4096]{1,0:T(8,128)(2,1)S(1)}, u32[]{:S(2)}, u32[]{:S(2)}) collective-permute-start(bf16[40,4096]{1,0:T(8,128)(2,1)S(1)} %get-tuple-element.120), channel_id=1, source_target_pairs={{0,24},{8,16},{16,8},{24,0},{1,25},{9,17},{17,9},{25,1},{2,26},{10... | collective-permute-start | bytes 983048 | tf_op jit(solution)/shard_map/ppermute | solution.py:17
  115.7 31.0 %collective-permute-start.29 = (bf16[64,4096]{1,0:T(8,128)(2,1)S(1)}, bf16[64,4096]{1,0:T(8,128)(2,1)S(1)}, u32[]{:S(2)}, u32[]{:S(2)}) collective-permute-start(bf16[64,4096]{1,0:T(8,128)(2,1)S(1)} %combine.4), channel_id=1, source_target_pairs={{0,6},{1,7},{2,4},{3,5},{4,2},{5,3},{6,0},{7,1},{8,14},{9,15},{10,... | collective-permute-start | bytes 1572872 | tf_op jit(solution)/shard_map/ppermute | solution.py:17
  118.2 23.2 %collective-permute-start.26 = (bf16[40,4096]{1,0:T(8,128)(2,1)S(1)}, bf16[40,4096]{1,0:T(8,128)(2,1)S(1)}, u32[]{:S(2)}, u32[]{:S(2)}) collective-permute-start(bf16[40,4096]{1,0:T(8,128)(2,1)S(1)} %get-tuple-element.123), channel_id=1, source_target_pairs={{0,8},{8,0},{16,24},{24,16},{1,9},{9,1},{17,25},{25,17},{2,10},{10... | collective-permute-start | bytes 983048 | tf_op jit(solution)/shard_map/ppermute | solution.py:17
  119.6 21.7 %collective-permute-start.27 = (bf16[40,4096]{1,0:T(8,128)(2,1)S(1)}, bf16[40,4096]{1,0:T(8,128)(2,1)S(1)}, u32[]{:S(2)}, u32[]{:S(2)}) collective-permute-start(bf16[40,4096]{1,0:T(8,128)(2,1)S(1)} %get-tuple-element.125), channel_id=1, source_target_pairs={{0,16},{8,24},{16,0},{24,8},{1,17},{9,25},{17,1},{25,9},{2,18},{10... | collective-permute-start | bytes 983048 | tf_op jit(solution)/shard_map/ppermute | solution.py:17
  126.1 15.3 %collective-permute-start.28 = (bf16[40,4096]{1,0:T(8,128)(2,1)S(1)}, bf16[40,4096]{1,0:T(8,128)(2,1)S(1)}, u32[]{:S(2)}, u32[]{:S(2)}) collective-permute-start(bf16[40,4096]{1,0:T(8,128)(2,1)S(1)} %get-tuple-element.127), channel_id=1, source_target_pairs={{0,24},{8,16},{16,8},{24,0},{1,25},{9,17},{17,9},{25,1},{2,26},{10... | collective-permute-start | bytes 983048 | tf_op jit(solution)/shard_map/ppermute | solution.py:17
  136.9 24.7 %collective-permute-start.33 = (bf16[64,4096]{1,0:T(8,128)(2,1)S(1)}, bf16[64,4096]{1,0:T(8,128)(2,1)S(1)}, u32[]{:S(2)}, u32[]{:S(2)}) collective-permute-start(bf16[64,4096]{1,0:T(8,128)(2,1)S(1)} %combine.5), channel_id=1, source_target_pairs={{0,4},{1,5},{2,6},{3,7},{4,0},{5,1},{6,2},{7,3},{8,12},{9,13},{10,... | collective-permute-start | bytes 1572872 | tf_op jit(solution)/shard_map/ppermute | solution.py:17
  143.5 24.7 %collective-permute-start.34 = (bf16[64,4096]{1,0:T(8,128)(2,1)S(1)}, bf16[64,4096]{1,0:T(8,128)(2,1)S(1)}, u32[]{:S(2)}, u32[]{:S(2)}) collective-permute-start(bf16[64,4096]{1,0:T(8,128)(2,1)S(1)} %combine.6), channel_id=1, source_target_pairs={{0,2},{1,3},{2,0},{3,1},{4,6},{5,7},{6,4},{7,5},{8,10},{9,11},{10,... | collective-permute-start | bytes 1572872 | tf_op jit(solution)/shard_map/ppermute | solution.py:17
  146.8 21.4 %collective-permute-start.30 = (bf16[40,4096]{1,0:T(8,128)(2,1)S(1)}, bf16[40,4096]{1,0:T(8,128)(2,1)S(1)}, u32[]{:S(2)}, u32[]{:S(2)}) collective-permute-start(bf16[40,4096]{1,0:T(8,128)(2,1)S(1)} %get-tuple-element.130), channel_id=1, source_target_pairs={{0,8},{8,0},{16,24},{24,16},{1,9},{9,1},{17,25},{25,17},{2,10},{10... | collective-permute-start | bytes 983048 | tf_op jit(solution)/shard_map/ppermute | solution.py:17
  148.2 20.0 %collective-permute-start.31 = (bf16[40,4096]{1,0:T(8,128)(2,1)S(1)}, bf16[40,4096]{1,0:T(8,128)(2,1)S(1)}, u32[]{:S(2)}, u32[]{:S(2)}) collective-permute-start(bf16[40,4096]{1,0:T(8,128)(2,1)S(1)} %get-tuple-element.132), channel_id=1, source_target_pairs={{0,16},{8,24},{16,0},{24,8},{1,17},{9,25},{17,1},{25,9},{2,18},{10... | collective-permute-start | bytes 983048 | tf_op jit(solution)/shard_map/ppermute | solution.py:17
  148.8 19.4 %collective-permute-start.32 = (bf16[40,4096]{1,0:T(8,128)(2,1)S(1)}, bf16[40,4096]{1,0:T(8,128)(2,1)S(1)}, u32[]{:S(2)}, u32[]{:S(2)}) collective-permute-start(bf16[40,4096]{1,0:T(8,128)(2,1)S(1)} %get-tuple-element.134), channel_id=1, source_target_pairs={{0,24},{8,16},{16,8},{24,0},{1,25},{9,17},{17,9},{25,1},{2,26},{10... | collective-permute-start | bytes 983048 | tf_op jit(solution)/shard_map/ppermute | solution.py:17
  (9 other events, 106.3 us)

commit v5 on v4

--- a/solution.py
+++ b/solution.py
@@ -29,8 +29,8 @@
 
 
 def meta_of(ids, gates):
-    parts = [ids[...].astype(jnp.float32)]
-    rest = gates[...]
+    parts = [ids]
+    rest = gates
     for _ in range(3):
         piece = rest.astype(jnp.bfloat16).astype(jnp.float32)
         parts.append(piece)
@@ -101,20 +101,19 @@
         out[...] = rows.astype(jnp.bfloat16)
 
 
-def first_kernel(top, chain, capacity, place, tokens_from, ids_from, gates_from, packed, *refs):
-    outs, (tokens, ids, gates, sems) = refs[:-4], refs[-4:]
+def first_kernel(top, chain, capacity, place, tokens_from, routing_from, packed, *refs):
+    outs, (tokens, routing, sems) = refs[:-3], refs[-3:]
     copies = [
         pltpu.make_async_copy(source, target, sems.at[i])
-        for i, (source, target) in enumerate(((ids_from, ids), (gates_from, gates), (tokens_from, tokens)))
+        for i, (source, target) in enumerate(((routing_from, routing), (tokens_from, tokens)))
     ]
     for copy in copies:
         copy.start()
     copies[0].wait()
+    width = tokens.shape[1]
+    meta = meta_of(routing[:top], routing[top:])
+    packed[:, width:] = meta.astype(jnp.bfloat16)
     copies[1].wait()
-    width = tokens.shape[1]
-    meta = meta_of(ids, gates)
-    packed[:, width:] = meta.astype(jnp.bfloat16)
-    copies[2].wait()
     packed[:, :width] = tokens[...]
     pick(top, chain, capacity, place, meta, tokens[...], outs)
 
@@ -218,15 +217,14 @@
         functools.partial(first_kernel, *sizes),
         "first",
         place,
-        [tokens, expert_ids.T, gate_weights.T],
+        [tokens, jnp.concatenate([expert_ids.T.astype(jnp.float32), gate_weights.T], axis=0)],
         [array(rows, width + LANES)] + [array(capacity, width)] * nodes,
         [
             pltpu.VMEM((rows, width), tokens.dtype),
-            pltpu.VMEM((top, rows), expert_ids.dtype),
-            pltpu.VMEM((top, rows), gate_weights.dtype),
-            pltpu.SemaphoreType.DMA((3,)),
+            pltpu.VMEM((2 * top, rows), jnp.float32),
+            pltpu.SemaphoreType.DMA((2,)),
         ],
-        stay=3,
+        stay=2,
     )
     arrived = {0: send(picked)}
     own = (w_gate, w_up, w_down)

time: 171 us -> 171 us (level)
    unnamed x12 -> x8, local copies, waits for them, and re-layouts: 6.46 us -> 4.82 us
  transfers between devices with their start and end apart: 35 -> 35, of which waited for: 13 -> 13; matrix products, arithmetic and copies ran while one was open for 0% -> 1% of each run, Pallas kernels for 18% -> 18%
where the time goes in v5:
time: 171 us
  waiting for transfers between devices  74.4 us (44%)
  starting transfers between devices  46.3 us (27%)
  Pallas kernels  43.7 us (26%)
  local copies, waits for them, and re-layouts  4.82 us (3%)
  other arithmetic  1.72 us (1%)
    ppermute x31, waiting for transfers between devices, swap(): return lax.ppermute(value, axis, pairs)  73.4 us
    pallas_call x12, Pallas kernels, call(): pl.pallas_call(kernel, out_shape=outs, in_specs=[smem()] + [vmem()] * (le...  43.7 us
    ppermute x31, starting transfers between devices, swap(): return lax.ppermute(value, axis, pairs)  42.1 us
    unnamed x8, local copies, waits for them, and re-layouts  4.82 us
    ppermute x4, starting transfers between devices, per_device(): hop = lambda value, pairs: lax.ppermute(value, 'local', chain_pairs(pairs))  4.14 us
  transfers between devices with their start and end apart: 35, of which 13 were waited for; matrix products, arithmetic and copies ran while one was open for 1% of the time, Pallas kernels for 18%

profile of v5, /device:TPU:0, one launch (start us, length us, event | category | flops | bytes accessed | tf_op | source)
XLA Modules:
  0.0 171.2 jit_solution(16766034943986206548)
XLA Ops:
  3.2 1.7 %first.1 = (bf16[64,4224]{1,0:T(8,128)(2,1)S(1)}, bf16[40,4096]{1,0:T(8,128)(2,1)S(1)}, bf16[40,4096]{1,0:T(8,128)(2,1)S(1)}, bf16[40,4096]{1,0:T(8,128)(2,1)S(1)}, bf16[40,4096]{1,0:T(8,128)(2,1)S(1)}) custom-call(s32[3]{0:T(128)S(1)} %pad_add_fusion.place, bf16[64,4096]{1,0:T(8,128)(2,1)S(1)} %copy-done.3, f32[16,64]{1,0:T(8,128)S(1)} %pad_maximum_fusion.routing_from), custom_call_target="tpu_custom_call" | custom-call | bytes 2377728 | tf_op jit(solution)/shard_map/first/pallas_call | solution.py:80
  5.0 2.6 %collective-permute-start = (bf16[64,4224]{1,0:T(8,128)(2,1)S(1)}, bf16[64,4224]{1,0:T(8,128)(2,1)S(1)}, u32[]{:S(2)}, u32[]{:S(2)}) collective-permute-start(bf16[64,4224]{1,0:T(8,128)(2,1)S(1)} %get-tuple-element.128.block), channel_id=1, source_target_pairs={{0,2},{1,3},{2,0},{3,1},{4,6},{5,7},{6,4},{7,5},{8,10},{9,11},{10,... | collective-permute-start | bytes 1622024 | tf_op jit(solution)/shard_map/ppermute | solution.py:17
  8.2 1.5 collective-permute-start.3
  9.8 1.5 collective-permute-start.4
  11.8 7.1 %collective-permute-done.3.refs_1_ = bf16[40,4096]{1,0:T(8,128)(2,1)S(1)} collective-permute-done((bf16[40,4096]{1,0:T(8,128)(2,1)S(1)}, bf16[40,4096]{1,0:T(8,128)(2,1)S(1)}, u32[]{:S(2)}, u32[]{:S(2)}) %collective-permute-start.3) | collective-permute-done | bytes 327712 | tf_op jit(solution)/shard_map/ppermute | solution.py:17
  18.9 7.5 %collective-permute-done.4.refs_2_ = bf16[40,4096]{1,0:T(8,128)(2,1)S(1)} collective-permute-done((bf16[40,4096]{1,0:T(8,128)(2,1)S(1)}, bf16[40,4096]{1,0:T(8,128)(2,1)S(1)}, u32[]{:S(2)}, u32[]{:S(2)}) %collective-permute-start.4) | collective-permute-done | bytes 327712 | tf_op jit(solution)/shard_map/ppermute | solution.py:17
  33.4 7.2 %collective-permute-done.8.refs_1_ = bf16[40,4096]{1,0:T(8,128)(2,1)S(1)} collective-permute-done((bf16[40,4096]{1,0:T(8,128)(2,1)S(1)}, bf16[40,4096]{1,0:T(8,128)(2,1)S(1)}, u32[]{:S(2)}, u32[]{:S(2)}) %collective-permute-start.8) | collective-permute-done | bytes 327712 | tf_op jit(solution)/shard_map/ppermute | solution.py:17
  40.6 6.3 %collective-permute-done.9.refs_2_ = bf16[40,4096]{1,0:T(8,128)(2,1)S(1)} collective-permute-done((bf16[40,4096]{1,0:T(8,128)(2,1)S(1)}, bf16[40,4096]{1,0:T(8,128)(2,1)S(1)}, u32[]{:S(2)}, u32[]{:S(2)}) %collective-permute-start.9) | collective-permute-done | bytes 327712 | tf_op jit(solution)/shard_map/ppermute | solution.py:17
  53.5 7.0 %collective-permute-done.13.refs_1_ = bf16[40,4096]{1,0:T(8,128)(2,1)S(1)} collective-permute-done((bf16[40,4096]{1,0:T(8,128)(2,1)S(1)}, bf16[40,4096]{1,0:T(8,128)(2,1)S(1)}, u32[]{:S(2)}, u32[]{:S(2)}) %collective-permute-start.13) | collective-permute-done | bytes 327712 | tf_op jit(solution)/shard_map/ppermute | solution.py:17
  60.5 7.0 %collective-permute-done.14.refs_2_ = bf16[40,4096]{1,0:T(8,128)(2,1)S(1)} collective-permute-done((bf16[40,4096]{1,0:T(8,128)(2,1)S(1)}, bf16[40,4096]{1,0:T(8,128)(2,1)S(1)}, u32[]{:S(2)}, u32[]{:S(2)}) %collective-permute-start.14) | collective-permute-done | bytes 327712 | tf_op jit(solution)/shard_map/ppermute | solution.py:17
  73.6 2.3 %collective-permute-done.16.refs_9_ = bf16[384,4096]{1,0:T(8,128)(2,1)S(1)} collective-permute-done((bf16[384,4096]{1,0:T(8,128)(2,1)}, bf16[384,4096]{1,0:T(8,128)(2,1)S(1)}, u32[]{:S(2)}, u32[]{:S(2)}) %collective-permute-start.16) | collective-permute-done | bytes 3145760 | tf_op jit(solution)/shard_map/ppermute | solution.py:17
  75.9 1.9 %copy-done.1 = bf16[4096,384]{1,0:T(8,128)(2,1)S(1)} copy-done((bf16[4096,384]{1,0:T(8,128)(2,1)S(1)}, bf16[4096,384]{1,0:T(8,128)(2,1)}, u32[]{:S(2)}) %copy-start.1) | copy-done | bytes 3145752
  77.8 1.9 %copy-done.2 = bf16[384,4096]{1,0:T(8,128)(2,1)S(1)} copy-done((bf16[384,4096]{1,0:T(8,128)(2,1)S(1)}, bf16[384,4096]{1,0:T(8,128)(2,1)}, u32[]{:S(2)}) %copy-start.2) | copy-done | bytes 3145752
  79.6 6.9 %expert.4 = (bf16[40,4096]{1,0:T(8,128)(2,1)S(1)}, bf16[40,4096]{1,0:T(8,128)(2,1)S(1)}, bf16[40,4096]{1,0:T(8,128)(2,1)S(1)}, bf16[40,4096]{1,0:T(8,128)(2,1)S(1)}) custom-call(s32[3]{0:T(128)S(1)} %pad_add_fusion.place, bf16[40,4096]{1,0:T(8,128)(2,1)S(1)} %get-tuple-element.90.refs_0_, bf16[40,4096]{1,0:T(8,128)(2,1)S(1)} %collective-permute-done.13.refs_1_, ...), custom_call_target="tpu_custom_call" | custom-call | flops 3019898880 | bytes 21495808 | tf_op jit(solution)/shard_map/expert/pallas_call | solution.py:80
  87.5 7.0 %expert.5 = (bf16[40,4096]{1,0:T(8,128)(2,1)S(1)}, bf16[40,4096]{1,0:T(8,128)(2,1)S(1)}, bf16[40,4096]{1,0:T(8,128)(2,1)S(1)}, bf16[40,4096]{1,0:T(8,128)(2,1)S(1)}) custom-call(s32[3]{0:T(128)S(1)} %pad_add_fusion.place, bf16[40,4096]{1,0:T(8,128)(2,1)S(1)} %get-tuple-element.97.refs_0_, bf16[40,4096]{1,0:T(8,128)(2,1)S(1)} %collective-permute-done.17.refs_1_, ...), custom_call_target="tpu_custom_call" | custom-call | flops 3019898880 | bytes 21495808 | tf_op jit(solution)/shard_map/expert/pallas_call | solution.py:80
  94.4 1.5 collective-permute-start.20
  96.5 1.5 collective-permute-start.22
  100.0 7.2 %expert.6 = (bf16[40,4096]{1,0:T(8,128)(2,1)S(1)}, bf16[40,4096]{1,0:T(8,128)(2,1)S(1)}, bf16[40,4096]{1,0:T(8,128)(2,1)S(1)}, bf16[40,4096]{1,0:T(8,128)(2,1)S(1)}) custom-call(s32[3]{0:T(128)S(1)} %pad_add_fusion.place, bf16[40,4096]{1,0:T(8,128)(2,1)S(1)} %get-tuple-element.107.refs_0_, bf16[40,4096]{1,0:T(8,128)(2,1)S(1)} %collective-permute-done.8.refs_1_, ...), custom_call_target="tpu_custom_call" | custom-call | flops 3019898880 | bytes 21495808 | tf_op jit(solution)/shard_map/expert/pallas_call | solution.py:80
  107.2 1.6 collective-permute-start.25
  108.8 4.8 %collective-permute-done.21.refs_2_ = bf16[40,4096]{1,0:T(8,128)(2,1)S(1)} collective-permute-done((bf16[40,4096]{1,0:T(8,128)(2,1)S(1)}, bf16[40,4096]{1,0:T(8,128)(2,1)S(1)}, u32[]{:S(2)}, u32[]{:S(2)}) %collective-permute-start.21) | collective-permute-done | bytes 327712 | tf_op jit(solution)/shard_map/ppermute | solution.py:17
  113.6 2.1 %combine.4 = bf16[64,4096]{1,0:T(8,128)(2,1)S(1)} custom-call(s32[3]{0:T(128)S(1)} %pad_add_fusion.place, bf16[64,4224]{1,0:T(8,128)(2,1)S(1)} %get-tuple-element.88.block, bf16[40,4096]{1,0:T(8,128)(2,1)S(1)} %get-tuple-element.101.refs_0_, bf16[40,4096]{1,0:T(8,128)(2,1)S(1)} %collective-permute-done.20.refs_1_, ...), custom_call_target="tpu_custom_call" | custom-call | bytes 2375680 | tf_op jit(solution)/shard_map/combine/pallas_call | solution.py:80
  115.7 2.4 %collective-permute-start.29 = (bf16[64,4096]{1,0:T(8,128)(2,1)S(1)}, bf16[64,4096]{1,0:T(8,128)(2,1)S(1)}, u32[]{:S(2)}, u32[]{:S(2)}) collective-permute-start(bf16[64,4096]{1,0:T(8,128)(2,1)S(1)} %combine.4), channel_id=1, source_target_pairs={{0,6},{1,7},{2,4},{3,5},{4,2},{5,3},{6,0},{7,1},{8,14},{9,15},{10,... | collective-permute-start | bytes 1572872 | tf_op jit(solution)/shard_map/ppermute | solution.py:17
  120.6 5.4 %collective-permute-done.24.refs_2_ = bf16[40,4096]{1,0:T(8,128)(2,1)S(1)} collective-permute-done((bf16[40,4096]{1,0:T(8,128)(2,1)S(1)}, bf16[40,4096]{1,0:T(8,128)(2,1)S(1)}, u32[]{:S(2)}, u32[]{:S(2)}) %collective-permute-start.24) | collective-permute-done | bytes 327712 | tf_op jit(solution)/shard_map/ppermute | solution.py:17
  126.1 1.5 collective-permute-start.28
  127.6 7.2 %expert.7 = (bf16[40,4096]{1,0:T(8,128)(2,1)S(1)}, bf16[40,4096]{1,0:T(8,128)(2,1)S(1)}, bf16[40,4096]{1,0:T(8,128)(2,1)S(1)}, bf16[40,4096]{1,0:T(8,128)(2,1)S(1)}) custom-call(s32[3]{0:T(128)S(1)} %pad_add_fusion.place, bf16[40,4096]{1,0:T(8,128)(2,1)S(1)} %get-tuple-element.112.refs_0_, bf16[40,4096]{1,0:T(8,128)(2,1)S(1)} %collective-permute-done.3.refs_1_, ...), custom_call_target="tpu_custom_call" | custom-call | flops 3019898880 | bytes 21495808 | tf_op jit(solution)/shard_map/expert/pallas_call | solution.py:80
  134.8 2.1 %combine.5 = bf16[64,4096]{1,0:T(8,128)(2,1)S(1)} custom-call(s32[3]{0:T(128)S(1)} %pad_add_fusion.place, bf16[64,4224]{1,0:T(8,128)(2,1)S(1)} %get-tuple-element.117.block, bf16[40,4096]{1,0:T(8,128)(2,1)S(1)} %get-tuple-element.96.refs_0_, bf16[40,4096]{1,0:T(8,128)(2,1)S(1)} %collective-permute-done.23.refs_1_, ...), custom_call_target="tpu_custom_call" | custom-call | bytes 2375680 | tf_op jit(solution)/shard_map/combine/pallas_call | solution.py:80
  136.9 4.1 %collective-permute-start.33 = (bf16[64,4096]{1,0:T(8,128)(2,1)S(1)}, bf16[64,4096]{1,0:T(8,128)(2,1)S(1)}, u32[]{:S(2)}, u32[]{:S(2)}) collective-permute-start(bf16[64,4096]{1,0:T(8,128)(2,1)S(1)} %combine.5), channel_id=1, source_target_pairs={{0,4},{1,5},{2,6},{3,7},{4,0},{5,1},{6,2},{7,3},{8,12},{9,13},{10,... | collective-permute-start | bytes 1572872 | tf_op jit(solution)/shard_map/ppermute | solution.py:17
  141.1 2.1 %combine.6 = bf16[64,4096]{1,0:T(8,128)(2,1)S(1)} custom-call(s32[3]{0:T(128)S(1)} %pad_add_fusion.place, bf16[64,4224]{1,0:T(8,128)(2,1)S(1)} %collective-permute-done.refs_0_.block, bf16[40,4096]{1,0:T(8,128)(2,1)S(1)} %get-tuple-element.111.refs_0_, bf16[40,4096]{1,0:T(8,128)(2,1)S(1)} %collective-permute-done.26.refs_1_, ...), custom_call_target="tpu_custom_call" | custom-call | bytes 2375680 | tf_op jit(solution)/shard_map/combine/pallas_call | solution.py:80
  143.2 3.6 %collective-permute-start.34 = (bf16[64,4096]{1,0:T(8,128)(2,1)S(1)}, bf16[64,4096]{1,0:T(8,128)(2,1)S(1)}, u32[]{:S(2)}, u32[]{:S(2)}) collective-permute-start(bf16[64,4096]{1,0:T(8,128)(2,1)S(1)} %combine.6), channel_id=1, source_target_pairs={{0,2},{1,3},{2,0},{3,1},{4,6},{5,7},{6,4},{7,5},{8,10},{9,11},{10,... | collective-permute-start | bytes 1572872 | tf_op jit(solution)/shard_map/ppermute | solution.py:17
  150.3 11.4 %collective-permute-done.33.refs_5_ = bf16[64,4096]{1,0:T(8,128)(2,1)S(1)} collective-permute-done((bf16[64,4096]{1,0:T(8,128)(2,1)S(1)}, bf16[64,4096]{1,0:T(8,128)(2,1)S(1)}, u32[]{:S(2)}, u32[]{:S(2)}) %collective-permute-start.33) | collective-permute-done | bytes 524320 | tf_op jit(solution)/shard_map/ppermute | solution.py:17
  161.6 6.6 %collective-permute-done.34.refs_6_ = bf16[64,4096]{1,0:T(8,128)(2,1)S(1)} collective-permute-done((bf16[64,4096]{1,0:T(8,128)(2,1)S(1)}, bf16[64,4096]{1,0:T(8,128)(2,1)S(1)}, u32[]{:S(2)}, u32[]{:S(2)}) %collective-permute-start.34) | collective-permute-done | bytes 524320 | tf_op jit(solution)/shard_map/ppermute | solution.py:17
  168.2 2.9 %combine.7 = bf16[64,4096]{1,0:T(8,128)(2,1)} custom-call(s32[3]{0:T(128)S(1)} %pad_add_fusion.place, bf16[64,4224]{1,0:T(8,128)(2,1)S(1)} %get-tuple-element.128.block, bf16[40,4096]{1,0:T(8,128)(2,1)S(1)} %get-tuple-element.116.refs_0_, bf16[40,4096]{1,0:T(8,128)(2,1)S(1)} %collective-permute-done.30.refs_1_, ...), custom_call_target="tpu_custom_call" | custom-call | bytes 3948544 | tf_op jit(solution)/shard_map/combine/pallas_call | solution.py:80
  (61 shorter events, 33.4 us)
Async XLA Ops:
  5.0 21.4 %collective-permute-start = (bf16[64,4224]{1,0:T(8,128)(2,1)S(1)}, bf16[64,4224]{1,0:T(8,128)(2,1)S(1)}, u32[]{:S(2)}, u32[]{:S(2)}) collective-permute-start(bf16[64,4224]{1,0:T(8,128)(2,1)S(1)} %get-tuple-element.128.block), channel_id=1, source_target_pairs={{0,2},{1,3},{2,0},{3,1},{4,6},{5,7},{6,4},{7,5},{8,10},{9,11},{10,... | collective-permute-start | bytes 1622024 | tf_op jit(solution)/shard_map/ppermute | solution.py:17
  7.6 18.8 %collective-permute-start.2 = (bf16[64,4224]{1,0:T(8,128)(2,1)S(1)}, bf16[64,4224]{1,0:T(8,128)(2,1)S(1)}, u32[]{:S(2)}, u32[]{:S(2)}) collective-permute-start(bf16[64,4224]{1,0:T(8,128)(2,1)S(1)} %get-tuple-element.128.block), channel_id=1, source_target_pairs={{2,4},{3,5},{4,2},{5,3},{10,12},{11,13},{12,10},{13,11},{18,20},{1... | collective-permute-start | bytes 1622024 | tf_op jit(solution)/shard_map/ppermute | solution.py:213
  8.2 10.6 %collective-permute-start.3 = (bf16[40,4096]{1,0:T(8,128)(2,1)S(1)}, bf16[40,4096]{1,0:T(8,128)(2,1)S(1)}, u32[]{:S(2)}, u32[]{:S(2)}) collective-permute-start(bf16[40,4096]{1,0:T(8,128)(2,1)S(1)} %get-tuple-element.72), channel_id=1, source_target_pairs={{0,8},{8,0},{16,24},{24,16},{1,9},{9,1},{17,25},{25,17},{2,10},{10... | collective-permute-start | bytes 983048 | tf_op jit(solution)/shard_map/ppermute | solution.py:17
  9.8 16.6 %collective-permute-start.4 = (bf16[40,4096]{1,0:T(8,128)(2,1)S(1)}, bf16[40,4096]{1,0:T(8,128)(2,1)S(1)}, u32[]{:S(2)}, u32[]{:S(2)}) collective-permute-start(bf16[40,4096]{1,0:T(8,128)(2,1)S(1)} %get-tuple-element.73), channel_id=1, source_target_pairs={{0,16},{8,24},{16,0},{24,8},{1,17},{9,25},{17,1},{25,9},{2,18},{10... | collective-permute-start | bytes 983048 | tf_op jit(solution)/shard_map/ppermute | solution.py:17
  11.3 15.1 %collective-permute-start.5 = (bf16[40,4096]{1,0:T(8,128)(2,1)S(1)}, bf16[40,4096]{1,0:T(8,128)(2,1)S(1)}, u32[]{:S(2)}, u32[]{:S(2)}) collective-permute-start(bf16[40,4096]{1,0:T(8,128)(2,1)S(1)} %get-tuple-element.74), channel_id=1, source_target_pairs={{0,24},{8,16},{16,8},{24,0},{1,25},{9,17},{17,9},{25,1},{2,26},{10... | collective-permute-start | bytes 983048 | tf_op jit(solution)/shard_map/ppermute | solution.py:17
  26.4 20.5 %collective-permute-start.7 = (bf16[64,4224]{1,0:T(8,128)(2,1)S(1)}, bf16[64,4224]{1,0:T(8,128)(2,1)S(1)}, u32[]{:S(2)}, u32[]{:S(2)}) collective-permute-start(bf16[64,4224]{1,0:T(8,128)(2,1)S(1)} %collective-permute-done.2.refs_0_), channel_id=1, source_target_pairs={{2,0},{3,1},{4,6},{5,7},{10,8},{11,9},{12,14},{13,15},{18,16},{19,... | collective-permute-start | bytes 1622024 | tf_op jit(solution)/shard_map/ppermute | solution.py:213
  27.7 19.2 %collective-permute-start.6 = (bf16[64,4224]{1,0:T(8,128)(2,1)S(1)}, bf16[64,4224]{1,0:T(8,128)(2,1)S(1)}, u32[]{:S(2)}, u32[]{:S(2)}) collective-permute-start(bf16[64,4224]{1,0:T(8,128)(2,1)S(1)} %collective-permute-done.refs_0_.block), channel_id=1, source_target_pairs={{2,4},{3,5},{4,2},{5,3},{10,12},{11,13},{12,10},{13,11},{18,20},{1... | collective-permute-start | bytes 1622024 | tf_op jit(solution)/shard_map/ppermute | solution.py:213
  29.9 10.7 %collective-permute-start.8 = (bf16[40,4096]{1,0:T(8,128)(2,1)S(1)}, bf16[40,4096]{1,0:T(8,128)(2,1)S(1)}, u32[]{:S(2)}, u32[]{:S(2)}) collective-permute-start(bf16[40,4096]{1,0:T(8,128)(2,1)S(1)} %get-tuple-element.77), channel_id=1, source_target_pairs={{0,8},{8,0},{16,24},{24,16},{1,9},{9,1},{17,25},{25,17},{2,10},{10... | collective-permute-start | bytes 983048 | tf_op jit(solution)/shard_map/ppermute | solution.py:17
  31.1 15.8 %collective-permute-start.9 = (bf16[40,4096]{1,0:T(8,128)(2,1)S(1)}, bf16[40,4096]{1,0:T(8,128)(2,1)S(1)}, u32[]{:S(2)}, u32[]{:S(2)}) collective-permute-start(bf16[40,4096]{1,0:T(8,128)(2,1)S(1)} %get-tuple-element.78), channel_id=1, source_target_pairs={{0,16},{8,24},{16,0},{24,8},{1,17},{9,25},{17,1},{25,9},{2,18},{10... | collective-permute-start | bytes 983048 | tf_op jit(solution)/shard_map/ppermute | solution.py:17
  32.0 14.9 %collective-permute-start.10 = (bf16[40,4096]{1,0:T(8,128)(2,1)S(1)}, bf16[40,4096]{1,0:T(8,128)(2,1)S(1)}, u32[]{:S(2)}, u32[]{:S(2)}) collective-permute-start(bf16[40,4096]{1,0:T(8,128)(2,1)S(1)} %get-tuple-element.79), channel_id=1, source_target_pairs={{0,24},{8,16},{16,8},{24,0},{1,25},{9,17},{17,9},{25,1},{2,26},{10... | collective-permute-start | bytes 983048 | tf_op jit(solution)/shard_map/ppermute | solution.py:17
  48.4 20.0 %collective-permute-start.12 = (bf16[4096,384]{1,0:T(8,128)(2,1)}, bf16[4096,384]{1,0:T(8,128)(2,1)S(1)}, u32[]{:S(2)}, u32[]{:S(2)}) collective-permute-start(bf16[4096,384]{1,0:T(8,128)(2,1)} %refs_5_.7), channel_id=1, source_target_pairs={{0,1},{1,0},{2,3},{3,2},{4,5},{5,4},{6,7},{7,6},{8,9},{9,8},{10,11... | collective-permute-start | bytes 9437192 | tf_op jit(solution)/shard_map/ppermute | solution.py:17
  48.5 20.0 %collective-permute-start.11 = (bf16[64,4224]{1,0:T(8,128)(2,1)S(1)}, bf16[64,4224]{1,0:T(8,128)(2,1)S(1)}, u32[]{:S(2)}, u32[]{:S(2)}) collective-permute-start(bf16[64,4224]{1,0:T(8,128)(2,1)S(1)} %get-tuple-element.117.block), channel_id=1, source_target_pairs={{2,0},{3,1},{4,6},{5,7},{10,8},{11,9},{12,14},{13,15},{18,16},{19,... | collective-permute-start | bytes 1622024 | tf_op jit(solution)/shard_map/ppermute | solution.py:213
  50.6 16.8 %collective-permute-start.14 = (bf16[40,4096]{1,0:T(8,128)(2,1)S(1)}, bf16[40,4096]{1,0:T(8,128)(2,1)S(1)}, u32[]{:S(2)}, u32[]{:S(2)}) collective-permute-start(bf16[40,4096]{1,0:T(8,128)(2,1)S(1)} %get-tuple-element.85), channel_id=1, source_target_pairs={{0,16},{8,24},{16,0},{24,8},{1,17},{9,25},{17,1},{25,9},{2,18},{10... | collective-permute-start | bytes 983048 | tf_op jit(solution)/shard_map/ppermute | solution.py:17
  52.1 15.4 %collective-permute-start.15 = (bf16[40,4096]{1,0:T(8,128)(2,1)S(1)}, bf16[40,4096]{1,0:T(8,128)(2,1)S(1)}, u32[]{:S(2)}, u32[]{:S(2)}) collective-permute-start(bf16[40,4096]{1,0:T(8,128)(2,1)S(1)} %get-tuple-element.86), channel_id=1, source_target_pairs={{0,24},{8,16},{16,8},{24,0},{1,25},{9,17},{17,9},{25,1},{2,26},{10... | collective-permute-start | bytes 983048 | tf_op jit(solution)/shard_map/ppermute | solution.py:17
  70.0 16.6 %collective-permute-start.17 = (bf16[40,4096]{1,0:T(8,128)(2,1)S(1)}, bf16[40,4096]{1,0:T(8,128)(2,1)S(1)}, u32[]{:S(2)}, u32[]{:S(2)}) collective-permute-start(bf16[40,4096]{1,0:T(8,128)(2,1)S(1)} %get-tuple-element.98), channel_id=1, source_target_pairs={{0,8},{8,0},{16,24},{24,16},{1,9},{9,1},{17,25},{25,17},{2,10},{10... | collective-permute-start | bytes 983048 | tf_op jit(solution)/shard_map/ppermute | solution.py:17
  70.7 16.8 %collective-permute-start.18 = (bf16[40,4096]{1,0:T(8,128)(2,1)S(1)}, bf16[40,4096]{1,0:T(8,128)(2,1)S(1)}, u32[]{:S(2)}, u32[]{:S(2)}) collective-permute-start(bf16[40,4096]{1,0:T(8,128)(2,1)S(1)} %get-tuple-element.99), channel_id=1, source_target_pairs={{0,16},{8,24},{16,0},{24,8},{1,17},{9,25},{17,1},{25,9},{2,18},{10... | collective-permute-start | bytes 983048 | tf_op jit(solution)/shard_map/ppermute | solution.py:17
  72.1 15.4 %collective-permute-start.19 = (bf16[40,4096]{1,0:T(8,128)(2,1)S(1)}, bf16[40,4096]{1,0:T(8,128)(2,1)S(1)}, u32[]{:S(2)}, u32[]{:S(2)}) collective-permute-start(bf16[40,4096]{1,0:T(8,128)(2,1)S(1)} %get-tuple-element.100), channel_id=1, source_target_pairs={{0,24},{8,16},{16,8},{24,0},{1,25},{9,17},{17,9},{25,1},{2,26},{10... | collective-permute-start | bytes 983048 | tf_op jit(solution)/shard_map/ppermute | solution.py:17
  94.4 12.7 %collective-permute-start.20 = (bf16[40,4096]{1,0:T(8,128)(2,1)S(1)}, bf16[40,4096]{1,0:T(8,128)(2,1)S(1)}, u32[]{:S(2)}, u32[]{:S(2)}) collective-permute-start(bf16[40,4096]{1,0:T(8,128)(2,1)S(1)} %get-tuple-element.102), channel_id=1, source_target_pairs={{0,8},{8,0},{16,24},{24,16},{1,9},{9,1},{17,25},{25,17},{2,10},{10... | collective-permute-start | bytes 983048 | tf_op jit(solution)/shard_map/ppermute | solution.py:17
  96.0 17.7 %collective-permute-start.21 = (bf16[40,4096]{1,0:T(8,128)(2,1)S(1)}, bf16[40,4096]{1,0:T(8,128)(2,1)S(1)}, u32[]{:S(2)}, u32[]{:S(2)}) collective-permute-start(bf16[40,4096]{1,0:T(8,128)(2,1)S(1)} %get-tuple-element.103), channel_id=1, source_target_pairs={{0,16},{8,24},{16,0},{24,8},{1,17},{9,25},{17,1},{25,9},{2,18},{10... | collective-permute-start | bytes 983048 | tf_op jit(solution)/shard_map/ppermute | solution.py:17
  96.5 17.1 %collective-permute-start.22 = (bf16[40,4096]{1,0:T(8,128)(2,1)S(1)}, bf16[40,4096]{1,0:T(8,128)(2,1)S(1)}, u32[]{:S(2)}, u32[]{:S(2)}) collective-permute-start(bf16[40,4096]{1,0:T(8,128)(2,1)S(1)} %get-tuple-element.104), channel_id=1, source_target_pairs={{0,24},{8,16},{16,8},{24,0},{1,25},{9,17},{17,9},{25,1},{2,26},{10... | collective-permute-start | bytes 983048 | tf_op jit(solution)/shard_map/ppermute | solution.py:17
  98.0 21.6 %collective-permute-start.23 = (bf16[40,4096]{1,0:T(8,128)(2,1)S(1)}, bf16[40,4096]{1,0:T(8,128)(2,1)S(1)}, u32[]{:S(2)}, u32[]{:S(2)}) collective-permute-start(bf16[40,4096]{1,0:T(8,128)(2,1)S(1)} %get-tuple-element.118), channel_id=1, source_target_pairs={{0,8},{8,0},{16,24},{24,16},{1,9},{9,1},{17,25},{25,17},{2,10},{10... | collective-permute-start | bytes 983048 | tf_op jit(solution)/shard_map/ppermute | solution.py:17
  99.4 26.6 %collective-permute-start.24 = (bf16[40,4096]{1,0:T(8,128)(2,1)S(1)}, bf16[40,4096]{1,0:T(8,128)(2,1)S(1)}, u32[]{:S(2)}, u32[]{:S(2)}) collective-permute-start(bf16[40,4096]{1,0:T(8,128)(2,1)S(1)} %get-tuple-element.119), channel_id=1, source_target_pairs={{0,16},{8,24},{16,0},{24,8},{1,17},{9,25},{17,1},{25,9},{2,18},{10... | collective-permute-start | bytes 983048 | tf_op jit(solution)/shard_map/ppermute | solution.py:17
  107.2 27.6 %collective-permute-start.25 = (bf16[40,4096]{1,0:T(8,128)(2,1)S(1)}, bf16[40,4096]{1,0:T(8,128)(2,1)S(1)}, u32[]{:S(2)}, u32[]{:S(2)}) collective-permute-start(bf16[40,4096]{1,0:T(8,128)(2,1)S(1)} %get-tuple-element.120), channel_id=1, source_target_pairs={{0,24},{8,16},{16,8},{24,0},{1,25},{9,17},{17,9},{25,1},{2,26},{10... | collective-permute-start | bytes 983048 | tf_op jit(solution)/shard_map/ppermute | solution.py:17
  115.7 31.0 %collective-permute-start.29 = (bf16[64,4096]{1,0:T(8,128)(2,1)S(1)}, bf16[64,4096]{1,0:T(8,128)(2,1)S(1)}, u32[]{:S(2)}, u32[]{:S(2)}) collective-permute-start(bf16[64,4096]{1,0:T(8,128)(2,1)S(1)} %combine.4), channel_id=1, source_target_pairs={{0,6},{1,7},{2,4},{3,5},{4,2},{5,3},{6,0},{7,1},{8,14},{9,15},{10,... | collective-permute-start | bytes 1572872 | tf_op jit(solution)/shard_map/ppermute | solution.py:17
  118.2 22.9 %collective-permute-start.26 = (bf16[40,4096]{1,0:T(8,128)(2,1)S(1)}, bf16[40,4096]{1,0:T(8,128)(2,1)S(1)}, u32[]{:S(2)}, u32[]{:S(2)}) collective-permute-start(bf16[40,4096]{1,0:T(8,128)(2,1)S(1)} %get-tuple-element.123), channel_id=1, source_target_pairs={{0,8},{8,0},{16,24},{24,16},{1,9},{9,1},{17,25},{25,17},{2,10},{10... | collective-permute-start | bytes 983048 | tf_op jit(solution)/shard_map/ppermute | solution.py:17
  119.6 21.5 %collective-permute-start.27 = (bf16[40,4096]{1,0:T(8,128)(2,1)S(1)}, bf16[40,4096]{1,0:T(8,128)(2,1)S(1)}, u32[]{:S(2)}, u32[]{:S(2)}) collective-permute-start(bf16[40,4096]{1,0:T(8,128)(2,1)S(1)} %get-tuple-element.125), channel_id=1, source_target_pairs={{0,16},{8,24},{16,0},{24,8},{1,17},{9,25},{17,1},{25,9},{2,18},{10... | collective-permute-start | bytes 983048 | tf_op jit(solution)/shard_map/ppermute | solution.py:17
  126.1 15.0 %collective-permute-start.28 = (bf16[40,4096]{1,0:T(8,128)(2,1)S(1)}, bf16[40,4096]{1,0:T(8,128)(2,1)S(1)}, u32[]{:S(2)}, u32[]{:S(2)}) collective-permute-start(bf16[40,4096]{1,0:T(8,128)(2,1)S(1)} %get-tuple-element.127), channel_id=1, source_target_pairs={{0,24},{8,16},{16,8},{24,0},{1,25},{9,17},{17,9},{25,1},{2,26},{10... | collective-permute-start | bytes 983048 | tf_op jit(solution)/shard_map/ppermute | solution.py:17
  136.9 24.7 %collective-permute-start.33 = (bf16[64,4096]{1,0:T(8,128)(2,1)S(1)}, bf16[64,4096]{1,0:T(8,128)(2,1)S(1)}, u32[]{:S(2)}, u32[]{:S(2)}) collective-permute-start(bf16[64,4096]{1,0:T(8,128)(2,1)S(1)} %combine.5), channel_id=1, source_target_pairs={{0,4},{1,5},{2,6},{3,7},{4,0},{5,1},{6,2},{7,3},{8,12},{9,13},{10,... | collective-permute-start | bytes 1572872 | tf_op jit(solution)/shard_map/ppermute | solution.py:17
  143.2 25.0 %collective-permute-start.34 = (bf16[64,4096]{1,0:T(8,128)(2,1)S(1)}, bf16[64,4096]{1,0:T(8,128)(2,1)S(1)}, u32[]{:S(2)}, u32[]{:S(2)}) collective-permute-start(bf16[64,4096]{1,0:T(8,128)(2,1)S(1)} %combine.6), channel_id=1, source_target_pairs={{0,2},{1,3},{2,0},{3,1},{4,6},{5,7},{6,4},{7,5},{8,10},{9,11},{10,... | collective-permute-start | bytes 1572872 | tf_op jit(solution)/shard_map/ppermute | solution.py:17
  146.8 21.4 %collective-permute-start.30 = (bf16[40,4096]{1,0:T(8,128)(2,1)S(1)}, bf16[40,4096]{1,0:T(8,128)(2,1)S(1)}, u32[]{:S(2)}, u32[]{:S(2)}) collective-permute-start(bf16[40,4096]{1,0:T(8,128)(2,1)S(1)} %get-tuple-element.130), channel_id=1, source_target_pairs={{0,8},{8,0},{16,24},{24,16},{1,9},{9,1},{17,25},{25,17},{2,10},{10... | collective-permute-start | bytes 983048 | tf_op jit(solution)/shard_map/ppermute | solution.py:17
  148.2 20.0 %collective-permute-start.31 = (bf16[40,4096]{1,0:T(8,128)(2,1)S(1)}, bf16[40,4096]{1,0:T(8,128)(2,1)S(1)}, u32[]{:S(2)}, u32[]{:S(2)}) collective-permute-start(bf16[40,4096]{1,0:T(8,128)(2,1)S(1)} %get-tuple-element.132), channel_id=1, source_target_pairs={{0,16},{8,24},{16,0},{24,8},{1,17},{9,25},{17,1},{25,9},{2,18},{10... | collective-permute-start | bytes 983048 | tf_op jit(solution)/shard_map/ppermute | solution.py:17
  148.8 19.4 %collective-permute-start.32 = (bf16[40,4096]{1,0:T(8,128)(2,1)S(1)}, bf16[40,4096]{1,0:T(8,128)(2,1)S(1)}, u32[]{:S(2)}, u32[]{:S(2)}) collective-permute-start(bf16[40,4096]{1,0:T(8,128)(2,1)S(1)} %get-tuple-element.134), channel_id=1, source_target_pairs={{0,24},{8,16},{16,8},{24,0},{1,25},{9,17},{17,9},{25,1},{2,26},{10... | collective-permute-start | bytes 983048 | tf_op jit(solution)/shard_map/ppermute | solution.py:17
  (7 other events, 104.7 us)
